TPU v7x, 32 devices: a whole 2x2x4 slice. The times are simulated.
32 devices in a mesh: space: 8 (over y, x, core), species: 4 (over z).
Axes of the slice: x: 2, y: 2, z: 4, core: 2. Of those that a mesh axis runs over, the one named last changes fastest.
Arguments:
- biomass: bfloat16 [512, 16, 1024], P('species', 'space'), may hold values from 0.019897461 to 1
- resources: float32 [128, 16, 1024], P('species', 'space'), may hold values from 0.1 to 4
- capacity: float32 [512, 128], P('species'), may hold values from 0.002 to 0.05
- affinity: float32 [512, 128], P('species'), may hold values from 0.2 to 5
- secretion: bfloat16 [128, 512], P(None, 'species'), may hold values from 0 to 0.059814453
- energy_yield: float32 [128], replicated, may hold values from 0.5 to 2
- maintenance: float32 [512], P('species'), may hold values from 0.3 to 3
- motility: float32 [512], P('species'), may hold values from 0.04 to 0.6
- diffusivity: float32 [128], P('species'), may hold values from 0.02 to 0.6
- supply: float32 [128], P('species'), may hold values from 0.4 to 4
Outputs:
- growth: float32 [512, 16, 1024], P('species', 'space')
- new_biomass: float32 [512, 16, 1024], P('species', 'space')
- new_resources: float32 [128, 16, 1024], P('species', 'space')
All inputs are finite; a program needn't handle non-finite values.
Results may differ from a plain program's by a relative error of at most 0.0003.
Values may be sent and summed in bfloat16 or wider, within the bound.
No kernel may reach another device: no remote copies, remote signals or barrier semaphores. Data moves between devices by JAX's collectives and lax.ppermute only.
A program may use at most 64 MiB of HBM per device.

v0:
```python
import math

import jax
import jax.numpy as jnp
from jax import lax
from jax.sharding import PartitionSpec as P

NY = 16
NZ = 64


time_step = 0.25


def extended_2(block, sides, width):
    for axis, dim in sides:
        count = lax.axis_size(axis)
        forward = [(i, i + 1) for i in range(count - 1)]
        forward.append((count - 1, 0))
        backward = [(target, source) for source, target in forward]
        low = lax.ppermute(
            lax.slice_in_dim(block, block.shape[dim] - width, None, axis=dim), axis, forward
        )
        high = lax.ppermute(lax.slice_in_dim(block, 0, width, axis=dim), axis, backward)
        block = jnp.concatenate([low, block, high], axis=dim)
    return block


def laplace(padded, depth_cells, width_cells):
    channel_count = padded.shape[0]
    inner_cells = padded[:, 1:-1, :]
    slab_rows = inner_cells.shape[1]
    block_view = inner_cells.reshape(channel_count, slab_rows, depth_cells, width_cells)
    extended = jnp.pad(block_view, ((0, 0), (0, 0), (1, 1), (1, 1)), mode="edge")
    beside_x = padded[:, 2:, :] + padded[:, :-2, :]
    beside_yz = (
        extended[:, :, 2:, 1:-1]
        + extended[:, :, :-2, 1:-1]
        + extended[:, :, 1:-1, 2:]
        + extended[:, :, 1:-1, :-2]
    )
    return beside_x + beside_yz.reshape(channel_count, slab_rows, -1) - 6.0 * inner_cells


def spread_biomass(biomass, motility):
    padded = extended_2(biomass, (("space", 1),), 1).astype(jnp.float32)
    return motility[:, None, None] * laplace(padded, NY, NZ)


def spread_resources(resources, diffusivity):
    padded = extended_2(resources, (("space", 1),), 1)
    return diffusivity[:, None, None] * laplace(padded, NY, NZ)


def per_device(
    biomass,
    resources,
    capacity,
    affinity,
    secretion,
    energy_yield,
    maintenance,
    motility,
    diffusivity,
    supply,
):
    local_strains, slab_rows, plane_cells = biomass.shape
    cells_dev = slab_rows * plane_cells
    seen = lax.all_gather(resources.astype(jnp.bfloat16), "species", axis=0, tiled=True)
    all_resources = seen.shape[0]
    seen_flat = seen.reshape(all_resources, cells_dev)
    mass_flat = biomass.reshape(local_strains, cells_dev)
    block_cells = math.gcd(256, cells_dev)
    block_count = cells_dev // block_cells

    def per_block(block_index, carry):
        growth_all, consumed_all, secreted_all = carry
        start = block_index * block_cells
        seen_block = lax.dynamic_slice_in_dim(seen_flat, start, block_cells, 1).astype(jnp.float32)
        mass_block = lax.dynamic_slice_in_dim(mass_flat, start, block_cells, 1).astype(jnp.float32)
        uptake = (
            capacity[:, :, None]
            * seen_block[None, :, :]
            / (affinity[:, :, None] + seen_block[None, :, :])
        )
        growth_block = jnp.sum(energy_yield[None, :, None] * uptake, axis=1) - maintenance[:, None]
        flux_block = jnp.sum(uptake, axis=1)
        product_block = (mass_block * flux_block).astype(jnp.bfloat16)
        consumed_block = jnp.sum(mass_block[:, None, :] * uptake, axis=0)
        secreted_block = jnp.dot(secretion, product_block, preferred_element_type=jnp.float32)
        growth_all = lax.dynamic_update_slice_in_dim(growth_all, growth_block, start, 1)
        consumed_all = lax.dynamic_update_slice_in_dim(consumed_all, consumed_block, start, 1)
        secreted_all = lax.dynamic_update_slice_in_dim(secreted_all, secreted_block, start, 1)
        return (growth_all, consumed_all, secreted_all)

    initial = (
        jnp.zeros((local_strains, cells_dev), jnp.float32),
        jnp.zeros((all_resources, cells_dev), jnp.float32),
        jnp.zeros((all_resources, cells_dev), jnp.float32),
    )
    growth_all, consumed_all, secreted_all = lax.fori_loop(0, block_count, per_block, initial)
    growth = growth_all.reshape(local_strains, slab_rows, plane_cells)
    consumed_all = consumed_all.reshape(all_resources, slab_rows, plane_cells)
    secreted_all = secreted_all.reshape(all_resources, slab_rows, plane_cells)
    net_owned = lax.psum_scatter(
        secreted_all - consumed_all, "species", scatter_dimension=0, tiled=True
    )
    mass_spread = spread_biomass(biomass, motility)
    resource_spread = spread_resources(resources, diffusivity)
    mass = biomass.astype(jnp.float32)
    new_biomass = mass + time_step * (mass * growth + mass_spread)
    new_resources = resources + time_step * (resource_spread + net_owned + supply[:, None, None])
    return (growth, new_biomass, new_resources)


def solution(mesh):
    return jax.shard_map(
        per_device,
        mesh=mesh,
        in_specs=(
            P("species", "space", None),
            P("species", "space", None),
            P("species", None),
            P("species", None),
            P(None, "species"),
            P(),
            P("species"),
            P("species"),
            P("species"),
            P("species"),
        ),
        out_specs=(
            P("species", "space", None),
            P("species", "space", None),
            P("species", "space", None),
        ),
        check_vma=False,
    )
```

profile of v0, /device:TPU:0, one launch (start us, length us, event | category | flops | bytes accessed | tf_op | source)
XLA Modules:
  0.0 182.2 jit_solution(13768835109332961769)
XLA Ops:
  7.2 2.0 %fusion.32 = (f32[32,1,1024]{2,1,0:T(1,128)}, f32[32,1,1024]{2,1,0:T(1,128)}) fusion(f32[32,2,1024]{2,1,0:T(2,128)} %param.13), kind=kLoop, calls=%fused_computation.70 | loop fusion | bytes 524288 | tf_op jit(solution)/shard_map/slice | solution.py:24
  9.2 3.3 %collective-permute-start.2 = (f32[32,1,1024]{2,1,0:T(1,128)}, f32[32,1,1024]{2,1,0:T(1,128)}, u32[]{:S(2)}, u32[]{:S(2)}) collective-permute-start(f32[32,1,1024]{2,1,0:T(1,128)} %get-tuple-element.280), channel_id=1, source_target_pairs={{4,0},{8,4},{12,8},{16,12},{20,16},{24,20},{28,24},{0,28},{5,1},{9... | collective-permute-start | bytes 393224 | tf_op jit(solution)/shard_map/ppermute | solution.py:24
  12.5 1.4 copy.38
  14.8 2.6 %collective-permute-start.1 = (bf16[128,1,1024]{0,2,1:T(8,128)(2,1)}, bf16[128,1,1024]{0,2,1:T(8,128)(2,1)}, u32[]{:S(2)}, u32[]{:S(2)}) collective-permute-start(bf16[128,1,1024]{0,2,1:T(8,128)(2,1)} %get-tuple-element.279), channel_id=1, source_target_pairs={{4,0},{8,4},{12,8},{16,12},{20,16},{24,20},{28,24},{0,28},{5,1},{9... | collective-permute-start | bytes 786440 | tf_op jit(solution)/shard_map/ppermute | solution.py:24
  17.6 16.2 %all_gather.3 = bf16[128,2,1024]{2,1,0:T(2,128)(2,1)S(1)} all-gather(bf16[32,2,1024]{2,1,0:T(2,128)(2,1)S(1)} %convert_element_type.30), channel_id=1, replica_groups=mesh['space'=8,'species'=4] {'species'}, dimensions={0}, use_global_device_ids=true | all-gather | bytes 655360 | tf_op jit(solution)/shard_map/all_gather | solution.py:69
  33.8 0.9 copy.51
  34.7 0.9 copy.52
  35.7 1.0 broadcast.12.clone2
  36.9 80.2 %while.17 = (s32[]{:T(128)}, f32[128,2048]{0,1:T(8,128)S(1)}, f32[128,2048]{0,1:T(8,128)}, f32[128,2048]{0,1:T(8,128)S(1)}, f32[128]{0:T(128)S(1)}, /*index=5*/f...) while((s32[]{:T(128)}, f32[128,2048]{0,1:T(8,128)S(1)}, ...), condition=%wide.region_4.0_spmd, body=%wide.region_0.0_spmd.sunk | while | flops 42041348 | bytes 2853063 | solution.py:101
  37.8 7.1 %fusion.38 = (f32[128,256]{1,0:T(8,128)S(1)}, f32[128,256]{1,0:T(8,128)S(1)}, f32[128,256]{1,0:T(8,128)S(1)}) fusion(f32[128,128]{1,0:T(8,128)S(1)} %get-tuple-element.396, f32[128,256]{1,0:T(8,128)S(1)} %get-tuple-element.354, f32[128,128]{1,0:T(8,128)S(1)} %get-tuple-element.394, f32[128,256]{1,0:T(8,128)S(1)} %get-tuple-element.355, ...), kind=kLoop, calls=%fused_computation.3.clone.1 | loop fusion | flops 33456128 | bytes 786944 | tf_op jit(solution)/shard_map/while/body/eval_jaxpr/reduce_sum | solution.py:87
  45.9 1.0 fusion.39
  47.8 7.1 %fusion.38 = (f32[128,256]{1,0:T(8,128)S(1)}, f32[128,256]{1,0:T(8,128)S(1)}, f32[128,256]{1,0:T(8,128)S(1)}) fusion(f32[128,128]{1,0:T(8,128)S(1)} %get-tuple-element.396, f32[128,256]{1,0:T(8,128)S(1)} %get-tuple-element.354, f32[128,128]{1,0:T(8,128)S(1)} %get-tuple-element.394, f32[128,256]{1,0:T(8,128)S(1)} %get-tuple-element.355, ...), kind=kLoop, calls=%fused_computation.3.clone.1 | loop fusion | flops 33456128 | bytes 786944 | tf_op jit(solution)/shard_map/while/body/eval_jaxpr/reduce_sum | solution.py:87
  55.9 1.0 fusion.39
  57.9 7.1 %fusion.38 = (f32[128,256]{1,0:T(8,128)S(1)}, f32[128,256]{1,0:T(8,128)S(1)}, f32[128,256]{1,0:T(8,128)S(1)}) fusion(f32[128,128]{1,0:T(8,128)S(1)} %get-tuple-element.396, f32[128,256]{1,0:T(8,128)S(1)} %get-tuple-element.354, f32[128,128]{1,0:T(8,128)S(1)} %get-tuple-element.394, f32[128,256]{1,0:T(8,128)S(1)} %get-tuple-element.355, ...), kind=kLoop, calls=%fused_computation.3.clone.1 | loop fusion | flops 33456128 | bytes 786944 | tf_op jit(solution)/shard_map/while/body/eval_jaxpr/reduce_sum | solution.py:87
  65.9 1.0 fusion.39
  67.9 7.1 %fusion.38 = (f32[128,256]{1,0:T(8,128)S(1)}, f32[128,256]{1,0:T(8,128)S(1)}, f32[128,256]{1,0:T(8,128)S(1)}) fusion(f32[128,128]{1,0:T(8,128)S(1)} %get-tuple-element.396, f32[128,256]{1,0:T(8,128)S(1)} %get-tuple-element.354, f32[128,128]{1,0:T(8,128)S(1)} %get-tuple-element.394, f32[128,256]{1,0:T(8,128)S(1)} %get-tuple-element.355, ...), kind=kLoop, calls=%fused_computation.3.clone.1 | loop fusion | flops 33456128 | bytes 786944 | tf_op jit(solution)/shard_map/while/body/eval_jaxpr/reduce_sum | solution.py:87
  76.0 1.0 fusion.39
  77.9 7.1 %fusion.38 = (f32[128,256]{1,0:T(8,128)S(1)}, f32[128,256]{1,0:T(8,128)S(1)}, f32[128,256]{1,0:T(8,128)S(1)}) fusion(f32[128,128]{1,0:T(8,128)S(1)} %get-tuple-element.396, f32[128,256]{1,0:T(8,128)S(1)} %get-tuple-element.354, f32[128,128]{1,0:T(8,128)S(1)} %get-tuple-element.394, f32[128,256]{1,0:T(8,128)S(1)} %get-tuple-element.355, ...), kind=kLoop, calls=%fused_computation.3.clone.1 | loop fusion | flops 33456128 | bytes 786944 | tf_op jit(solution)/shard_map/while/body/eval_jaxpr/reduce_sum | solution.py:87
  86.0 1.0 fusion.39
  87.9 7.1 %fusion.38 = (f32[128,256]{1,0:T(8,128)S(1)}, f32[128,256]{1,0:T(8,128)S(1)}, f32[128,256]{1,0:T(8,128)S(1)}) fusion(f32[128,128]{1,0:T(8,128)S(1)} %get-tuple-element.396, f32[128,256]{1,0:T(8,128)S(1)} %get-tuple-element.354, f32[128,128]{1,0:T(8,128)S(1)} %get-tuple-element.394, f32[128,256]{1,0:T(8,128)S(1)} %get-tuple-element.355, ...), kind=kLoop, calls=%fused_computation.3.clone.1 | loop fusion | flops 33456128 | bytes 786944 | tf_op jit(solution)/shard_map/while/body/eval_jaxpr/reduce_sum | solution.py:87
  96.0 1.0 fusion.39
  98.0 7.1 %fusion.38 = (f32[128,256]{1,0:T(8,128)S(1)}, f32[128,256]{1,0:T(8,128)S(1)}, f32[128,256]{1,0:T(8,128)S(1)}) fusion(f32[128,128]{1,0:T(8,128)S(1)} %get-tuple-element.396, f32[128,256]{1,0:T(8,128)S(1)} %get-tuple-element.354, f32[128,128]{1,0:T(8,128)S(1)} %get-tuple-element.394, f32[128,256]{1,0:T(8,128)S(1)} %get-tuple-element.355, ...), kind=kLoop, calls=%fused_computation.3.clone.1 | loop fusion | flops 33456128 | bytes 786944 | tf_op jit(solution)/shard_map/while/body/eval_jaxpr/reduce_sum | solution.py:87
  106.0 1.0 fusion.39
  108.0 7.1 %fusion.38 = (f32[128,256]{1,0:T(8,128)S(1)}, f32[128,256]{1,0:T(8,128)S(1)}, f32[128,256]{1,0:T(8,128)S(1)}) fusion(f32[128,128]{1,0:T(8,128)S(1)} %get-tuple-element.396, f32[128,256]{1,0:T(8,128)S(1)} %get-tuple-element.354, f32[128,128]{1,0:T(8,128)S(1)} %get-tuple-element.394, f32[128,256]{1,0:T(8,128)S(1)} %get-tuple-element.355, ...), kind=kLoop, calls=%fused_computation.3.clone.1 | loop fusion | flops 33456128 | bytes 786944 | tf_op jit(solution)/shard_map/while/body/eval_jaxpr/reduce_sum | solution.py:87
  116.1 1.0 fusion.39
  117.1 2.3 %sub.34 = f32[128,2048]{0,1:T(8,128)} subtract(f32[128,2048]{0,1:T(8,128)S(1)} %get-tuple-element.190, f32[128,2048]{0,1:T(8,128)} %get-tuple-element.191) | non-fusion elementwise | flops 262144 | bytes 3145728 | tf_op jit(solution)/shard_map/sub | solution.py:106
  119.4 2.3 %copy.46 = f32[128,2,1024]{2,1,0:T(2,128)} copy(f32[128,2,1024]{0,2,1:T(8,128)} %bitcast.25) | data formatting | bytes 2097152 | tf_op jit(solution)/shard_map/sub | solution.py:106
  124.7 1.3 copy.44
  126.0 1.2 maximum_convert_fusion
  128.3 1.3 copy.45
  129.6 43.3 %all-reduce.3.cloned.1.call-done = f32[128,2,1024]{2,1,0:T(2,128)} async-done(((f32[128,2,1024]{2,1,0:T(2,128)}), f32[128,2,1024]{2,1,0:T(2,128)}) %all-reduce.3.cloned.1.call-update) | async-done | bytes 1048592
  172.9 2.5 %fusion.27 = f32[32,2,1024]{2,1,0:T(2,128)} fusion(f32[32,2,1024]{2,1,0:T(2,128)S(1)} %copy-done, f32[128,2,1024]{2,1,0:T(2,128)} %all-reduce.3.cloned.1.call-done, u32[]{:T(128)S(6)} %multiply.5, f32[32,2,1024]{2,1,0:T(2,128)S(1)} %reshape.45, f32[32,1,1024]{2,1,0:T(1,128)} %collective-permute-done.3, f32[32,1,1024]{2,1,0:T(1,128)} %collective-permute-done.2, ...), kind=kLoop, calls=%fused_computation.65 | loop fusion | flops 720896 | bytes 1310980 | tf_op jit(solution)/shard_map/add | solution.py:112
  (91 shorter events, 19.2 us)
Async XLA Ops:
  7.2 10.3 %copy-start = (f32[32,2,1024]{2,1,0:T(2,128)S(1)}, f32[32,2,1024]{2,1,0:T(2,128)}, u32[]{:S(2)}) copy-start(f32[32,2,1024]{2,1,0:T(2,128)} %param.13) | copy-start | bytes 786436
  7.2 165.7 %all-reduce.3.cloned.1.call-start = ((), (), s32[]{:S(2)}) async-start(), calls=%async_computation | async-start | bytes 2097152
  9.2 120.4 %collective-permute-start.2 = (f32[32,1,1024]{2,1,0:T(1,128)}, f32[32,1,1024]{2,1,0:T(1,128)}, u32[]{:S(2)}, u32[]{:S(2)}) collective-permute-start(f32[32,1,1024]{2,1,0:T(1,128)} %get-tuple-element.280), channel_id=1, source_target_pairs={{4,0},{8,4},{12,8},{16,12},{20,16},{24,20},{28,24},{0,28},{5,1},{9... | collective-permute-start | bytes 393224 | tf_op jit(solution)/shard_map/ppermute | solution.py:24
  12.5 22.2 %copy-start.1 = (bf16[128,2,1024]{2,1,0:T(2,128)(2,1)S(1)}, bf16[128,2,1024]{2,1,0:T(2,128)(2,1)}, u32[]{:S(2)}) copy-start(bf16[128,2,1024]{2,1,0:T(2,128)(2,1)} %param.12) | copy-start | bytes 1572868
  12.5 117.1 %collective-permute-start.3 = (f32[32,1,1024]{2,1,0:T(1,128)}, f32[32,1,1024]{2,1,0:T(1,128)}, u32[]{:S(2)}, u32[]{:S(2)}) collective-permute-start(f32[32,1,1024]{2,1,0:T(1,128)} %get-tuple-element.281), channel_id=1, source_target_pairs={{0,4},{4,8},{8,12},{12,16},{16,20},{20,24},{24,28},{28,0},{1,5},{5... | collective-permute-start | bytes 393224 | tf_op jit(solution)/shard_map/ppermute | solution.py:21
  14.8 111.2 %collective-permute-start = (bf16[128,1,1024]{0,2,1:T(8,128)(2,1)}, bf16[128,1,1024]{0,2,1:T(8,128)(2,1)}, u32[]{:S(2)}, u32[]{:S(2)}) collective-permute-start(bf16[128,1,1024]{0,2,1:T(8,128)(2,1)} %get-tuple-element.278), channel_id=1, source_target_pairs={{0,4},{4,8},{8,12},{12,16},{16,20},{20,24},{24,28},{28,0},{1,5},{5... | collective-permute-start | bytes 786440 | tf_op jit(solution)/shard_map/ppermute | solution.py:21
  14.8 111.2 %collective-permute-start.1 = (bf16[128,1,1024]{0,2,1:T(8,128)(2,1)}, bf16[128,1,1024]{0,2,1:T(8,128)(2,1)}, u32[]{:S(2)}, u32[]{:S(2)}) collective-permute-start(bf16[128,1,1024]{0,2,1:T(8,128)(2,1)} %get-tuple-element.279), channel_id=1, source_target_pairs={{4,0},{8,4},{12,8},{16,12},{20,16},{24,20},{28,24},{0,28},{5,1},{9... | collective-permute-start | bytes 786440 | tf_op jit(solution)/shard_map/ppermute | solution.py:24
  34.7 2.1 %copy-start.2 = (f32[128,128]{1,0:T(8,128)S(1)}, f32[128,128]{1,0:T(8,128)}, u32[]{:S(2)}) copy-start(f32[128,128]{1,0:T(8,128)} %param.14) | copy-start | bytes 196612
  34.7 2.1 %copy-start.3 = (f32[128,128]{1,0:T(8,128)S(1)}, f32[128,128]{1,0:T(8,128)}, u32[]{:S(2)}) copy-start(f32[128,128]{1,0:T(8,128)} %param.15) | copy-start | bytes 196612
  34.7 2.1 %copy-start.4 = (f32[128]{0:T(128)S(1)}, f32[128]{0:T(128)}, u32[]{:S(2)}) copy-start(f32[128]{0:T(128)} %param.18) | copy-start | bytes 1540
  34.7 2.1 %copy-start.5 = (f32[128]{0:T(128)S(1)}, f32[128]{0:T(128)}, u32[]{:S(2)}) copy-start(f32[128]{0:T(128)} %param.17) | copy-start | bytes 1540
  122.5 0.7 copy-start.9
  127.3 0.7 copy-start.6
  128.3 44.6 %copy-start.7 = (f32[32]{0:T(128)S(1)}, f32[32]{0:T(128)}, u32[]{:S(2)}) copy-start(f32[32]{0:T(128)} %param.21) | copy-start | bytes 388
  128.3 44.6 %copy-start.8 = (f32[32]{0:T(128)S(1)}, f32[32]{0:T(128)}, u32[]{:S(2)}) copy-start(f32[32]{0:T(128)} %param.20) | copy-start | bytes 388
Sparse Core Ops, SparseCore 0:
  121.8 51.0 all-reduce.2
where the time goes:
time: 183 us; the launch traced here: 182 us
  other arithmetic  72.1 us (39%)
  waiting for transfers between devices  43.3 us (24%)
  local copies, waits for them, and re-layouts  21 us (11%)
  blocking collectives  16.2 us (9%)
  between operations  14.9 us (8%)
  matrix products  8.23 us (4%)
  starting transfers between devices  6.02 us (3%)
    reduce_sum x8, other arithmetic, per_block(): flux_block = jnp.sum(uptake, axis=1)  56.7 us
    unnamed x2, waiting for transfers between devices  43.3 us
    all_gather x1, blocking collectives, per_device(): lax.all_gather(resources.astype(jnp.bfloat16), 'species', axis=0, tiled=T...  16.2 us
    dot_general x8, matrix products, per_block(): jnp.dot(secretion, product_block, preferred_element_type=jnp.float32)  8.23 us
    convert_element_type x8, other arithmetic, per_block(): lax.dynamic_slice_in_dim(mass_flat, start, block_cells, 1)  7.17 us
    unnamed x26, local copies, waits for them, and re-layouts  6.79 us
    dynamic_update_slice x16, local copies, waits for them, and re-layouts, per_block(): lax.dynamic_update_slice_in_dim(consumed_all, consumed_block, start, 1)  6.11 us
    ppermute x2, starting transfers between devices, extended_2(): lax.ppermute(lax.slice_in_dim(block, 0, width, axis=dim), axis, backward)  5.98 us
  transfers between devices with their start and end apart: 5, of which 1 were waited for; matrix products, arithmetic and copies ran while one was open for 53% of the time, Pallas kernels for 0%

commit v1 on v0

v1 whole, which is shorter than its diff:
```python
import functools

import jax
import jax.numpy as jnp
from jax import lax
from jax.experimental import pallas as pl
from jax.experimental.pallas import tpu as pltpu
from jax.sharding import PartitionSpec as P

NY = 16
NZ = 64

time_step = 0.25

bf16 = jnp.bfloat16
f32 = jnp.float32
LANES = 128
GROUP = 16
WIDE = 256


def whole():
    return pl.BlockSpec(memory_space=pltpu.VMEM)


def anywhere():
    return pl.BlockSpec(memory_space=pl.ANY)


def params(limit):
    return pltpu.CompilerParams(vmem_limit_bytes=limit << 20)


def estimate(elements):
    return pl.CostEstimate(flops=40 * elements, bytes_accessed=1 << 20, transcendentals=elements)


def spread_kernel(first_ref, capacity_ref, affinity_ref, yield_ref, slope_ref, level_ref):
    strains, resources = capacity_ref.shape
    shift = lax.rem(2 * resources - first_ref[0] - GROUP * pl.program_id(0), resources)
    shift = lax.rem(shift + resources, resources)
    yields = yield_ref[...]
    for group in range(strains // GROUP):
        rows = pl.ds(group * GROUP, GROUP)
        level = 1.0 / (capacity_ref[rows, :] * yields)
        slope = pltpu.roll(affinity_ref[rows, :] * level, shift, 1)
        level = pltpu.roll(level, shift, 1)
        for r in range(GROUP):
            slope_ref[r, group] = jnp.broadcast_to(slope[:, r : r + 1], (GROUP, LANES))
            level_ref[r, group] = jnp.broadcast_to(level[:, r : r + 1], (GROUP, LANES))


def spread_coefficients(first, capacity, affinity, energy_yield):
    strains, resources = capacity.shape
    groups = strains // GROUP
    shape = jax.ShapeDtypeStruct((resources, groups, GROUP, LANES), f32)
    block = pl.BlockSpec((GROUP, groups, GROUP, LANES), lambda i: (i, 0, 0, 0))
    return pl.pallas_call(
        spread_kernel,
        grid=(resources // GROUP,),
        out_shape=(shape, shape),
        in_specs=[pl.BlockSpec(memory_space=pltpu.SMEM)] + [whole()] * 3,
        out_specs=(block, block),
        compiler_params=params(16),
        cost_estimate=estimate(resources * strains * LANES),
    )(first, capacity, affinity, energy_yield[None, :])


def uptake_sums(row0, seen_refs, slope_hbm, level_hbm, inverse_ref, mass_s, growth_ref, flux_ref,
                consumed_ref, y_s, slope_s, level_s, eaten_s, sem):
    rows, cells = y_s.shape
    groups = mass_s.shape[0] // GROUP
    blocks = rows // GROUP

    def fetch(block, slot):
        part = pl.ds(row0 + block * GROUP, GROUP)
        return (
            pltpu.make_async_copy(slope_hbm.at[part], slope_s.at[slot], sem.at[0, slot]),
            pltpu.make_async_copy(level_hbm.at[part], level_s.at[slot], sem.at[1, slot]),
        )

    for copy in fetch(0, 0):
        copy.start()
    start = 0
    for ref in seen_refs:
        count = ref.shape[0]
        y_s[start : start + count, :] = 1.0 / ref[...].astype(f32)
        start += count

    def per_block(block, _):
        slot = lax.rem(block, 2)
        for copy in fetch(block, slot):
            copy.wait()

        @pl.when(block + 1 < blocks)
        def _():
            for copy in fetch(block + 1, 1 - slot):
                copy.start()

        r0 = pl.multiple_of(block * GROUP, GROUP)

        def per_tile(tile, _):
            lanes = pl.ds(pl.multiple_of(tile * LANES, LANES), LANES)
            y_rows = y_s[pl.ds(r0, GROUP), lanes]
            inverse = inverse_ref[pl.ds(row0 + r0, GROUP), :]
            growth = [growth_ref[g * GROUP : (g + 1) * GROUP, lanes] for g in range(groups)]
            flux = [None] * groups
            for r in range(GROUP):
                y = jnp.broadcast_to(y_rows[r : r + 1], (GROUP, LANES))
                scale = jnp.broadcast_to(inverse[r : r + 1], (GROUP, LANES)).astype(bf16)
                eaten = None
                for g in range(groups):
                    gain = pl.reciprocal(slope_s[slot, r, g] * y + level_s[slot, r, g], approx=True)
                    growth[g] = growth[g] + gain
                    short = gain.astype(bf16)
                    taken = short * scale
                    flux[g] = taken if r == 0 else flux[g] + taken
                    part = short * mass_s[g * GROUP : (g + 1) * GROUP, lanes]
                    eaten = part if g == 0 else eaten + part
                eaten_s[r0 + r, :, lanes] = eaten
            for g in range(groups):
                strains = slice(g * GROUP, (g + 1) * GROUP)
                growth_ref[strains, lanes] = growth[g]
                flux_ref[strains, lanes] += flux[g].astype(f32)
            return 0

        lax.fori_loop(0, cells // LANES, per_tile, 0)
        return 0

    lax.fori_loop(0, blocks, per_block, 0)

    shape = (GROUP, GROUP * GROUP)
    ones = lax.broadcasted_iota(jnp.int32, shape, 1) // GROUP
    ones = (ones == lax.broadcasted_iota(jnp.int32, shape, 0)).astype(f32).astype(bf16)
    for block in range(blocks):
        part = slice(block * GROUP, (block + 1) * GROUP)
        inverse = inverse_ref[row0 + block * GROUP : row0 + (block + 1) * GROUP, :1]
        for tile in range(cells // WIDE):
            lanes = slice(tile * WIDE, (tile + 1) * WIDE)
            sums = jnp.dot(
                ones, eaten_s[part, :, lanes].reshape(GROUP * GROUP, WIDE), preferred_element_type=f32
            )
            consumed_ref[part, lanes] = sums * inverse


def copy_mass(mass_ref, mass_s):
    mass_s[...] = mass_ref[...].astype(f32).astype(bf16)


def first_kernel(row0, parts, *refs):
    seen = refs[:parts]
    slope, level, inverse, mass_ref = refs[parts : parts + 4]
    growth_ref, flux_ref, consumed_ref = refs[parts + 4 : parts + 7]
    y_s, mass_s, slope_s, level_s, eaten_s, sem = refs[parts + 7 :]
    copy_mass(mass_ref, mass_s)
    growth_ref[...] = jnp.zeros_like(growth_ref)
    flux_ref[...] = jnp.zeros_like(flux_ref)
    uptake_sums(row0, seen, slope, level, inverse, mass_s, growth_ref, flux_ref, consumed_ref,
                y_s, slope_s, level_s, eaten_s, sem)


def finish(flux_ref, mass_ref, secretion_ref, consumed_refs, net_refs):
    cells = flux_ref.shape[1]
    for tile in range(cells // WIDE):
        lanes = slice(tile * WIDE, (tile + 1) * WIDE)
        product = (mass_ref[:, lanes].astype(f32) * flux_ref[:, lanes]).astype(bf16)
        secreted = jnp.dot(secretion_ref[...], product, preferred_element_type=f32)
        consumed = [ref[:, lanes] for ref in consumed_refs]
        net = secreted - (consumed[0] if len(consumed) == 1 else jnp.concatenate(consumed, axis=0))
        start = 0
        for ref in net_refs:
            count = ref.shape[0]
            ref[:, lanes] = net[start : start + count].astype(ref.dtype)
            start += count


def second_kernel(row0, parts, owners, *refs):
    seen = refs[:parts]
    slope, level, inverse, mass_ref = refs[parts : parts + 4]
    growth_in, flux_in, consumed_in, secretion_ref = refs[parts + 4 : parts + 8]
    growth_ref = refs[parts + 8]
    net_refs = refs[parts + 9 : parts + 9 + owners]
    flux_s, consumed_s, y_s, mass_s, slope_s, level_s, eaten_s, sem = refs[parts + 9 + owners :]
    copy_mass(mass_ref, mass_s)
    growth_ref[...] = growth_in[...]
    flux_s[...] = flux_in[...]
    uptake_sums(row0, seen, slope, level, inverse, mass_s, growth_ref, flux_s, consumed_s,
                y_s, slope_s, level_s, eaten_s, sem)
    finish(flux_s, mass_ref, secretion_ref, (consumed_in, consumed_s), net_refs)


def only_kernel(row0, parts, owners, *refs):
    seen = refs[:parts]
    slope, level, inverse, mass_ref, secretion_ref = refs[parts : parts + 5]
    growth_ref = refs[parts + 5]
    net_refs = refs[parts + 6 : parts + 6 + owners]
    flux_s, consumed_s, y_s, mass_s, slope_s, level_s, eaten_s, sem = refs[parts + 6 + owners :]
    copy_mass(mass_ref, mass_s)
    growth_ref[...] = jnp.zeros_like(growth_ref)
    flux_s[...] = jnp.zeros_like(flux_s)
    uptake_sums(row0, seen, slope, level, inverse, mass_s, growth_ref, flux_s, consumed_s,
                y_s, slope_s, level_s, eaten_s, sem)
    finish(flux_s, mass_ref, secretion_ref, (consumed_s,), net_refs)


def work_space(rows, strains, cells):
    groups = strains // GROUP
    return [
        pltpu.VMEM((rows, cells), f32),
        pltpu.VMEM((strains, cells), bf16),
        pltpu.VMEM((2, GROUP, groups, GROUP, LANES), f32),
        pltpu.VMEM((2, GROUP, groups, GROUP, LANES), f32),
        pltpu.VMEM((rows, GROUP, cells), bf16),
        pltpu.SemaphoreType.DMA((2, 2)),
    ]


def exchange(own, others, slope, level, inverse, mass, secretion):
    strains, cells = mass.shape
    held = own.shape[0]
    total = inverse.shape[0]
    sums = jax.ShapeDtypeStruct((strains, cells), f32)
    nets = tuple(
        jax.ShapeDtypeStruct((held, cells), f32 if i == 0 else bf16) for i in range(total // held)
    )
    hbm = [anywhere(), anywhere(), whole(), whole()]
    if held % GROUP:
        seen = jnp.concatenate([own] + others, axis=0)
        outs = pl.pallas_call(
            functools.partial(only_kernel, 0, 1, len(nets)),
            out_shape=(sums,) + nets,
            in_specs=[whole()] + hbm + [whole()],
            out_specs=(whole(),) * (1 + len(nets)),
            scratch_shapes=[pltpu.VMEM((strains, cells), f32), pltpu.VMEM((total, cells), f32)]
            + work_space(total, strains, cells),
            compiler_params=params(56),
            cost_estimate=estimate(total * strains * cells),
        )(seen, slope, level, inverse, mass, secretion)
        return outs[0], outs[1:]
    growth, flux, consumed = pl.pallas_call(
        functools.partial(first_kernel, 0, 1),
        out_shape=(sums, sums, jax.ShapeDtypeStruct((held, cells), f32)),
        in_specs=[whole()] + hbm,
        out_specs=(whole(),) * 3,
        scratch_shapes=work_space(held, strains, cells),
        compiler_params=params(40),
        cost_estimate=estimate(held * strains * cells),
    )(own, slope, level, inverse, mass)
    rest = total - held
    outs = pl.pallas_call(
        functools.partial(second_kernel, held, len(others), len(nets)),
        out_shape=(sums,) + nets,
        in_specs=[whole()] * len(others) + hbm + [whole()] * 4,
        out_specs=(whole(),) * (1 + len(nets)),
        scratch_shapes=[pltpu.VMEM((strains, cells), f32), pltpu.VMEM((rest, cells), f32)]
        + work_space(rest, strains, cells),
        compiler_params=params(56),
        cost_estimate=estimate(rest * strains * cells),
    )(*others, slope, level, inverse, mass, growth, flux, consumed, secretion)
    return outs[0], outs[1:]


def laplace(field, low, high, planes, plane):
    cell = lax.broadcasted_iota(jnp.int32, (field[0].shape[0], plane), 1)
    z = lax.rem(cell, NZ)
    out = []
    for x in range(planes):
        v = field[x]
        beside = (low if x == 0 else field[x - 1]) + (high if x == planes - 1 else field[x + 1])
        beside += jnp.where(z == 0, v, pltpu.roll(v, 1, 1))
        beside += jnp.where(z == NZ - 1, v, pltpu.roll(v, plane - 1, 1))
        beside += jnp.where(cell < NZ, v, pltpu.roll(v, NZ, 1))
        beside += jnp.where(cell >= plane - NZ, v, pltpu.roll(v, plane - NZ, 1))
        out.append(beside - 6.0 * v)
    return out


def planes_of(ref, rows, planes, plane):
    return [ref[rows, x * plane : (x + 1) * plane].astype(f32) for x in range(planes)]


def step_kernel(planes, plane, mass_ref, low_ref, high_ref, sum_ref, maintenance_ref, motility_ref,
                growth_ref, new_ref):
    def per_group(group, _):
        rows = pl.ds(pl.multiple_of(group * GROUP, GROUP), GROUP)
        mass = planes_of(mass_ref, rows, planes, plane)
        spread = laplace(mass, low_ref[rows, :].astype(f32), high_ref[rows, :].astype(f32), planes, plane)
        maintenance = maintenance_ref[rows, :1]
        motility = motility_ref[rows, :1]
        for x in range(planes):
            lanes = slice(x * plane, (x + 1) * plane)
            growth = sum_ref[rows, lanes] - maintenance
            growth_ref[rows, lanes] = growth
            new_ref[rows, lanes] = mass[x] + time_step * (mass[x] * growth + motility * spread[x])
        return 0

    lax.fori_loop(0, mass_ref.shape[0] // GROUP, per_group, 0)


def resource_kernel(planes, plane, field_ref, low_ref, high_ref, net_ref, diffusivity_ref, supply_ref,
                    new_ref):
    rows = slice(0, field_ref.shape[0])
    field = planes_of(field_ref, rows, planes, plane)
    spread = laplace(field, low_ref[...], high_ref[...], planes, plane)
    for x in range(planes):
        lanes = slice(x * plane, (x + 1) * plane)
        change = diffusivity_ref[:, :1] * spread[x] + net_ref[:, lanes] + supply_ref[:, :1]
        new_ref[:, lanes] = field[x] + time_step * change


def column(values):
    return jnp.broadcast_to(values[:, None], (values.shape[0], LANES))


def halo(block, axis):
    count = lax.axis_size(axis)
    forward = [(i, (i + 1) % count) for i in range(count)]
    backward = [(target, source) for source, target in forward]
    low = lax.ppermute(block[:, -1, :], axis, forward)
    high = lax.ppermute(block[:, 0, :], axis, backward)
    return low, high


def shifted(value, axis, shift):
    count = lax.axis_size(axis)
    return lax.ppermute(value, axis, [(i, (i + shift) % count) for i in range(count)])


def per_device(
    biomass,
    resources,
    capacity,
    affinity,
    secretion,
    energy_yield,
    maintenance,
    motility,
    diffusivity,
    supply,
):
    strains, slab_rows, plane = biomass.shape
    cells = slab_rows * plane
    held = resources.shape[0]
    count = lax.axis_size("species")
    total = held * count
    mass = biomass.reshape(strains, cells)
    field = resources.reshape(held, cells)
    own = field.astype(bf16)
    others = [shifted(own, "species", -j) for j in range(1, count)]
    first = lax.axis_index("species") * held
    turned = lax.dynamic_slice_in_dim(jnp.concatenate([energy_yield, energy_yield]), first, total)
    inverse = column(1.0 / turned)
    secretion = lax.dynamic_slice_in_dim(jnp.concatenate([secretion, secretion]), first, total, 0)
    slope, level = spread_coefficients(first[None].astype(jnp.int32), capacity, affinity, energy_yield)
    mass_low, mass_high = halo(biomass, "space")
    field_low, field_high = halo(resources, "space")
    gained, nets = exchange(own, others, slope, level, inverse, mass, secretion)
    arrived = [shifted(nets[j], "species", j) for j in range(1, count)]
    sums = jax.ShapeDtypeStruct((strains, cells), f32)
    growth, new_biomass = pl.pallas_call(
        functools.partial(step_kernel, slab_rows, plane),
        out_shape=(sums, sums),
        in_specs=[whole()] * 6,
        out_specs=(whole(),) * 2,
        compiler_params=params(32),
        cost_estimate=estimate(strains * cells * 8),
    )(mass, mass_low, mass_high, gained, column(maintenance), column(motility))
    partial = pl.pallas_call(
        functools.partial(resource_kernel, slab_rows, plane),
        out_shape=jax.ShapeDtypeStruct((held, cells), f32),
        in_specs=[whole()] * 6,
        out_specs=whole(),
        compiler_params=params(32),
        cost_estimate=estimate(held * cells * 8),
    )(field, field_low, field_high, nets[0], column(diffusivity), column(supply))
    received = arrived[0].astype(f32)
    for part in arrived[1:]:
        received = received + part.astype(f32)
    new_resources = partial + time_step * received
    shape = (strains, slab_rows, plane)
    return growth.reshape(shape), new_biomass.reshape(shape), new_resources.reshape(resources.shape)


def solution(mesh):
    return jax.shard_map(
        per_device,
        mesh=mesh,
        in_specs=(
            P("species", "space", None),
            P("species", "space", None),
            P("species", None),
            P("species", None),
            P(None, "species"),
            P(),
            P("species"),
            P("species"),
            P("species"),
            P("species"),
        ),
        out_specs=(
            P("species", "space", None),
            P("species", "space", None),
            P("species", "space", None),
        ),
        check_vma=False,
    )
```

time: 183 us -> 102 us (0.56)
  other arithmetic: 72.1 us -> 1.61 us
  Pallas kernels: 0 us -> 58 us
  waiting for transfers between devices: 43.3 us -> 3.49 us
  blocking collectives: 16.2 us -> 0 us
  between operations: 14.9 us -> 0.92 us
  starting transfers between devices: 6.02 us -> 16.5 us
  matrix products: 8.23 us -> 0 us
    pallas_call x0 -> x5, Pallas kernels: none -> 58 us  [the longest x1 31.7 us: exchange(): pl.pallas_call(functools.partial(second_kernel, held, len(others), len(ne...]
    reduce_sum x8 -> x0, other arithmetic: 56.7 us -> none  [per_block(): flux_block = jnp.sum(uptake, axis=1)]
    unnamed x2 -> x0, waiting for transfers between devices: 43.3 us -> none
    all_gather x1 -> x0, blocking collectives: 16.2 us -> none  [per_device(): lax.all_gather(resources.astype(jnp.bfloat16), 'species', axis=0, tiled=T...]
    ppermute x4 -> x10, starting transfers between devices: 5.98 us -> 16.5 us  [the longest x6 11.1 us: shifted(): lax.ppermute(value, axis, [(i, (i + shift) % count) for i in range(count)])]
    convert_element_type x10 -> x1, other arithmetic: 8.48 us -> 0.02 us  [per_device(): own = field.astype(bf16)]
    dot_general x8 -> x0, matrix products: 8.23 us -> none  [per_block(): jnp.dot(secretion, product_block, preferred_element_type=jnp.float32)]
    dynamic_update_slice x32 -> x0, local copies, waits for them, and re-layouts: 6.92 us -> none  [the longest x16 6.11 us: per_block(): lax.dynamic_update_slice_in_dim(consumed_all, consumed_block, start, 1)]
  transfers between devices with their start and end apart: 5 -> 10, of which waited for: 1 -> 2; matrix products, arithmetic and copies ran while one was open for 53% -> 6% of each run, Pallas kernels for 0% -> 56%
where the time goes in v1:
time: 102 us; the launch traced here: 101 us
  Pallas kernels  58 us (57%)
  local copies, waits for them, and re-layouts  20.6 us (20%)
  starting transfers between devices  16.5 us (16%)
  waiting for transfers between devices  3.49 us (3%)
  other arithmetic  1.61 us (2%)
    pallas_call x1, Pallas kernels, exchange(): pl.pallas_call(functools.partial(second_kernel, held, len(others), len(ne...  31.7 us
    unnamed x50, local copies, waits for them, and re-layouts  13.7 us
    pallas_call x1, Pallas kernels, spread_coefficients(): pl.pallas_call(spread_kernel, grid=(resources // GROUP,), out_shape=(shap...  13.2 us
    pallas_call x1, Pallas kernels, exchange(): pl.pallas_call(functools.partial(first_kernel, 0, 1), out_shape=(sums, su...  11.4 us
    ppermute x6, starting transfers between devices, shifted(): lax.ppermute(value, axis, [(i, (i + shift) % count) for i in range(count)])  11.1 us
    ppermute x2, starting transfers between devices, halo(): high = lax.ppermute(block[:, 0, :], axis, backward)  5.3 us
    ppermute x6, waiting for transfers between devices, shifted(): lax.ppermute(value, axis, [(i, (i + shift) % count) for i in range(count)])  2.12 us
  transfers between devices with their start and end apart: 10, of which 2 were waited for; matrix products, arithmetic and copies ran while one was open for 6% of the time, Pallas kernels for 56%

profile of v1, /device:TPU:0, one launch (start us, length us, event | category | flops | bytes accessed | tf_op | source)
XLA Modules:
  0.0 101.1 jit_solution(10458137371282446688)
XLA Ops:
  0.6 1.0 %copy.22 = f32[4,8,2,1024]{3,1,2,0:T(8,128)S(1)} copy(f32[4,8,2,1024]{3,2,1,0:T(2,128)} %bitcast.25) | data formatting | bytes 524288
  1.7 5.1 %collective-permute-start.2 = (bf16[32,2048]{1,0:T(8,128)(2,1)S(1)}, bf16[32,2048]{1,0:T(8,128)(2,1)S(1)}, u32[]{:S(2)}, u32[]{:S(2)}) collective-permute-start(bf16[32,2048]{1,0:T(8,128)(2,1)S(1)} %convert_element_type.12.refs_0_), channel_id=1, source_target_pairs={{0,3},{1,0},{2,1},{3,2},{4,7},{5,4},{6,5},{7,6},{8,11},{9,8},{10,9... | collective-permute-start | bytes 393224 | tf_op jit(solution)/shard_map/ppermute | solution.py:326
  6.8 1.0 collective-permute-start.4
  7.8 1.3 %fusion.2 = (f32[32,1,1024]{2,1,0:T(1,128)S(1)}, f32[32,1,1024]{2,1,0:T(1,128)S(1)}) fusion(f32[32,2,1024]{2,1,0:T(2,128)} %param.11), kind=kLoop, calls=%fused_computation.11 | loop fusion | bytes 524288 | tf_op jit(solution)/shard_map/slice | solution.py:320
  9.2 2.7 %collective-permute-start.6 = (f32[32,1024]{1,0:T(8,128)S(1)}, f32[32,1024]{1,0:T(8,128)S(1)}, u32[]{:S(2)}, u32[]{:S(2)}) collective-permute-start(f32[32,1024]{1,0:T(8,128)S(1)} %bitcast.28), channel_id=1, source_target_pairs={{4,0},{8,4},{12,8},{16,12},{20,16},{24,20},{28,24},{0,28},{5,1},{9... | collective-permute-start | bytes 393224 | tf_op jit(solution)/shard_map/ppermute | solution.py:320
  11.9 0.7 pad_maximum_fusion
  12.6 1.2 %copy.21 = bf16[16,8,2,1024]{3,1,2,0:T(8,128)(2,1)S(1)} copy(bf16[16,8,2,1024]{3,2,1,0:T(2,128)(2,1)} %bitcast.24) | data formatting | bytes 1048576
  13.9 0.9 copy-done.9
  14.8 0.8 copy-done.10
  15.6 0.7 copy-done.11
  16.3 13.2 %shard_map.121 = (f32[128,8,16,128]{3,2,1,0:T(8,128)S(1)}, f32[128,8,16,128]{3,2,1,0:T(8,128)S(1)}) custom-call(s32[1]{0:T(128)} %bitcast.2.first_ref, f32[128,128]{1,0:T(8,128)S(1)} %copy-done.9, f32[128,128]{1,0:T(8,128)S(1)} %copy-done.10, f32[1,128]{1,0:T(1,128)S(1)} %bitcast.23), custom_call_target="tpu_custom_call" | custom-call | flops 83886080 | bytes 1048576 | tf_op jit(solution)/shard_map/pallas_call | solution.py:58
  29.5 3.2 %copy-done.1 = f32[128,8,16,128]{3,2,1,0:T(8,128)} copy-done((f32[128,8,16,128]{3,2,1,0:T(8,128)}, f32[128,8,16,128]{3,2,1,0:T(8,128)S(1)}, u32[]{:S(2)}) %copy-start.1) | copy-done | bytes 8388632
  32.8 11.4 %shard_map.122 = (f32[128,2048]{1,0:T(8,128)S(1)}, f32[128,2048]{1,0:T(8,128)S(1)}, f32[32,2048]{1,0:T(8,128)S(1)}) custom-call(bf16[32,2048]{1,0:T(8,128)(2,1)S(1)} %convert_element_type.12.refs_0_, f32[128,8,16,128]{3,2,1,0:T(8,128)S(1)} %get-tuple-element.15.refs_1_.refs_3_, f32[128,8,16,128]{3,2,1,0:T(8,128)} %copy-done.1, ...), custom_call_target="tpu_custom_call" | custom-call | flops 335544320 | bytes 1048576 | tf_op jit(solution)/shard_map/pallas_call | solution.py:240
  44.3 1.0 copy-done.6
  45.3 1.0 copy-done.7
  46.3 0.7 copy-done.8
  47.0 0.7 fusion.refs_10_
  47.7 0.6 copy-done.19
  48.5 31.7 %shard_map.123 = (f32[128,2048]{1,0:T(8,128)}, f32[32,2048]{1,0:T(8,128)}, bf16[32,2048]{1,0:T(8,128)(2,1)}, bf16[32,2048]{1,0:T(8,128)(2,1)}, bf16[32,2048]{1,0:T(8,128)(2,1)}) custom-call(bf16[32,2048]{1,0:T(8,128)(2,1)} %copy-done.19, bf16[32,2048]{1,0:T(8,128)(2,1)} %copy-done.20, bf16[32,2048]{1,0:T(8,128)(2,1)} %copy-done.21, ...), custom_call_target="tpu_custom_call" | custom-call | flops 1006632960 | bytes 1048576 | tf_op jit(solution)/shard_map/pallas_call | solution.py:250
  80.1 2.5 %collective-permute-start.7 = (bf16[32,2048]{1,0:T(8,128)(2,1)}, bf16[32,2048]{1,0:T(8,128)(2,1)S(1)}, u32[]{:S(2)}, u32[]{:S(2)}) collective-permute-start(bf16[32,2048]{1,0:T(8,128)(2,1)} %get-tuple-element.24), channel_id=1, source_target_pairs={{0,1},{1,2},{2,3},{3,0},{4,5},{5,6},{6,7},{7,4},{8,9},{9,10},{10,1... | collective-permute-start | bytes 393224 | tf_op jit(solution)/shard_map/ppermute | solution.py:326
  82.7 0.9 collective-permute-start.8
  83.6 1.5 %collective-permute-start.9 = (bf16[32,2048]{1,0:T(8,128)(2,1)}, bf16[32,2048]{1,0:T(8,128)(2,1)S(1)}, u32[]{:S(2)}, u32[]{:S(2)}) collective-permute-start(bf16[32,2048]{1,0:T(8,128)(2,1)} %get-tuple-element.26), channel_id=1, source_target_pairs={{0,3},{1,0},{2,1},{3,2},{4,7},{5,4},{6,5},{7,6},{8,11},{9,8},{10,9... | collective-permute-start | bytes 393224 | tf_op jit(solution)/shard_map/ppermute | solution.py:326
  85.1 0.7 fusion.1
  86.1 2.6 %collective-permute-start.1 = (bf16[128,1024]{1,0:T(8,128)(2,1)S(1)}, bf16[128,1024]{1,0:T(8,128)(2,1)S(1)}, u32[]{:S(2)}, u32[]{:S(2)}) collective-permute-start(bf16[128,1024]{1,0:T(8,128)(2,1)S(1)} %bitcast.26), channel_id=1, source_target_pairs={{4,0},{8,4},{12,8},{16,12},{20,16},{24,20},{28,24},{0,28},{5,1},{9... | collective-permute-start | bytes 786440 | tf_op jit(solution)/shard_map/ppermute | solution.py:320
  88.9 1.0 copy-done.5
  90.2 2.1 %collective-permute-done.8 = bf16[32,2048]{1,0:T(8,128)(2,1)S(1)} collective-permute-done((bf16[32,2048]{1,0:T(8,128)(2,1)}, bf16[32,2048]{1,0:T(8,128)(2,1)S(1)}, u32[]{:S(2)}, u32[]{:S(2)}) %collective-permute-start.8) | collective-permute-done | bytes 131104 | tf_op jit(solution)/shard_map/ppermute | solution.py:326
  92.4 0.9 reshape.30
  93.3 1.4 %collective-permute-done.low_ref = bf16[128,1024]{1,0:T(8,128)(2,1)S(1)} collective-permute-done((bf16[128,1024]{1,0:T(8,128)(2,1)S(1)}, bf16[128,1024]{1,0:T(8,128)(2,1)S(1)}, u32[]{:S(2)}, u32[]{:S(2)}) %collective-permute-start) | collective-permute-done | bytes 262176 | tf_op jit(solution)/shard_map/ppermute | solution.py:319
  94.8 1.2 %copy-done.12 = f32[128,2048]{1,0:T(8,128)S(1)} copy-done((f32[128,2048]{1,0:T(8,128)S(1)}, f32[128,2048]{1,0:T(8,128)}, u32[]{:S(2)}) %copy-start.12) | copy-done | bytes 1048600
  96.0 1.3 %shard_map.124 = (f32[128,2048]{1,0:T(8,128)S(1)}, f32[128,2048]{1,0:T(8,128)S(1)}) custom-call(bf16[128,2048]{1,0:T(8,128)(2,1)S(1)} %bitcast.22, bf16[128,1024]{1,0:T(8,128)(2,1)S(1)} %collective-permute-done.low_ref, bf16[128,1024]{1,0:T(8,128)(2,1)S(1)} %collective-permute-done.1.high_ref, f32[128,2048]{1,0:T(8,128)S(1)} %copy-done.12, ...), custom_call_target="tpu_custom_call" | custom-call | flops 83886080 | bytes 1048576 | tf_op jit(solution)/shard_map/pallas_call | solution.py:360
  97.4 1.9 %reshape.28 = f32[128,2,1024]{2,1,0:T(2,128)} reshape(f32[128,2048]{1,0:T(8,128)S(1)} %get-tuple-element.21) | data formatting | bytes 2097152 | tf_op jit(solution)/shard_map/reshape | solution.py:381
  99.2 1.9 %reshape.29 = f32[128,2,1024]{2,1,0:T(2,128)} reshape(f32[128,2048]{1,0:T(8,128)S(1)} %get-tuple-element.22) | data formatting | bytes 2097152 | tf_op jit(solution)/shard_map/reshape | solution.py:381
  (58 shorter events, 1.4 us)
Async XLA Ops:
  1.7 46.0 %collective-permute-start.2 = (bf16[32,2048]{1,0:T(8,128)(2,1)S(1)}, bf16[32,2048]{1,0:T(8,128)(2,1)S(1)}, u32[]{:S(2)}, u32[]{:S(2)}) collective-permute-start(bf16[32,2048]{1,0:T(8,128)(2,1)S(1)} %convert_element_type.12.refs_0_), channel_id=1, source_target_pairs={{0,3},{1,0},{2,1},{3,2},{4,7},{5,4},{6,5},{7,6},{8,11},{9,8},{10,9... | collective-permute-start | bytes 393224 | tf_op jit(solution)/shard_map/ppermute | solution.py:326
  6.8 40.9 %collective-permute-start.3 = (bf16[32,2048]{1,0:T(8,128)(2,1)S(1)}, bf16[32,2048]{1,0:T(8,128)(2,1)S(1)}, u32[]{:S(2)}, u32[]{:S(2)}) collective-permute-start(bf16[32,2048]{1,0:T(8,128)(2,1)S(1)} %convert_element_type.12.refs_0_), channel_id=1, source_target_pairs={{0,2},{1,3},{2,0},{3,1},{4,6},{5,7},{6,4},{7,5},{8,10},{9,11},{10,... | collective-permute-start | bytes 393224 | tf_op jit(solution)/shard_map/ppermute | solution.py:326
  6.8 40.9 %collective-permute-start.4 = (bf16[32,2048]{1,0:T(8,128)(2,1)S(1)}, bf16[32,2048]{1,0:T(8,128)(2,1)S(1)}, u32[]{:S(2)}, u32[]{:S(2)}) collective-permute-start(bf16[32,2048]{1,0:T(8,128)(2,1)S(1)} %convert_element_type.12.refs_0_), channel_id=1, source_target_pairs={{0,1},{1,2},{2,3},{3,0},{4,5},{5,6},{6,7},{7,4},{8,9},{9,10},{10,1... | collective-permute-start | bytes 393224 | tf_op jit(solution)/shard_map/ppermute | solution.py:326
  9.1 76.9 %collective-permute-start.5 = (f32[32,1024]{1,0:T(8,128)S(1)}, f32[32,1024]{1,0:T(8,128)S(1)}, u32[]{:S(2)}, u32[]{:S(2)}) collective-permute-start(f32[32,1024]{1,0:T(8,128)S(1)} %bitcast.29), channel_id=1, source_target_pairs={{0,4},{4,8},{8,12},{12,16},{16,20},{20,24},{24,28},{28,0},{1,5},{5... | collective-permute-start | bytes 393224 | tf_op jit(solution)/shard_map/ppermute | solution.py:319
  9.2 76.9 %collective-permute-start.6 = (f32[32,1024]{1,0:T(8,128)S(1)}, f32[32,1024]{1,0:T(8,128)S(1)}, u32[]{:S(2)}, u32[]{:S(2)}) collective-permute-start(f32[32,1024]{1,0:T(8,128)S(1)} %bitcast.28), channel_id=1, source_target_pairs={{4,0},{8,4},{12,8},{16,12},{20,16},{24,20},{28,24},{0,28},{5,1},{9... | collective-permute-start | bytes 393224 | tf_op jit(solution)/shard_map/ppermute | solution.py:320
  13.8 30.5 %copy-start.2 = (bf16[16,8,2,1024]{3,1,2,0:T(8,128)(2,1)}, bf16[16,8,2,1024]{3,1,2,0:T(8,128)(2,1)S(1)}, u32[]{:S(2)}) copy-start(bf16[16,8,2,1024]{3,1,2,0:T(8,128)(2,1)S(1)} %copy.21) | copy-start | bytes 1572868
  13.9 0.9 copy-start.9
  14.8 0.8 copy-start.10
  15.6 0.7 copy-start.11
  29.5 3.3 %copy-start.1 = (f32[128,8,16,128]{3,2,1,0:T(8,128)}, f32[128,8,16,128]{3,2,1,0:T(8,128)S(1)}, u32[]{:S(2)}) copy-start(f32[128,8,16,128]{3,2,1,0:T(8,128)S(1)} %get-tuple-element.16.refs_2_.refs_4_) | copy-start | bytes 25165828
  32.7 11.6 %copy-start = (f32[128,8,16,128]{3,2,1,0:T(8,128)}, f32[128,8,16,128]{3,2,1,0:T(8,128)S(1)}, u32[]{:S(2)}) copy-start(f32[128,8,16,128]{3,2,1,0:T(8,128)S(1)} %get-tuple-element.15.refs_1_.refs_3_) | copy-start | bytes 25165828
  32.8 11.5 %copy-start.4 = (f32[128,128]{1,0:T(8,128)}, f32[128,128]{1,0:T(8,128)S(1)}, u32[]{:S(2)}) copy-start(f32[128,128]{1,0:T(8,128)S(1)} %broadcast_in_dim.16.refs_3_.refs_5_) | copy-start | bytes 196612
  32.8 14.1 %copy-start.14 = (bf16[128,128]{1,0:T(8,128)(2,1)S(1)}, bf16[128,128]{1,0:T(8,128)(2,1)}, u32[]{:S(2)}) copy-start(bf16[128,128]{1,0:T(8,128)(2,1)} %param.14) | copy-start | bytes 98308
  44.3 1.0 copy-start.6
  45.3 1.0 copy-start.7
  46.3 0.7 copy-start.8
  47.7 0.6 copy-start.19
  47.7 0.7 copy-start.20
  47.7 0.7 copy-start.21
  48.4 36.7 %copy-start.13 = (bf16[128,2,1024]{2,1,0:T(2,128)(2,1)S(1)}, bf16[128,2,1024]{2,1,0:T(2,128)(2,1)}, u32[]{:S(2)}) copy-start(bf16[128,2,1024]{2,1,0:T(2,128)(2,1)} %param.10) | copy-start | bytes 1572868
  48.4 40.3 %copy-start.17 = (f32[32]{0:T(128)S(1)}, f32[32]{0:T(128)}, u32[]{:S(2)}) copy-start(f32[32]{0:T(128)} %param.18) | copy-start | bytes 388
  48.4 40.4 %copy-start.18 = (f32[32]{0:T(128)S(1)}, f32[32]{0:T(128)}, u32[]{:S(2)}) copy-start(f32[32]{0:T(128)} %param.19) | copy-start | bytes 388
  48.4 46.2 %copy-start.15 = (f32[128]{0:T(128)S(1)}, f32[128]{0:T(128)}, u32[]{:S(2)}) copy-start(f32[128]{0:T(128)} %param.16) | copy-start | bytes 1540
  48.4 46.3 %copy-start.16 = (f32[128]{0:T(128)S(1)}, f32[128]{0:T(128)}, u32[]{:S(2)}) copy-start(f32[128]{0:T(128)} %param.17) | copy-start | bytes 1540
  48.4 46.4 %copy-start.3 = (bf16[16,8,2,1024]{3,1,2,0:T(8,128)(2,1)S(1)}, bf16[16,8,2,1024]{3,1,2,0:T(8,128)(2,1)}, u32[]{:S(2)}) copy-start(bf16[16,8,2,1024]{3,1,2,0:T(8,128)(2,1)} %copy-done.2) | copy-start | bytes 1572868
  80.1 10.0 %collective-permute-start.7 = (bf16[32,2048]{1,0:T(8,128)(2,1)}, bf16[32,2048]{1,0:T(8,128)(2,1)S(1)}, u32[]{:S(2)}, u32[]{:S(2)}) collective-permute-start(bf16[32,2048]{1,0:T(8,128)(2,1)} %get-tuple-element.24), channel_id=1, source_target_pairs={{0,1},{1,2},{2,3},{3,0},{4,5},{5,6},{6,7},{7,4},{8,9},{9,10},{10,1... | collective-permute-start | bytes 393224 | tf_op jit(solution)/shard_map/ppermute | solution.py:326
  82.7 9.6 %collective-permute-start.8 = (bf16[32,2048]{1,0:T(8,128)(2,1)}, bf16[32,2048]{1,0:T(8,128)(2,1)S(1)}, u32[]{:S(2)}, u32[]{:S(2)}) collective-permute-start(bf16[32,2048]{1,0:T(8,128)(2,1)} %get-tuple-element.25), channel_id=1, source_target_pairs={{0,2},{1,3},{2,0},{3,1},{4,6},{5,7},{6,4},{7,5},{8,10},{9,11},{10,... | collective-permute-start | bytes 393224 | tf_op jit(solution)/shard_map/ppermute | solution.py:326
  83.6 8.7 %collective-permute-start.9 = (bf16[32,2048]{1,0:T(8,128)(2,1)}, bf16[32,2048]{1,0:T(8,128)(2,1)S(1)}, u32[]{:S(2)}, u32[]{:S(2)}) collective-permute-start(bf16[32,2048]{1,0:T(8,128)(2,1)} %get-tuple-element.26), channel_id=1, source_target_pairs={{0,3},{1,0},{2,1},{3,2},{4,7},{5,4},{6,5},{7,6},{8,11},{9,8},{10,9... | collective-permute-start | bytes 393224 | tf_op jit(solution)/shard_map/ppermute | solution.py:326
  86.0 8.6 %collective-permute-start = (bf16[128,1024]{1,0:T(8,128)(2,1)S(1)}, bf16[128,1024]{1,0:T(8,128)(2,1)S(1)}, u32[]{:S(2)}, u32[]{:S(2)}) collective-permute-start(bf16[128,1024]{1,0:T(8,128)(2,1)S(1)} %bitcast.27), channel_id=1, source_target_pairs={{0,4},{4,8},{8,12},{12,16},{16,20},{20,24},{24,28},{28,0},{1,5},{5... | collective-permute-start | bytes 786440 | tf_op jit(solution)/shard_map/ppermute | solution.py:319
  86.1 8.5 %collective-permute-start.1 = (bf16[128,1024]{1,0:T(8,128)(2,1)S(1)}, bf16[128,1024]{1,0:T(8,128)(2,1)S(1)}, u32[]{:S(2)}, u32[]{:S(2)}) collective-permute-start(bf16[128,1024]{1,0:T(8,128)(2,1)S(1)} %bitcast.26), channel_id=1, source_target_pairs={{4,0},{8,4},{12,8},{16,12},{20,16},{24,20},{28,24},{0,28},{5,1},{9... | collective-permute-start | bytes 786440 | tf_op jit(solution)/shard_map/ppermute | solution.py:320
  88.9 1.0 copy-start.5
  94.8 1.2 %copy-start.12 = (f32[128,2048]{1,0:T(8,128)S(1)}, f32[128,2048]{1,0:T(8,128)}, u32[]{:S(2)}) copy-start(f32[128,2048]{1,0:T(8,128)} %get-tuple-element.20.sum_ref) | copy-start | bytes 3145732

commit v2 on v1

--- a/solution.py
+++ b/solution.py
@@ -23,10 +23,6 @@
     return pl.BlockSpec(memory_space=pltpu.VMEM)
 
 
-def anywhere():
-    return pl.BlockSpec(memory_space=pl.ANY)
-
-
 def params(limit):
     return pltpu.CompilerParams(vmem_limit_bytes=limit << 20)
 
@@ -35,69 +31,32 @@
     return pl.CostEstimate(flops=40 * elements, bytes_accessed=1 << 20, transcendentals=elements)
 
 
-def spread_kernel(first_ref, capacity_ref, affinity_ref, yield_ref, slope_ref, level_ref):
+def uptake_sums(row0, seen_refs, first_ref, capacity_ref, affinity_ref, yield_ref, inverse_ref, mass_s,
+                growth_ref, flux_ref, consumed_ref, y_s, slopes_s, levels_s, slope_s, level_s, eaten_s):
+    rows, cells = y_s.shape
     strains, resources = capacity_ref.shape
-    shift = lax.rem(2 * resources - first_ref[0] - GROUP * pl.program_id(0), resources)
-    shift = lax.rem(shift + resources, resources)
-    yields = yield_ref[...]
-    for group in range(strains // GROUP):
-        rows = pl.ds(group * GROUP, GROUP)
-        level = 1.0 / (capacity_ref[rows, :] * yields)
-        slope = pltpu.roll(affinity_ref[rows, :] * level, shift, 1)
-        level = pltpu.roll(level, shift, 1)
-        for r in range(GROUP):
-            slope_ref[r, group] = jnp.broadcast_to(slope[:, r : r + 1], (GROUP, LANES))
-            level_ref[r, group] = jnp.broadcast_to(level[:, r : r + 1], (GROUP, LANES))
-
-
-def spread_coefficients(first, capacity, affinity, energy_yield):
-    strains, resources = capacity.shape
     groups = strains // GROUP
-    shape = jax.ShapeDtypeStruct((resources, groups, GROUP, LANES), f32)
-    block = pl.BlockSpec((GROUP, groups, GROUP, LANES), lambda i: (i, 0, 0, 0))
-    return pl.pallas_call(
-        spread_kernel,
-        grid=(resources // GROUP,),
-        out_shape=(shape, shape),
-        in_specs=[pl.BlockSpec(memory_space=pltpu.SMEM)] + [whole()] * 3,
-        out_specs=(block, block),
-        compiler_params=params(16),
-        cost_estimate=estimate(resources * strains * LANES),
-    )(first, capacity, affinity, energy_yield[None, :])
-
-
-def uptake_sums(row0, seen_refs, slope_hbm, level_hbm, inverse_ref, mass_s, growth_ref, flux_ref,
-                consumed_ref, y_s, slope_s, level_s, eaten_s, sem):
-    rows, cells = y_s.shape
-    groups = mass_s.shape[0] // GROUP
     blocks = rows // GROUP
-
-    def fetch(block, slot):
-        part = pl.ds(row0 + block * GROUP, GROUP)
-        return (
-            pltpu.make_async_copy(slope_hbm.at[part], slope_s.at[slot], sem.at[0, slot]),
-            pltpu.make_async_copy(level_hbm.at[part], level_s.at[slot], sem.at[1, slot]),
-        )
-
-    for copy in fetch(0, 0):
-        copy.start()
     start = 0
     for ref in seen_refs:
         count = ref.shape[0]
         y_s[start : start + count, :] = 1.0 / ref[...].astype(f32)
         start += count
+    turn = lax.rem(2 * resources - first_ref[0] - row0, resources)
+    level = 1.0 / (capacity_ref[...] * yield_ref[...])
+    slopes_s[...] = pltpu.roll(affinity_ref[...] * level, turn, 1)
+    levels_s[...] = pltpu.roll(level, turn, 1)
 
     def per_block(block, _):
-        slot = lax.rem(block, 2)
-        for copy in fetch(block, slot):
-            copy.wait()
-
-        @pl.when(block + 1 < blocks)
-        def _():
-            for copy in fetch(block + 1, 1 - slot):
-                copy.start()
-
         r0 = pl.multiple_of(block * GROUP, GROUP)
+        turn = lax.rem(resources - r0, resources)
+        members = [pl.ds(g * GROUP, GROUP) for g in range(groups)]
+        slopes = [pltpu.roll(slopes_s[m, :], turn, 1) for m in members]
+        levels = [pltpu.roll(levels_s[m, :], turn, 1) for m in members]
+        for r in range(GROUP):
+            for g in range(groups):
+                slope_s[r, g] = jnp.broadcast_to(slopes[g][:, r : r + 1], (GROUP, LANES))
+                level_s[r, g] = jnp.broadcast_to(levels[g][:, r : r + 1], (GROUP, LANES))
 
         def per_tile(tile, _):
             lanes = pl.ds(pl.multiple_of(tile * LANES, LANES), LANES)
@@ -110,7 +69,7 @@
                 scale = jnp.broadcast_to(inverse[r : r + 1], (GROUP, LANES)).astype(bf16)
                 eaten = None
                 for g in range(groups):
-                    gain = pl.reciprocal(slope_s[slot, r, g] * y + level_s[slot, r, g], approx=True)
+                    gain = pl.reciprocal(slope_s[r, g] * y + level_s[r, g], approx=True)
                     growth[g] = growth[g] + gain
                     short = gain.astype(bf16)
                     taken = short * scale
@@ -149,14 +108,13 @@
 
 def first_kernel(row0, parts, *refs):
     seen = refs[:parts]
-    slope, level, inverse, mass_ref = refs[parts : parts + 4]
-    growth_ref, flux_ref, consumed_ref = refs[parts + 4 : parts + 7]
-    y_s, mass_s, slope_s, level_s, eaten_s, sem = refs[parts + 7 :]
+    coefficients, mass_ref = refs[parts : parts + 5], refs[parts + 5]
+    growth_ref, flux_ref, consumed_ref = refs[parts + 6 : parts + 9]
+    mass_s, *work = refs[parts + 9 :]
     copy_mass(mass_ref, mass_s)
     growth_ref[...] = jnp.zeros_like(growth_ref)
     flux_ref[...] = jnp.zeros_like(flux_ref)
-    uptake_sums(row0, seen, slope, level, inverse, mass_s, growth_ref, flux_ref, consumed_ref,
-                y_s, slope_s, level_s, eaten_s, sem)
+    uptake_sums(row0, seen, *coefficients, mass_s, growth_ref, flux_ref, consumed_ref, *work)
 
 
 def finish(flux_ref, mass_ref, secretion_ref, consumed_refs, net_refs):
@@ -176,87 +134,86 @@
 
 def second_kernel(row0, parts, owners, *refs):
     seen = refs[:parts]
-    slope, level, inverse, mass_ref = refs[parts : parts + 4]
-    growth_in, flux_in, consumed_in, secretion_ref = refs[parts + 4 : parts + 8]
-    growth_ref = refs[parts + 8]
-    net_refs = refs[parts + 9 : parts + 9 + owners]
-    flux_s, consumed_s, y_s, mass_s, slope_s, level_s, eaten_s, sem = refs[parts + 9 + owners :]
+    coefficients, mass_ref = refs[parts : parts + 5], refs[parts + 5]
+    growth_in, flux_in, consumed_in, secretion_ref = refs[parts + 6 : parts + 10]
+    growth_ref = refs[parts + 10]
+    net_refs = refs[parts + 11 : parts + 11 + owners]
+    flux_s, consumed_s, mass_s, *work = refs[parts + 11 + owners :]
     copy_mass(mass_ref, mass_s)
     growth_ref[...] = growth_in[...]
     flux_s[...] = flux_in[...]
-    uptake_sums(row0, seen, slope, level, inverse, mass_s, growth_ref, flux_s, consumed_s,
-                y_s, slope_s, level_s, eaten_s, sem)
+    uptake_sums(row0, seen, *coefficients, mass_s, growth_ref, flux_s, consumed_s, *work)
     finish(flux_s, mass_ref, secretion_ref, (consumed_in, consumed_s), net_refs)
 
 
 def only_kernel(row0, parts, owners, *refs):
     seen = refs[:parts]
-    slope, level, inverse, mass_ref, secretion_ref = refs[parts : parts + 5]
-    growth_ref = refs[parts + 5]
-    net_refs = refs[parts + 6 : parts + 6 + owners]
-    flux_s, consumed_s, y_s, mass_s, slope_s, level_s, eaten_s, sem = refs[parts + 6 + owners :]
+    coefficients, mass_ref, secretion_ref = refs[parts : parts + 5], refs[parts + 5], refs[parts + 6]
+    growth_ref = refs[parts + 7]
+    net_refs = refs[parts + 8 : parts + 8 + owners]
+    flux_s, consumed_s, mass_s, *work = refs[parts + 8 + owners :]
     copy_mass(mass_ref, mass_s)
     growth_ref[...] = jnp.zeros_like(growth_ref)
     flux_s[...] = jnp.zeros_like(flux_s)
-    uptake_sums(row0, seen, slope, level, inverse, mass_s, growth_ref, flux_s, consumed_s,
-                y_s, slope_s, level_s, eaten_s, sem)
+    uptake_sums(row0, seen, *coefficients, mass_s, growth_ref, flux_s, consumed_s, *work)
     finish(flux_s, mass_ref, secretion_ref, (consumed_s,), net_refs)
 
 
-def work_space(rows, strains, cells):
+def work_space(rows, strains, cells, resources):
     groups = strains // GROUP
     return [
+        pltpu.VMEM((strains, cells), bf16),
         pltpu.VMEM((rows, cells), f32),
-        pltpu.VMEM((strains, cells), bf16),
-        pltpu.VMEM((2, GROUP, groups, GROUP, LANES), f32),
-        pltpu.VMEM((2, GROUP, groups, GROUP, LANES), f32),
+        pltpu.VMEM((strains, resources), f32),
+        pltpu.VMEM((strains, resources), f32),
+        pltpu.VMEM((GROUP, groups, GROUP, LANES), f32),
+        pltpu.VMEM((GROUP, groups, GROUP, LANES), f32),
         pltpu.VMEM((rows, GROUP, cells), bf16),
-        pltpu.SemaphoreType.DMA((2, 2)),
     ]
 
 
-def exchange(own, others, slope, level, inverse, mass, secretion):
+def exchange(own, others, coefficients, mass, secretion):
     strains, cells = mass.shape
     held = own.shape[0]
-    total = inverse.shape[0]
+    total = coefficients[1].shape[1]
     sums = jax.ShapeDtypeStruct((strains, cells), f32)
     nets = tuple(
         jax.ShapeDtypeStruct((held, cells), f32 if i == 0 else bf16) for i in range(total // held)
     )
-    hbm = [anywhere(), anywhere(), whole(), whole()]
+    given = [pl.BlockSpec(memory_space=pltpu.SMEM)] + [whole()] * 5
     if held % GROUP:
         seen = jnp.concatenate([own] + others, axis=0)
         outs = pl.pallas_call(
             functools.partial(only_kernel, 0, 1, len(nets)),
             out_shape=(sums,) + nets,
-            in_specs=[whole()] + hbm + [whole()],
+            in_specs=[whole()] + given + [whole()],
             out_specs=(whole(),) * (1 + len(nets)),
             scratch_shapes=[pltpu.VMEM((strains, cells), f32), pltpu.VMEM((total, cells), f32)]
-            + work_space(total, strains, cells),
-            compiler_params=params(56),
+            + work_space(total, strains, cells, total),
+            compiler_params=params(60),
             cost_estimate=estimate(total * strains * cells),
-        )(seen, slope, level, inverse, mass, secretion)
+        )(seen, *coefficients, mass, secretion)
         return outs[0], outs[1:]
     growth, flux, consumed = pl.pallas_call(
         functools.partial(first_kernel, 0, 1),
         out_shape=(sums, sums, jax.ShapeDtypeStruct((held, cells), f32)),
-        in_specs=[whole()] + hbm,
+        in_specs=[whole()] + given,
         out_specs=(whole(),) * 3,
-        scratch_shapes=work_space(held, strains, cells),
-        compiler_params=params(40),
+        scratch_shapes=work_space(held, strains, cells, total),
+        compiler_params=params(60),
         cost_estimate=estimate(held * strains * cells),
-    )(own, slope, level, inverse, mass)
+    )(own, *coefficients, mass)
     rest = total - held
     outs = pl.pallas_call(
         functools.partial(second_kernel, held, len(others), len(nets)),
         out_shape=(sums,) + nets,
-        in_specs=[whole()] * len(others) + hbm + [whole()] * 4,
+        in_specs=[whole()] * len(others) + given + [whole()] * 4,
         out_specs=(whole(),) * (1 + len(nets)),
         scratch_shapes=[pltpu.VMEM((strains, cells), f32), pltpu.VMEM((rest, cells), f32)]
-        + work_space(rest, strains, cells),
-        compiler_params=params(56),
+        + work_space(rest, strains, cells, total),
+        compiler_params=params(60),
         cost_estimate=estimate(rest * strains * cells),
-    )(*others, slope, level, inverse, mass, growth, flux, consumed, secretion)
+    )(*others, *coefficients, mass, growth, flux, consumed, secretion)
     return outs[0], outs[1:]
 
 
@@ -301,7 +258,7 @@
                     new_ref):
     rows = slice(0, field_ref.shape[0])
     field = planes_of(field_ref, rows, planes, plane)
-    spread = laplace(field, low_ref[...], high_ref[...], planes, plane)
+    spread = laplace(field, low_ref[...].astype(f32), high_ref[...].astype(f32), planes, plane)
     for x in range(planes):
         lanes = slice(x * plane, (x + 1) * plane)
         change = diffusivity_ref[:, :1] * spread[x] + net_ref[:, lanes] + supply_ref[:, :1]
@@ -343,18 +300,19 @@
     held = resources.shape[0]
     count = lax.axis_size("species")
     total = held * count
-    mass = biomass.reshape(strains, cells)
     field = resources.reshape(held, cells)
     own = field.astype(bf16)
     others = [shifted(own, "species", -j) for j in range(1, count)]
+    mass = biomass.reshape(strains, cells)
     first = lax.axis_index("species") * held
     turned = lax.dynamic_slice_in_dim(jnp.concatenate([energy_yield, energy_yield]), first, total)
     inverse = column(1.0 / turned)
     secretion = lax.dynamic_slice_in_dim(jnp.concatenate([secretion, secretion]), first, total, 0)
-    slope, level = spread_coefficients(first[None].astype(jnp.int32), capacity, affinity, energy_yield)
-    mass_low, mass_high = halo(biomass, "space")
-    field_low, field_high = halo(resources, "space")
-    gained, nets = exchange(own, others, slope, level, inverse, mass, secretion)
+    coefficients = (first[None].astype(jnp.int32), capacity, affinity, energy_yield[None, :], inverse)
+    edges = jnp.concatenate([biomass, resources.astype(bf16)], axis=0)
+    low, high = halo(edges, "space")
+    low, high, secretion = lax.optimization_barrier((low, high, secretion))
+    gained, nets = exchange(own, others, coefficients, mass, secretion)
     arrived = [shifted(nets[j], "species", j) for j in range(1, count)]
     sums = jax.ShapeDtypeStruct((strains, cells), f32)
     growth, new_biomass = pl.pallas_call(
@@ -362,23 +320,25 @@
         out_shape=(sums, sums),
         in_specs=[whole()] * 6,
         out_specs=(whole(),) * 2,
-        compiler_params=params(32),
+        compiler_params=params(60),
         cost_estimate=estimate(strains * cells * 8),
-    )(mass, mass_low, mass_high, gained, column(maintenance), column(motility))
+    )(mass, low[:strains], high[:strains], gained, column(maintenance), column(motility))
     partial = pl.pallas_call(
         functools.partial(resource_kernel, slab_rows, plane),
         out_shape=jax.ShapeDtypeStruct((held, cells), f32),
         in_specs=[whole()] * 6,
         out_specs=whole(),
-        compiler_params=params(32),
+        compiler_params=params(60),
         cost_estimate=estimate(held * cells * 8),
-    )(field, field_low, field_high, nets[0], column(diffusivity), column(supply))
+    )(field, low[strains:], high[strains:], nets[0], column(diffusivity), column(supply))
+    shape = (strains, slab_rows, plane)
+    growth, new_biomass = growth.reshape(shape), new_biomass.reshape(shape)
+    arrived, partial, growth, new_biomass = lax.optimization_barrier((arrived, partial, growth, new_biomass))
     received = arrived[0].astype(f32)
     for part in arrived[1:]:
         received = received + part.astype(f32)
     new_resources = partial + time_step * received
-    shape = (strains, slab_rows, plane)
-    return growth.reshape(shape), new_biomass.reshape(shape), new_resources.reshape(resources.shape)
+    return growth, new_biomass, new_resources.reshape(resources.shape)
 
 
 def solution(mesh):

time: 102 us -> 88 us (0.86)
  Pallas kernels: 58 us -> 54.3 us
  local copies, waits for them, and re-layouts: 20.6 us -> 17 us
  waiting for transfers between devices: 3.49 us -> 0.02 us
  starting transfers between devices: 16.5 us -> 13.7 us
    pallas_call x1 -> x0, Pallas kernels: 13.2 us -> none  [spread_coefficients(): pl.pallas_call(spread_kernel, grid=(resources // GROUP,), out_shape=(shap...]
    unnamed x50 -> x32, local copies, waits for them, and re-layouts: 13.7 us -> 4.9 us
    pallas_call x1, Pallas kernels: 31.7 us -> 35 us  [exchange(): pl.pallas_call(functools.partial(second_kernel, held, len(others), len(ne...]
    broadcast_in_dim x5, local copies, waits for them, and re-layouts: 0.36 us -> 3.44 us  [column(): return jnp.broadcast_to(values[:, None], (values.shape[0], LANES))]
    pallas_call x1, Pallas kernels: 1.33 us -> 4.15 us  [per_device(): pl.pallas_call(functools.partial(step_kernel, slab_rows, plane), out_shap...]
    ppermute x2 -> x1, starting transfers between devices: 5.3 us -> 2.63 us  [halo(): high = lax.ppermute(block[:, 0, :], axis, backward)]
    ppermute x6, waiting for transfers between devices: 2.12 us -> 0.02 us  [shifted(): lax.ppermute(value, axis, [(i, (i + shift) % count) for i in range(count)])]
    pallas_call x1, Pallas kernels: 0.34 us -> 2.12 us  [per_device(): pl.pallas_call(functools.partial(resource_kernel, slab_rows, plane), out_...]
  transfers between devices with their start and end apart: 10 -> 8, of which waited for: 2 -> 0; matrix products, arithmetic and copies ran while one was open for 6% -> 15% of each run, Pallas kernels for 56% -> 22%
where the time goes in v2:
time: 88 us; the launch traced here: 87.7 us
  Pallas kernels  54.3 us (62%)
  local copies, waits for them, and re-layouts  17 us (19%)
  starting transfers between devices  13.7 us (16%)
  other arithmetic  1.88 us (2%)
    pallas_call x1, Pallas kernels, exchange(): pl.pallas_call(functools.partial(second_kernel, held, len(others), len(ne...  35 us
    pallas_call x1, Pallas kernels, exchange(): pl.pallas_call(functools.partial(first_kernel, 0, 1), out_shape=(sums, su...  13.1 us
    ppermute x6, starting transfers between devices, shifted(): lax.ppermute(value, axis, [(i, (i + shift) % count) for i in range(count)])  11 us
    reshape x2, local copies, waits for them, and re-layouts, per_device(): growth, new_biomass = (growth.reshape(shape), new_biomass.reshape(shape))  5.03 us
    unnamed x32, local copies, waits for them, and re-layouts  4.9 us
    pallas_call x1, Pallas kernels, per_device(): pl.pallas_call(functools.partial(step_kernel, slab_rows, plane), out_shap...  4.15 us
    broadcast_in_dim x5, local copies, waits for them, and re-layouts, column(): return jnp.broadcast_to(values[:, None], (values.shape[0], LANES))  3.44 us
    ppermute x1, starting transfers between devices, halo(): high = lax.ppermute(block[:, 0, :], axis, backward)  2.63 us
  transfers between devices with their start and end apart: 8, of which 0 were waited for; matrix products, arithmetic and copies ran while one was open for 15% of the time, Pallas kernels for 22%

profile of v2, /device:TPU:0, one launch (start us, length us, event | category | flops | bytes accessed | tf_op | source)
XLA Modules:
  0.0 87.7 jit_solution(15197184984242149498)
XLA Ops:
  0.6 1.1 %copy.15 = f32[4,8,2,1024]{3,1,2,0:T(8,128)S(1)} copy(f32[4,8,2,1024]{3,2,1,0:T(2,128)} %bitcast.11) | data formatting | bytes 524288
  1.8 5.1 %collective-permute-start = (bf16[32,2048]{1,0:T(8,128)(2,1)S(1)}, bf16[32,2048]{1,0:T(8,128)(2,1)S(1)}, u32[]{:S(2)}, u32[]{:S(2)}) collective-permute-start(bf16[32,2048]{1,0:T(8,128)(2,1)S(1)} %convert_element_type.15.refs_0_), channel_id=1, source_target_pairs={{0,3},{1,0},{2,1},{3,2},{4,7},{5,4},{6,5},{7,6},{8,11},{9,8},{10,9... | collective-permute-start | bytes 393224 | tf_op jit(solution)/shard_map/ppermute | solution.py:283
  6.9 1.0 %collective-permute-start.2 = (bf16[32,2048]{1,0:T(8,128)(2,1)S(1)}, bf16[32,2048]{1,0:T(8,128)(2,1)S(1)}, u32[]{:S(2)}, u32[]{:S(2)}) collective-permute-start(bf16[32,2048]{1,0:T(8,128)(2,1)S(1)} %convert_element_type.15.refs_0_), channel_id=1, source_target_pairs={{0,1},{1,2},{2,3},{3,0},{4,5},{5,6},{6,7},{7,4},{8,9},{9,10},{10,1... | collective-permute-start | bytes 393224 | tf_op jit(solution)/shard_map/ppermute | solution.py:283
  8.0 0.1 copy.14
  8.3 2.6 %collective-permute-start.4 = (bf16[160,1024]{1,0:T(8,128)(2,1)S(1)}, bf16[160,1024]{1,0:T(8,128)(2,1)S(1)}, u32[]{:S(2)}, u32[]{:S(2)}) collective-permute-start(bf16[160,1024]{1,0:T(8,128)(2,1)S(1)} %get-tuple-element.41), channel_id=1, source_target_pairs={{4,0},{8,4},{12,8},{16,12},{20,16},{24,20},{28,24},{0,28},{5,1},{9... | collective-permute-start | bytes 983048 | tf_op jit(solution)/shard_map/ppermute | solution.py:277
  10.9 0.9 %copy.16 = bf16[16,8,2,1024]{3,1,2,0:T(8,128)(2,1)} copy(bf16[16,8,2,1024]{3,2,1,0:T(2,128)(2,1)S(1)} %bitcast.10) | data formatting | bytes 1048576
  11.8 0.7 copy-done.13
  12.5 0.1 dynamic-slice_divide_fusion
  12.5 0.7 broadcast_in_dim.16.refs_5_.refs_7_
  13.3 13.1 %shard_map.121 = (f32[128,2048]{1,0:T(8,128)}, f32[128,2048]{1,0:T(8,128)}, f32[32,2048]{1,0:T(8,128)}) custom-call(bf16[32,2048]{1,0:T(8,128)(2,1)} %copy-done.4, s32[1]{0:T(128)} %bitcast.refs_1_.refs_3_, f32[128,128]{1,0:T(8,128)} %refs_4_.1, f32[128,128]{1,0:T(8,128)} %refs_5_.1, f32[1,128]{1,0:T(1,128)} %bitcast.17, ...), custom_call_target="tpu_custom_call" | custom-call | flops 335544320 | bytes 1048576 | tf_op jit(solution)/shard_map/pallas_call | solution.py:197
  26.3 0.7 fusion.3.refs_12_
  27.1 0.6 copy-done.10
  27.8 35.0 %shard_map.122 = (f32[128,2048]{1,0:T(8,128)}, f32[32,2048]{1,0:T(8,128)}, bf16[32,2048]{1,0:T(8,128)(2,1)}, bf16[32,2048]{1,0:T(8,128)(2,1)}, bf16[32,2048]{1,0:T(8,128)(2,1)}) custom-call(bf16[32,2048]{1,0:T(8,128)(2,1)} %copy-done.10, bf16[32,2048]{1,0:T(8,128)(2,1)} %copy-done.11, bf16[32,2048]{1,0:T(8,128)(2,1)} %copy-done.12, s32[1]{0:T(128)} %bitcast.refs_1_.refs_3_, ...), custom_call_target="tpu_custom_call" | custom-call | flops 1006632960 | bytes 1048576 | tf_op jit(solution)/shard_map/pallas_call | solution.py:207
  62.8 2.5 %collective-permute-start.5 = (bf16[32,2048]{1,0:T(8,128)(2,1)}, bf16[32,2048]{1,0:T(8,128)(2,1)S(1)}, u32[]{:S(2)}, u32[]{:S(2)}) collective-permute-start(bf16[32,2048]{1,0:T(8,128)(2,1)} %get-tuple-element.26), channel_id=1, source_target_pairs={{0,1},{1,2},{2,3},{3,0},{4,5},{5,6},{6,7},{7,4},{8,9},{9,10},{10,1... | collective-permute-start | bytes 393224 | tf_op jit(solution)/shard_map/ppermute | solution.py:283
  65.3 0.9 %collective-permute-start.6 = (bf16[32,2048]{1,0:T(8,128)(2,1)}, bf16[32,2048]{1,0:T(8,128)(2,1)S(1)}, u32[]{:S(2)}, u32[]{:S(2)}) collective-permute-start(bf16[32,2048]{1,0:T(8,128)(2,1)} %get-tuple-element.27), channel_id=1, source_target_pairs={{0,2},{1,3},{2,0},{3,1},{4,6},{5,7},{6,4},{7,5},{8,10},{9,11},{10,... | collective-permute-start | bytes 393224 | tf_op jit(solution)/shard_map/ppermute | solution.py:283
  66.2 1.5 %collective-permute-start.7 = (bf16[32,2048]{1,0:T(8,128)(2,1)}, bf16[32,2048]{1,0:T(8,128)(2,1)S(1)}, u32[]{:S(2)}, u32[]{:S(2)}) collective-permute-start(bf16[32,2048]{1,0:T(8,128)(2,1)} %get-tuple-element.28), channel_id=1, source_target_pairs={{0,3},{1,0},{2,1},{3,2},{4,7},{5,4},{6,5},{7,6},{8,11},{9,8},{10,9... | collective-permute-start | bytes 393224 | tf_op jit(solution)/shard_map/ppermute | solution.py:283
  67.7 0.7 slice.22.low_ref
  68.4 0.6 slice.20.low_ref
  69.0 0.7 slice.23.high_ref
  69.8 0.6 slice.21.high_ref
  70.4 0.7 copy-done.6
  71.1 0.7 broadcast_in_dim.19.maintenance_ref
  71.8 0.7 broadcast_in_dim.20.motility_ref
  72.5 4.1 %shard_map.124 = (f32[128,2048]{1,0:T(8,128)}, f32[128,2048]{1,0:T(8,128)}) custom-call(bf16[128,2048]{1,0:T(8,128)(2,1)} %bitcast.16, bf16[128,1024]{1,0:T(8,128)(2,1)} %slice.22.low_ref, bf16[128,1024]{1,0:T(8,128)(2,1)} %slice.23.high_ref, f32[128,2048]{1,0:T(8,128)} %get-tuple-element.32.sum_ref, f32[128,128]{1,0:T(8,128)} %broadcast_in_dim.19.maintenance_ref, ...), custom_call_target="tpu_custom_call" | custom-call | flops 83886080 | bytes 1048576 | tf_op jit(solution)/shard_map/pallas_call | solution.py:318
  76.6 3.2 %reshape.28 = f32[128,2,1024]{2,1,0:T(2,128)} reshape(f32[128,2048]{1,0:T(8,128)} %get-tuple-element.33) | data formatting | bytes 2097152 | tf_op jit(solution)/shard_map/reshape | solution.py:335
  79.8 1.9 %reshape.29 = f32[128,2,1024]{2,1,0:T(2,128)} reshape(f32[128,2048]{1,0:T(8,128)S(1)} %copy-done.1) | data formatting | bytes 2097152 | tf_op jit(solution)/shard_map/reshape | solution.py:335
  81.6 0.7 copy-done.8
  82.3 0.7 broadcast_in_dim.17.diffusivity_ref
  83.0 0.7 broadcast_in_dim.18.supply_ref
  83.6 2.1 %shard_map.123 = f32[32,2048]{1,0:T(8,128)} custom-call(f32[32,2048]{1,0:T(8,128)} %bitcast.13, bf16[32,1024]{1,0:T(8,128)(2,1)} %slice.20.low_ref, bf16[32,1024]{1,0:T(8,128)(2,1)} %slice.21.high_ref, f32[32,2048]{1,0:T(8,128)} %get-tuple-element.31.net_ref, f32[32,128]{1,0:T(8,128)} %broadcast_in_dim.17.diffusivity_ref, f32[32,128]{1,0:T(8,128)} %broadcast_in_dim.18.supply_ref), custom_call_target="tpu_custom_call" | custom-call | flops 20971520 | bytes 1048576 | tf_op jit(solution)/shard_map/pallas_call | solution.py:326
  85.8 1.0 %multiply_add_fusion = f32[32,2048]{1,0:T(8,128)S(1)} fusion(f32[32,2048]{1,0:T(8,128)} %shard_map.123, bf16[32,2048]{1,0:T(8,128)(2,1)S(1)} %collective-permute-done.7, bf16[32,2048]{1,0:T(8,128)(2,1)S(1)} %collective-permute-done.6, bf16[32,2048]{1,0:T(8,128)(2,1)S(1)} %collective-permute-done.5), kind=kLoop, calls=%fused_computation.7 | loop fusion | flops 458752 | bytes 917504 | tf_op jit(solution)/shard_map/add | solution.py:340
  86.8 0.9 %reshape.30 = f32[32,2,1024]{2,1,0:T(2,128)} reshape(f32[32,2048]{1,0:T(8,128)S(1)} %multiply_add_fusion) | data formatting | bytes 524288 | tf_op jit(solution)/shard_map/reshape | solution.py:341
  (38 shorter events, 0.4 us)
Async XLA Ops:
  0.6 7.3 %copy-start.2 = (f32[32,2,1024]{2,1,0:T(2,128)S(1)}, f32[32,2,1024]{2,1,0:T(2,128)}, u32[]{:S(2)}) copy-start(f32[32,2,1024]{2,1,0:T(2,128)} %param.11) | copy-start | bytes 786436
  1.7 6.3 %copy-start.3 = (f32[4,8,2,1024]{3,1,2,0:T(8,128)}, f32[4,8,2,1024]{3,1,2,0:T(8,128)S(1)}, u32[]{:S(2)}) copy-start(f32[4,8,2,1024]{3,1,2,0:T(8,128)S(1)} %copy.15) | copy-start | bytes 786436
  1.7 6.3 %copy-start = (bf16[128,2,1024]{2,1,0:T(2,128)(2,1)S(1)}, bf16[128,2,1024]{2,1,0:T(2,128)(2,1)}, u32[]{:S(2)}) copy-start(bf16[128,2,1024]{2,1,0:T(2,128)(2,1)} %param.10) | copy-start | bytes 1572868
  1.8 6.2 %copy-start.4 = (bf16[32,2048]{1,0:T(8,128)(2,1)}, bf16[32,2048]{1,0:T(8,128)(2,1)S(1)}, u32[]{:S(2)}) copy-start(bf16[32,2048]{1,0:T(8,128)(2,1)S(1)} %convert_element_type.15.refs_0_) | copy-start | bytes 393220
  1.8 25.3 %collective-permute-start = (bf16[32,2048]{1,0:T(8,128)(2,1)S(1)}, bf16[32,2048]{1,0:T(8,128)(2,1)S(1)}, u32[]{:S(2)}, u32[]{:S(2)}) collective-permute-start(bf16[32,2048]{1,0:T(8,128)(2,1)S(1)} %convert_element_type.15.refs_0_), channel_id=1, source_target_pairs={{0,3},{1,0},{2,1},{3,2},{4,7},{5,4},{6,5},{7,6},{8,11},{9,8},{10,9... | collective-permute-start | bytes 393224 | tf_op jit(solution)/shard_map/ppermute | solution.py:283
  6.9 20.2 %collective-permute-start.1 = (bf16[32,2048]{1,0:T(8,128)(2,1)S(1)}, bf16[32,2048]{1,0:T(8,128)(2,1)S(1)}, u32[]{:S(2)}, u32[]{:S(2)}) collective-permute-start(bf16[32,2048]{1,0:T(8,128)(2,1)S(1)} %convert_element_type.15.refs_0_), channel_id=1, source_target_pairs={{0,2},{1,3},{2,0},{3,1},{4,6},{5,7},{6,4},{7,5},{8,10},{9,11},{10,... | collective-permute-start | bytes 393224 | tf_op jit(solution)/shard_map/ppermute | solution.py:283
  6.9 20.2 %collective-permute-start.2 = (bf16[32,2048]{1,0:T(8,128)(2,1)S(1)}, bf16[32,2048]{1,0:T(8,128)(2,1)S(1)}, u32[]{:S(2)}, u32[]{:S(2)}) collective-permute-start(bf16[32,2048]{1,0:T(8,128)(2,1)S(1)} %convert_element_type.15.refs_0_), channel_id=1, source_target_pairs={{0,1},{1,2},{2,3},{3,0},{4,5},{5,6},{6,7},{7,4},{8,9},{9,10},{10,1... | collective-permute-start | bytes 393224 | tf_op jit(solution)/shard_map/ppermute | solution.py:283
  8.2 18.9 %collective-permute-start.3 = (bf16[160,1024]{1,0:T(8,128)(2,1)S(1)}, bf16[160,1024]{1,0:T(8,128)(2,1)S(1)}, u32[]{:S(2)}, u32[]{:S(2)}) collective-permute-start(bf16[160,1024]{1,0:T(8,128)(2,1)S(1)} %get-tuple-element.42), channel_id=1, source_target_pairs={{0,4},{4,8},{8,12},{12,16},{16,20},{20,24},{24,28},{28,0},{1,5},{5... | collective-permute-start | bytes 983048 | tf_op jit(solution)/shard_map/ppermute | solution.py:276
  8.3 18.8 %collective-permute-start.4 = (bf16[160,1024]{1,0:T(8,128)(2,1)S(1)}, bf16[160,1024]{1,0:T(8,128)(2,1)S(1)}, u32[]{:S(2)}, u32[]{:S(2)}) collective-permute-start(bf16[160,1024]{1,0:T(8,128)(2,1)S(1)} %get-tuple-element.41), channel_id=1, source_target_pairs={{4,0},{8,4},{12,8},{16,12},{20,16},{24,20},{28,24},{0,28},{5,1},{9... | collective-permute-start | bytes 983048 | tf_op jit(solution)/shard_map/ppermute | solution.py:277
  11.8 0.7 copy-start.13
  13.3 13.1 %copy-start.5 = (bf16[128,128]{1,0:T(8,128)(2,1)S(1)}, bf16[128,128]{1,0:T(8,128)(2,1)}, u32[]{:S(2)}) copy-start(bf16[128,128]{1,0:T(8,128)(2,1)} %param.14) | copy-start | bytes 98308
  27.1 0.6 copy-start.10
  27.1 0.7 copy-start.11
  27.1 0.7 copy-start.12
  62.8 22.9 %collective-permute-start.5 = (bf16[32,2048]{1,0:T(8,128)(2,1)}, bf16[32,2048]{1,0:T(8,128)(2,1)S(1)}, u32[]{:S(2)}, u32[]{:S(2)}) collective-permute-start(bf16[32,2048]{1,0:T(8,128)(2,1)} %get-tuple-element.26), channel_id=1, source_target_pairs={{0,1},{1,2},{2,3},{3,0},{4,5},{5,6},{6,7},{7,4},{8,9},{9,10},{10,1... | collective-permute-start | bytes 393224 | tf_op jit(solution)/shard_map/ppermute | solution.py:283
  65.3 20.5 %collective-permute-start.6 = (bf16[32,2048]{1,0:T(8,128)(2,1)}, bf16[32,2048]{1,0:T(8,128)(2,1)S(1)}, u32[]{:S(2)}, u32[]{:S(2)}) collective-permute-start(bf16[32,2048]{1,0:T(8,128)(2,1)} %get-tuple-element.27), channel_id=1, source_target_pairs={{0,2},{1,3},{2,0},{3,1},{4,6},{5,7},{6,4},{7,5},{8,10},{9,11},{10,... | collective-permute-start | bytes 393224 | tf_op jit(solution)/shard_map/ppermute | solution.py:283
  66.2 19.6 %collective-permute-start.7 = (bf16[32,2048]{1,0:T(8,128)(2,1)}, bf16[32,2048]{1,0:T(8,128)(2,1)S(1)}, u32[]{:S(2)}, u32[]{:S(2)}) collective-permute-start(bf16[32,2048]{1,0:T(8,128)(2,1)} %get-tuple-element.28), channel_id=1, source_target_pairs={{0,3},{1,0},{2,1},{3,2},{4,7},{5,4},{6,5},{7,6},{8,11},{9,8},{10,9... | collective-permute-start | bytes 393224 | tf_op jit(solution)/shard_map/ppermute | solution.py:283
  70.4 0.7 copy-start.6
  71.1 0.7 copy-start.7
  76.6 3.2 %copy-start.1 = (f32[128,2048]{1,0:T(8,128)S(1)}, f32[128,2048]{1,0:T(8,128)}, u32[]{:S(2)}) copy-start(f32[128,2048]{1,0:T(8,128)} %get-tuple-element.34) | copy-start | bytes 3145732
  81.6 0.7 copy-start.8
  82.3 0.7 copy-start.9

commit v3 on v2

--- a/solution.py
+++ b/solution.py
@@ -119,17 +119,26 @@
 
 def finish(flux_ref, mass_ref, secretion_ref, consumed_refs, net_refs):
     cells = flux_ref.shape[1]
+    base = None
     for tile in range(cells // WIDE):
         lanes = slice(tile * WIDE, (tile + 1) * WIDE)
         product = (mass_ref[:, lanes].astype(f32) * flux_ref[:, lanes]).astype(bf16)
         secreted = jnp.dot(secretion_ref[...], product, preferred_element_type=f32)
         consumed = [ref[:, lanes] for ref in consumed_refs]
         net = secreted - (consumed[0] if len(consumed) == 1 else jnp.concatenate(consumed, axis=0))
+        if base is None:
+            base = jnp.mean(net, axis=1, keepdims=True).astype(bf16).astype(f32)
+            base = jnp.broadcast_to(base, (net.shape[0], LANES))
         start = 0
         for ref in net_refs:
-            count = ref.shape[0]
-            ref[:, lanes] = net[start : start + count].astype(ref.dtype)
-            start += count
+            rows = slice(start, start + ref.shape[0])
+            start += ref.shape[0]
+            if ref.dtype == f32:
+                ref[:, lanes] = net[rows]
+                continue
+            ref[:, lanes] = (net[rows] - base[rows, :1]).astype(bf16)
+            if tile == 0:
+                ref[:, cells : cells + LANES] = base[rows].astype(bf16)
 
 
 def second_kernel(row0, parts, owners, *refs):
@@ -172,13 +181,14 @@
     ]
 
 
-def exchange(own, others, coefficients, mass, secretion):
+def exchange(own, others, coefficients, mass, secretion, edges):
     strains, cells = mass.shape
     held = own.shape[0]
     total = coefficients[1].shape[1]
     sums = jax.ShapeDtypeStruct((strains, cells), f32)
     nets = tuple(
-        jax.ShapeDtypeStruct((held, cells), f32 if i == 0 else bf16) for i in range(total // held)
+        jax.ShapeDtypeStruct((held, cells) if i == 0 else (held, cells + LANES), f32 if i == 0 else bf16)
+        for i in range(total // held)
     )
     given = [pl.BlockSpec(memory_space=pltpu.SMEM)] + [whole()] * 5
     if held % GROUP:
@@ -193,7 +203,7 @@
             compiler_params=params(60),
             cost_estimate=estimate(total * strains * cells),
         )(seen, *coefficients, mass, secretion)
-        return outs[0], outs[1:]
+        return *halo(edges, "space"), outs[0], outs[1:]
     growth, flux, consumed = pl.pallas_call(
         functools.partial(first_kernel, 0, 1),
         out_shape=(sums, sums, jax.ShapeDtypeStruct((held, cells), f32)),
@@ -203,6 +213,8 @@
         compiler_params=params(60),
         cost_estimate=estimate(held * strains * cells),
     )(own, *coefficients, mass)
+    edges, consumed = lax.optimization_barrier((edges, consumed))
+    low, high = halo(edges, "space")
     rest = total - held
     outs = pl.pallas_call(
         functools.partial(second_kernel, held, len(others), len(nets)),
@@ -214,7 +226,7 @@
         compiler_params=params(60),
         cost_estimate=estimate(rest * strains * cells),
     )(*others, *coefficients, mass, growth, flux, consumed, secretion)
-    return outs[0], outs[1:]
+    return low, high, outs[0], outs[1:]
 
 
 def laplace(field, low, high, planes, plane):
@@ -236,37 +248,52 @@
     return [ref[rows, x * plane : (x + 1) * plane].astype(f32) for x in range(planes)]
 
 
-def step_kernel(planes, plane, mass_ref, low_ref, high_ref, sum_ref, maintenance_ref, motility_ref,
-                growth_ref, new_ref):
+def column(row):
+    size = row.shape[1]
+    shape = (size, size)
+    own = lax.broadcasted_iota(jnp.int32, shape, 0) == lax.broadcasted_iota(jnp.int32, shape, 1)
+    return jnp.sum(jnp.where(own, jnp.broadcast_to(row, shape), 0.0), axis=1, keepdims=True)
+
+
+def step_kernel(planes, plane, mass_ref, field_ref, low_ref, high_ref, sum_ref, net_ref, maintenance_ref,
+                motility_ref, diffusivity_ref, supply_ref, growth_ref, new_ref, partial_ref, traits_s):
+    strains = mass_ref.shape[0]
+    held = field_ref.shape[0]
+    traits_s[:, 0:1] = column(maintenance_ref[...])
+    traits_s[:, 1:2] = column(motility_ref[...])
+
     def per_group(group, _):
         rows = pl.ds(pl.multiple_of(group * GROUP, GROUP), GROUP)
         mass = planes_of(mass_ref, rows, planes, plane)
         spread = laplace(mass, low_ref[rows, :].astype(f32), high_ref[rows, :].astype(f32), planes, plane)
-        maintenance = maintenance_ref[rows, :1]
-        motility = motility_ref[rows, :1]
+        maintenance = traits_s[rows, 0:1]
+        motility = traits_s[rows, 1:2]
         for x in range(planes):
-            lanes = slice(x * plane, (x + 1) * plane)
-            growth = sum_ref[rows, lanes] - maintenance
-            growth_ref[rows, lanes] = growth
-            new_ref[rows, lanes] = mass[x] + time_step * (mass[x] * growth + motility * spread[x])
+            growth = sum_ref[rows, x * plane : (x + 1) * plane] - maintenance
+            growth_ref[rows, x, :] = growth
+            new_ref[rows, x, :] = mass[x] + time_step * (mass[x] * growth + motility * spread[x])
         return 0
 
-    lax.fori_loop(0, mass_ref.shape[0] // GROUP, per_group, 0)
-
-
-def resource_kernel(planes, plane, field_ref, low_ref, high_ref, net_ref, diffusivity_ref, supply_ref,
-                    new_ref):
-    rows = slice(0, field_ref.shape[0])
-    field = planes_of(field_ref, rows, planes, plane)
-    spread = laplace(field, low_ref[...].astype(f32), high_ref[...].astype(f32), planes, plane)
+    lax.fori_loop(0, strains // GROUP, per_group, 0)
+    field = planes_of(field_ref, slice(0, held), planes, plane)
+    beyond = slice(strains, strains + held)
+    spread = laplace(field, low_ref[beyond, :].astype(f32), high_ref[beyond, :].astype(f32), planes, plane)
+    diffusivity = column(diffusivity_ref[...])
+    supply = column(supply_ref[...])
     for x in range(planes):
         lanes = slice(x * plane, (x + 1) * plane)
-        change = diffusivity_ref[:, :1] * spread[x] + net_ref[:, lanes] + supply_ref[:, :1]
-        new_ref[:, lanes] = field[x] + time_step * change
-
-
-def column(values):
-    return jnp.broadcast_to(values[:, None], (values.shape[0], LANES))
+        change = diffusivity * spread[x] + net_ref[:, lanes] + supply
+        partial_ref[:, lanes] = field[x] + time_step * change
+
+
+def close_kernel(planes, plane, partial_ref, *refs):
+    *arrived, new_ref = refs
+    cells = planes * plane
+    base = sum(ref[:, cells : cells + LANES].astype(f32) for ref in arrived)[:, :1]
+    for x in range(planes):
+        lanes = slice(x * plane, (x + 1) * plane)
+        net = sum(ref[:, lanes].astype(f32) for ref in arrived) + base
+        new_ref[:, x, :] = partial_ref[:, lanes] + time_step * net
 
 
 def halo(block, axis):
@@ -306,39 +333,33 @@
     mass = biomass.reshape(strains, cells)
     first = lax.axis_index("species") * held
     turned = lax.dynamic_slice_in_dim(jnp.concatenate([energy_yield, energy_yield]), first, total)
-    inverse = column(1.0 / turned)
+    inverse = jnp.broadcast_to((1.0 / turned)[:, None], (total, LANES))
     secretion = lax.dynamic_slice_in_dim(jnp.concatenate([secretion, secretion]), first, total, 0)
     coefficients = (first[None].astype(jnp.int32), capacity, affinity, energy_yield[None, :], inverse)
     edges = jnp.concatenate([biomass, resources.astype(bf16)], axis=0)
-    low, high = halo(edges, "space")
-    low, high, secretion = lax.optimization_barrier((low, high, secretion))
-    gained, nets = exchange(own, others, coefficients, mass, secretion)
+    low, high, gained, nets = exchange(own, others, coefficients, mass, secretion, edges)
     arrived = [shifted(nets[j], "species", j) for j in range(1, count)]
-    sums = jax.ShapeDtypeStruct((strains, cells), f32)
-    growth, new_biomass = pl.pallas_call(
+    sums = jax.ShapeDtypeStruct(biomass.shape, f32)
+    growth, new_biomass, partial = pl.pallas_call(
         functools.partial(step_kernel, slab_rows, plane),
-        out_shape=(sums, sums),
-        in_specs=[whole()] * 6,
-        out_specs=(whole(),) * 2,
+        out_shape=(sums, sums, jax.ShapeDtypeStruct((held, cells), f32)),
+        in_specs=[whole()] * 10,
+        out_specs=(whole(),) * 3,
+        scratch_shapes=[pltpu.VMEM((strains, LANES), f32)],
         compiler_params=params(60),
         cost_estimate=estimate(strains * cells * 8),
-    )(mass, low[:strains], high[:strains], gained, column(maintenance), column(motility))
-    partial = pl.pallas_call(
-        functools.partial(resource_kernel, slab_rows, plane),
-        out_shape=jax.ShapeDtypeStruct((held, cells), f32),
-        in_specs=[whole()] * 6,
+    )(mass, field, low, high, gained, nets[0], maintenance[None, :], motility[None, :],
+      diffusivity[None, :], supply[None, :])
+    arrived, partial = lax.optimization_barrier((arrived, partial))
+    new_resources = pl.pallas_call(
+        functools.partial(close_kernel, slab_rows, plane),
+        out_shape=jax.ShapeDtypeStruct(resources.shape, f32),
+        in_specs=[whole()] * count,
         out_specs=whole(),
         compiler_params=params(60),
-        cost_estimate=estimate(held * cells * 8),
-    )(field, low[strains:], high[strains:], nets[0], column(diffusivity), column(supply))
-    shape = (strains, slab_rows, plane)
-    growth, new_biomass = growth.reshape(shape), new_biomass.reshape(shape)
-    arrived, partial, growth, new_biomass = lax.optimization_barrier((arrived, partial, growth, new_biomass))
-    received = arrived[0].astype(f32)
-    for part in arrived[1:]:
-        received = received + part.astype(f32)
-    new_resources = partial + time_step * received
-    return growth, new_biomass, new_resources.reshape(resources.shape)
+        cost_estimate=estimate(held * cells),
+    )(partial, *arrived)
+    return growth, new_biomass, new_resources
 
 
 def solution(mesh):

time: 88 us -> 78.4 us (0.89)
  local copies, waits for them, and re-layouts: 17 us -> 5.25 us
  waiting for transfers between devices: 0.02 us -> 1.93 us
  other arithmetic: 1.88 us -> 0.86 us
    reshape x3 -> x0, local copies, waits for them, and re-layouts: 5.95 us -> none  [the longest x2 5.03 us: per_device(): growth, new_biomass = (growth.reshape(shape), new_biomass.reshape(shape))]
    broadcast_in_dim x5 -> x1, local copies, waits for them, and re-layouts: 3.44 us -> 0.72 us  [per_device(): inverse = jnp.broadcast_to((1.0 / turned)[:, None], (total, LANES))]
    slice x4 -> x0, local copies, waits for them, and re-layouts: 2.68 us -> none  [the longest x1 0.72 us: per_device(): low[:strains]]
    ppermute x6, waiting for transfers between devices: 0.02 us -> 1.92 us  [shifted(): lax.ppermute(value, axis, [(i, (i + shift) % count) for i in range(count)])]
    add x1 -> x0, other arithmetic: 1.02 us -> none  [per_device(): new_resources = partial + time_step * received]
  transfers between devices with their start and end apart: 8 -> 8, of which waited for: 0 -> 1; matrix products, arithmetic and copies ran while one was open for 15% -> 4% of each run, Pallas kernels for 22% -> 68%
where the time goes in v3:
time: 78.4 us; the launch traced here: 77.6 us
  Pallas kernels  55 us (70%)
  starting transfers between devices  13.7 us (17%)
  local copies, waits for them, and re-layouts  5.25 us (7%)
  waiting for transfers between devices  1.93 us (2%)
  other arithmetic  0.86 us (1%)
  between operations  0.79 us (1%)
    pallas_call x1, Pallas kernels, exchange(): pl.pallas_call(functools.partial(second_kernel, held, len(others), len(ne...  35 us
    pallas_call x1, Pallas kernels, exchange(): pl.pallas_call(functools.partial(first_kernel, 0, 1), out_shape=(sums, su...  13.1 us
    ppermute x6, starting transfers between devices, shifted(): lax.ppermute(value, axis, [(i, (i + shift) % count) for i in range(count)])  11 us
    pallas_call x1, Pallas kernels, per_device(): pl.pallas_call(functools.partial(step_kernel, slab_rows, plane), out_shap...  4.96 us
    unnamed x32, local copies, waits for them, and re-layouts  4.49 us
    ppermute x1, starting transfers between devices, halo(): high = lax.ppermute(block[:, 0, :], axis, backward)  2.63 us
    pallas_call x1, Pallas kernels, per_device(): pl.pallas_call(functools.partial(close_kernel, slab_rows, plane), out_sha...  1.97 us
    ppermute x6, waiting for transfers between devices, shifted(): lax.ppermute(value, axis, [(i, (i + shift) % count) for i in range(count)])  1.92 us
  transfers between devices with their start and end apart: 8, of which 1 were waited for; matrix products, arithmetic and copies ran while one was open for 4% of the time, Pallas kernels for 68%

profile of v3, /device:TPU:0, one launch (start us, length us, event | category | flops | bytes accessed | tf_op | source)
XLA Modules:
  0.0 77.6 jit_solution(2347476918189414530)
XLA Ops:
  0.6 1.1 %copy.16 = f32[4,8,2,1024]{3,1,2,0:T(8,128)S(1)} copy(f32[4,8,2,1024]{3,2,1,0:T(2,128)} %bitcast.15) | data formatting | bytes 524288
  1.8 0.0 copy-start.2
  1.8 5.1 %collective-permute-start.2 = (bf16[32,2048]{1,0:T(8,128)(2,1)S(1)}, bf16[32,2048]{1,0:T(8,128)(2,1)S(1)}, u32[]{:S(2)}, u32[]{:S(2)}) collective-permute-start(bf16[32,2048]{1,0:T(8,128)(2,1)S(1)} %convert_element_type.7.refs_0_), channel_id=1, source_target_pairs={{0,3},{1,0},{2,1},{3,2},{4,7},{5,4},{6,5},{7,6},{8,11},{9,8},{10,9... | collective-permute-start | bytes 393224 | tf_op jit(solution)/shard_map/ppermute | solution.py:310
  6.9 0.0 collective-permute-start.3
  6.9 1.0 %collective-permute-start.4 = (bf16[32,2048]{1,0:T(8,128)(2,1)S(1)}, bf16[32,2048]{1,0:T(8,128)(2,1)S(1)}, u32[]{:S(2)}, u32[]{:S(2)}) collective-permute-start(bf16[32,2048]{1,0:T(8,128)(2,1)S(1)} %convert_element_type.7.refs_0_), channel_id=1, source_target_pairs={{0,1},{1,2},{2,3},{3,0},{4,5},{5,6},{6,7},{7,4},{8,9},{9,10},{10,1... | collective-permute-start | bytes 393224 | tf_op jit(solution)/shard_map/ppermute | solution.py:310
  7.9 0.1 copy.18
  8.0 0.0 copy-start.13
  8.0 0.1 copy.14
  8.1 0.9 %copy.15 = bf16[16,8,2,1024]{3,1,2,0:T(8,128)(2,1)} copy(bf16[16,8,2,1024]{3,2,1,0:T(2,128)(2,1)S(1)} %bitcast.14) | data formatting | bytes 1048576
  9.1 0.1 dynamic-slice_divide_fusion
  9.2 0.7 broadcast_in_dim.26.refs_5_.refs_7_
  9.9 13.1 %shard_map.121 = (f32[128,2048]{1,0:T(8,128)}, f32[128,2048]{1,0:T(8,128)}, f32[32,2048]{1,0:T(8,128)}) custom-call(bf16[32,2048]{1,0:T(8,128)(2,1)} %copy-done.6, s32[1]{0:T(128)} %bitcast.refs_1_.refs_3_, f32[128,128]{1,0:T(8,128)} %refs_4_.1, f32[128,128]{1,0:T(8,128)} %refs_5_.1, f32[1,128]{1,0:T(1,128)} %bitcast.21, ...), custom_call_target="tpu_custom_call" | custom-call | flops 335544320 | bytes 1048576 | tf_op jit(solution)/shard_map/pallas_call | solution.py:207
  23.1 0.1 collective-permute-start
  23.1 2.6 %collective-permute-start.1 = (bf16[160,1024]{1,0:T(8,128)(2,1)S(1)}, bf16[160,1024]{1,0:T(8,128)(2,1)S(1)}, u32[]{:S(2)}, u32[]{:S(2)}) collective-permute-start(bf16[160,1024]{1,0:T(8,128)(2,1)S(1)} %get-tuple-element.37), channel_id=1, source_target_pairs={{4,0},{8,4},{12,8},{16,12},{20,16},{24,20},{28,24},{0,28},{5,1},{9... | collective-permute-start | bytes 983048 | tf_op jit(solution)/shard_map/ppermute | solution.py:304
  25.8 0.7 fusion.refs_12_
  26.5 0.0 collective-permute-done.3.refs_1_
  26.5 0.0 collective-permute-done.4.refs_2_
  26.5 0.6 copy-done.10
  27.1 0.1 copy-done.11
  27.2 0.0 copy-done.12
  27.3 35.0 %shard_map.122 = (f32[128,2048]{1,0:T(8,128)}, f32[32,2048]{1,0:T(8,128)}, bf16[32,2176]{1,0:T(8,128)(2,1)}, bf16[32,2176]{1,0:T(8,128)(2,1)}, bf16[32,2176]{1,0:T(8,128)(2,1)}) custom-call(bf16[32,2048]{1,0:T(8,128)(2,1)} %copy-done.10, bf16[32,2048]{1,0:T(8,128)(2,1)} %copy-done.11, bf16[32,2048]{1,0:T(8,128)(2,1)} %copy-done.12, s32[1]{0:T(128)} %bitcast.refs_1_.refs_3_, ...), custom_call_target="tpu_custom_call" | custom-call | flops 1006632960 | bytes 1048576 | tf_op jit(solution)/shard_map/pallas_call | solution.py:219
  62.3 2.5 %collective-permute-start.5 = (bf16[32,2176]{1,0:T(8,128)(2,1)}, bf16[32,2176]{1,0:T(8,128)(2,1)S(1)}, u32[]{:S(2)}, u32[]{:S(2)}) collective-permute-start(bf16[32,2176]{1,0:T(8,128)(2,1)} %get-tuple-element.29), channel_id=1, source_target_pairs={{0,1},{1,2},{2,3},{3,0},{4,5},{5,6},{6,7},{7,4},{8,9},{9,10},{10,1... | collective-permute-start | bytes 417800 | tf_op jit(solution)/shard_map/ppermute | solution.py:310
  64.7 0.9 %collective-permute-start.6 = (bf16[32,2176]{1,0:T(8,128)(2,1)}, bf16[32,2176]{1,0:T(8,128)(2,1)S(1)}, u32[]{:S(2)}, u32[]{:S(2)}) collective-permute-start(bf16[32,2176]{1,0:T(8,128)(2,1)} %get-tuple-element.30), channel_id=1, source_target_pairs={{0,2},{1,3},{2,0},{3,1},{4,6},{5,7},{6,4},{7,5},{8,10},{9,11},{10,... | collective-permute-start | bytes 417800 | tf_op jit(solution)/shard_map/ppermute | solution.py:310
  65.6 1.5 %collective-permute-start.7 = (bf16[32,2176]{1,0:T(8,128)(2,1)}, bf16[32,2176]{1,0:T(8,128)(2,1)S(1)}, u32[]{:S(2)}, u32[]{:S(2)}) collective-permute-start(bf16[32,2176]{1,0:T(8,128)(2,1)} %get-tuple-element.31), channel_id=1, source_target_pairs={{0,3},{1,0},{2,1},{3,2},{4,7},{5,4},{6,5},{7,6},{8,11},{9,8},{10,9... | collective-permute-start | bytes 417800 | tf_op jit(solution)/shard_map/ppermute | solution.py:310
  67.2 0.7 copy-done.8
  67.9 0.1 copy-done.9
  68.0 5.0 %shard_map.123 = (f32[128,2,1024]{2,1,0:T(2,128)}, f32[128,2,1024]{2,1,0:T(2,128)}, f32[32,2048]{1,0:T(8,128)}) custom-call(bf16[128,2048]{1,0:T(8,128)(2,1)} %bitcast.20, f32[32,2048]{1,0:T(8,128)} %bitcast.17, bf16[160,1024]{1,0:T(8,128)(2,1)} %copy-done.8, bf16[160,1024]{1,0:T(8,128)(2,1)} %copy-done.9, f32[128,2048]{1,0:T(8,128)} %get-tuple-element.25.sum_ref, ...), custom_call_target="tpu_custom_call" | custom-call | flops 83886080 | bytes 1048576 | tf_op jit(solution)/shard_map/pallas_call | solution.py:343
  73.0 1.9 %collective-permute-done.6.refs_1_ = bf16[32,2176]{1,0:T(8,128)(2,1)S(1)} collective-permute-done((bf16[32,2176]{1,0:T(8,128)(2,1)}, bf16[32,2176]{1,0:T(8,128)(2,1)S(1)}, u32[]{:S(2)}, u32[]{:S(2)}) %collective-permute-start.6) | collective-permute-done | bytes 139296 | tf_op jit(solution)/shard_map/ppermute | solution.py:310
  74.9 0.0 collective-permute-done.7.refs_2_
  74.9 0.6 copy-done.4
  75.5 0.1 copy-done.5
  75.6 2.0 %shard_map.124 = f32[32,2,1024]{2,1,0:T(2,128)} custom-call(f32[32,2048]{1,0:T(8,128)} %get-tuple-element.33.partial_ref, bf16[32,2176]{1,0:T(8,128)(2,1)} %copy-done.3, bf16[32,2176]{1,0:T(8,128)(2,1)} %copy-done.4, bf16[32,2176]{1,0:T(8,128)(2,1)} %copy-done.5), custom_call_target="tpu_custom_call" | custom-call | flops 2621440 | bytes 1048576 | tf_op jit(solution)/shard_map/pallas_call | solution.py:354
  (27 shorter events, 0.2 us)
Async XLA Ops:
  0.6 7.3 %copy-start.1 = (f32[32,2,1024]{2,1,0:T(2,128)S(1)}, f32[32,2,1024]{2,1,0:T(2,128)}, u32[]{:S(2)}) copy-start(f32[32,2,1024]{2,1,0:T(2,128)} %param.11) | copy-start | bytes 786436
  0.6 7.4 %copy-start = (bf16[128,2,1024]{2,1,0:T(2,128)(2,1)S(1)}, bf16[128,2,1024]{2,1,0:T(2,128)(2,1)}, u32[]{:S(2)}) copy-start(bf16[128,2,1024]{2,1,0:T(2,128)(2,1)} %param.10) | copy-start | bytes 1572868
  1.8 7.3 %copy-start.2 = (f32[4,8,2,1024]{3,1,2,0:T(8,128)}, f32[4,8,2,1024]{3,1,2,0:T(8,128)S(1)}, u32[]{:S(2)}) copy-start(f32[4,8,2,1024]{3,1,2,0:T(8,128)S(1)} %copy.16) | copy-start | bytes 786436
  1.8 7.3 %copy-start.6 = (bf16[32,2048]{1,0:T(8,128)(2,1)}, bf16[32,2048]{1,0:T(8,128)(2,1)S(1)}, u32[]{:S(2)}) copy-start(bf16[32,2048]{1,0:T(8,128)(2,1)S(1)} %convert_element_type.7.refs_0_) | copy-start | bytes 393220
  1.8 24.7 %collective-permute-start.2 = (bf16[32,2048]{1,0:T(8,128)(2,1)S(1)}, bf16[32,2048]{1,0:T(8,128)(2,1)S(1)}, u32[]{:S(2)}, u32[]{:S(2)}) collective-permute-start(bf16[32,2048]{1,0:T(8,128)(2,1)S(1)} %convert_element_type.7.refs_0_), channel_id=1, source_target_pairs={{0,3},{1,0},{2,1},{3,2},{4,7},{5,4},{6,5},{7,6},{8,11},{9,8},{10,9... | collective-permute-start | bytes 393224 | tf_op jit(solution)/shard_map/ppermute | solution.py:310
  6.9 19.6 %collective-permute-start.3 = (bf16[32,2048]{1,0:T(8,128)(2,1)S(1)}, bf16[32,2048]{1,0:T(8,128)(2,1)S(1)}, u32[]{:S(2)}, u32[]{:S(2)}) collective-permute-start(bf16[32,2048]{1,0:T(8,128)(2,1)S(1)} %convert_element_type.7.refs_0_), channel_id=1, source_target_pairs={{0,2},{1,3},{2,0},{3,1},{4,6},{5,7},{6,4},{7,5},{8,10},{9,11},{10,... | collective-permute-start | bytes 393224 | tf_op jit(solution)/shard_map/ppermute | solution.py:310
  6.9 19.6 %collective-permute-start.4 = (bf16[32,2048]{1,0:T(8,128)(2,1)S(1)}, bf16[32,2048]{1,0:T(8,128)(2,1)S(1)}, u32[]{:S(2)}, u32[]{:S(2)}) collective-permute-start(bf16[32,2048]{1,0:T(8,128)(2,1)S(1)} %convert_element_type.7.refs_0_), channel_id=1, source_target_pairs={{0,1},{1,2},{2,3},{3,0},{4,5},{5,6},{6,7},{7,4},{8,9},{9,10},{10,1... | collective-permute-start | bytes 393224 | tf_op jit(solution)/shard_map/ppermute | solution.py:310
  8.0 1.1 %copy-start.13 = (f32[128]{0:T(128)S(1)}, f32[128]{0:T(128)}, u32[]{:S(2)}) copy-start(f32[128]{0:T(128)} %param.15) | copy-start | bytes 1540
  23.0 2.7 %copy-start.7 = (bf16[128,128]{1,0:T(8,128)(2,1)S(1)}, bf16[128,128]{1,0:T(8,128)(2,1)}, u32[]{:S(2)}) copy-start(bf16[128,128]{1,0:T(8,128)(2,1)} %param.14) | copy-start | bytes 98308
  23.1 44.1 %collective-permute-start = (bf16[160,1024]{1,0:T(8,128)(2,1)S(1)}, bf16[160,1024]{1,0:T(8,128)(2,1)S(1)}, u32[]{:S(2)}, u32[]{:S(2)}) collective-permute-start(bf16[160,1024]{1,0:T(8,128)(2,1)S(1)} %get-tuple-element.38), channel_id=1, source_target_pairs={{0,4},{4,8},{8,12},{12,16},{16,20},{20,24},{24,28},{28,0},{1,5},{5... | collective-permute-start | bytes 983048 | tf_op jit(solution)/shard_map/ppermute | solution.py:303
  23.1 44.0 %collective-permute-start.1 = (bf16[160,1024]{1,0:T(8,128)(2,1)S(1)}, bf16[160,1024]{1,0:T(8,128)(2,1)S(1)}, u32[]{:S(2)}, u32[]{:S(2)}) collective-permute-start(bf16[160,1024]{1,0:T(8,128)(2,1)S(1)} %get-tuple-element.37), channel_id=1, source_target_pairs={{4,0},{8,4},{12,8},{16,12},{20,16},{24,20},{28,24},{0,28},{5,1},{9... | collective-permute-start | bytes 983048 | tf_op jit(solution)/shard_map/ppermute | solution.py:304
  26.5 0.7 copy-start.10
  26.5 0.7 copy-start.11
  26.5 0.7 copy-start.12
  62.3 10.7 %collective-permute-start.5 = (bf16[32,2176]{1,0:T(8,128)(2,1)}, bf16[32,2176]{1,0:T(8,128)(2,1)S(1)}, u32[]{:S(2)}, u32[]{:S(2)}) collective-permute-start(bf16[32,2176]{1,0:T(8,128)(2,1)} %get-tuple-element.29), channel_id=1, source_target_pairs={{0,1},{1,2},{2,3},{3,0},{4,5},{5,6},{6,7},{7,4},{8,9},{9,10},{10,1... | collective-permute-start | bytes 417800 | tf_op jit(solution)/shard_map/ppermute | solution.py:310
  64.7 10.1 %collective-permute-start.6 = (bf16[32,2176]{1,0:T(8,128)(2,1)}, bf16[32,2176]{1,0:T(8,128)(2,1)S(1)}, u32[]{:S(2)}, u32[]{:S(2)}) collective-permute-start(bf16[32,2176]{1,0:T(8,128)(2,1)} %get-tuple-element.30), channel_id=1, source_target_pairs={{0,2},{1,3},{2,0},{3,1},{4,6},{5,7},{6,4},{7,5},{8,10},{9,11},{10,... | collective-permute-start | bytes 417800 | tf_op jit(solution)/shard_map/ppermute | solution.py:310
  65.6 9.2 %collective-permute-start.7 = (bf16[32,2176]{1,0:T(8,128)(2,1)}, bf16[32,2176]{1,0:T(8,128)(2,1)S(1)}, u32[]{:S(2)}, u32[]{:S(2)}) collective-permute-start(bf16[32,2176]{1,0:T(8,128)(2,1)} %get-tuple-element.31), channel_id=1, source_target_pairs={{0,3},{1,0},{2,1},{3,2},{4,7},{5,4},{6,5},{7,6},{8,11},{9,8},{10,9... | collective-permute-start | bytes 417800 | tf_op jit(solution)/shard_map/ppermute | solution.py:310
  67.2 0.7 copy-start.8
  67.2 0.8 %copy-start.9 = (bf16[160,1024]{1,0:T(8,128)(2,1)}, bf16[160,1024]{1,0:T(8,128)(2,1)S(1)}, u32[]{:S(2)}) copy-start(bf16[160,1024]{1,0:T(8,128)(2,1)S(1)} %collective-permute-done.1.high_ref) | copy-start | bytes 983044
  73.0 1.9 %copy-start.3 = (bf16[32,2176]{1,0:T(8,128)(2,1)}, bf16[32,2176]{1,0:T(8,128)(2,1)S(1)}, u32[]{:S(2)}) copy-start(bf16[32,2176]{1,0:T(8,128)(2,1)S(1)} %collective-permute-done.5.refs_0_) | copy-start | bytes 417796
  74.9 0.7 copy-start.4
  74.9 0.7 copy-start.5

commit v4 on v3

--- a/solution.py
+++ b/solution.py
@@ -31,13 +31,22 @@
     return pl.CostEstimate(flops=40 * elements, bytes_accessed=1 << 20, transcendentals=elements)
 
 
-def uptake_sums(row0, seen_refs, first_ref, capacity_ref, affinity_ref, yield_ref, inverse_ref, mass_s,
-                growth_ref, flux_ref, consumed_ref, y_s, slopes_s, levels_s, slope_s, level_s, eaten_s):
+def column(row):
+    size = row.shape[1]
+    shape = (size, size)
+    own = lax.broadcasted_iota(jnp.int32, shape, 0) == lax.broadcasted_iota(jnp.int32, shape, 1)
+    return jnp.sum(jnp.where(own, jnp.broadcast_to(row, shape), 0.0), axis=1, keepdims=True)
+
+
+def uptake_sums(row0, seen_refs, first_ref, capacity_ref, affinity_ref, yield_ref, mass_s, growth_ref,
+                flux_ref, consumed_ref, y_s, slopes_s, levels_s, inverse_s, spread_s, eaten_s):
     rows, cells = y_s.shape
     strains, resources = capacity_ref.shape
     groups = strains // GROUP
     blocks = rows // GROUP
+    tiles = cells // LANES
     start = 0
+    eaten_s[0:GROUP] = jnp.zeros_like(eaten_s[0:GROUP])
     for ref in seen_refs:
         count = ref.shape[0]
         y_s[start : start + count, :] = 1.0 / ref[...].astype(f32)
@@ -46,22 +55,35 @@
     level = 1.0 / (capacity_ref[...] * yield_ref[...])
     slopes_s[...] = pltpu.roll(affinity_ref[...] * level, turn, 1)
     levels_s[...] = pltpu.roll(level, turn, 1)
+    inverse_s[...] = jnp.broadcast_to(1.0 / column(pltpu.roll(yield_ref[...], turn, 1))[:rows], inverse_s.shape)
+
+    shape = (GROUP, GROUP * GROUP)
+    ones = lax.broadcasted_iota(jnp.int32, shape, 1) // GROUP
+    ones = (ones == lax.broadcasted_iota(jnp.int32, shape, 0)).astype(f32).astype(bf16)
+
+    def sum_block(block):
+        part = pl.ds(pl.multiple_of(block * GROUP, GROUP), GROUP)
+        inverse = inverse_s[part, :1]
+        for tile in range(cells // WIDE):
+            lanes = slice(tile * WIDE, (tile + 1) * WIDE)
+            eaten = eaten_s[part, :, lanes].reshape(GROUP * GROUP, WIDE)
+            consumed_ref[part, lanes] = jnp.dot(ones, eaten, preferred_element_type=f32) * inverse
 
     def per_block(block, _):
         r0 = pl.multiple_of(block * GROUP, GROUP)
-        turn = lax.rem(resources - r0, resources)
-        members = [pl.ds(g * GROUP, GROUP) for g in range(groups)]
-        slopes = [pltpu.roll(slopes_s[m, :], turn, 1) for m in members]
-        levels = [pltpu.roll(levels_s[m, :], turn, 1) for m in members]
         for r in range(GROUP):
+            chosen = jnp.full((GROUP, LANES), r0 + r, jnp.int32)
             for g in range(groups):
-                slope_s[r, g] = jnp.broadcast_to(slopes[g][:, r : r + 1], (GROUP, LANES))
-                level_s[r, g] = jnp.broadcast_to(levels[g][:, r : r + 1], (GROUP, LANES))
+                members = slice(g * GROUP, (g + 1) * GROUP)
+                spread_s[0, r, g] = jnp.take_along_axis(slopes_s[members, :], chosen, axis=1)
+                spread_s[1, r, g] = jnp.take_along_axis(levels_s[members, :], chosen, axis=1)
+
+        sum_block(jnp.maximum(block - 1, 0))
 
         def per_tile(tile, _):
             lanes = pl.ds(pl.multiple_of(tile * LANES, LANES), LANES)
             y_rows = y_s[pl.ds(r0, GROUP), lanes]
-            inverse = inverse_ref[pl.ds(row0 + r0, GROUP), :]
+            inverse = inverse_s[pl.ds(r0, GROUP), :]
             growth = [growth_ref[g * GROUP : (g + 1) * GROUP, lanes] for g in range(groups)]
             flux = [None] * groups
             for r in range(GROUP):
@@ -69,7 +91,7 @@
                 scale = jnp.broadcast_to(inverse[r : r + 1], (GROUP, LANES)).astype(bf16)
                 eaten = None
                 for g in range(groups):
-                    gain = pl.reciprocal(slope_s[r, g] * y + level_s[r, g], approx=True)
+                    gain = pl.reciprocal(spread_s[0, r, g] * y + spread_s[1, r, g], approx=True)
                     growth[g] = growth[g] + gain
                     short = gain.astype(bf16)
                     taken = short * scale
@@ -83,23 +105,11 @@
                 flux_ref[strains, lanes] += flux[g].astype(f32)
             return 0
 
-        lax.fori_loop(0, cells // LANES, per_tile, 0)
+        lax.fori_loop(0, tiles, per_tile, 0, unroll=4)
         return 0
 
     lax.fori_loop(0, blocks, per_block, 0)
-
-    shape = (GROUP, GROUP * GROUP)
-    ones = lax.broadcasted_iota(jnp.int32, shape, 1) // GROUP
-    ones = (ones == lax.broadcasted_iota(jnp.int32, shape, 0)).astype(f32).astype(bf16)
-    for block in range(blocks):
-        part = slice(block * GROUP, (block + 1) * GROUP)
-        inverse = inverse_ref[row0 + block * GROUP : row0 + (block + 1) * GROUP, :1]
-        for tile in range(cells // WIDE):
-            lanes = slice(tile * WIDE, (tile + 1) * WIDE)
-            sums = jnp.dot(
-                ones, eaten_s[part, :, lanes].reshape(GROUP * GROUP, WIDE), preferred_element_type=f32
-            )
-            consumed_ref[part, lanes] = sums * inverse
+    sum_block(blocks - 1)
 
 
 def copy_mass(mass_ref, mass_s):
@@ -108,22 +118,25 @@
 
 def first_kernel(row0, parts, *refs):
     seen = refs[:parts]
-    coefficients, mass_ref = refs[parts : parts + 5], refs[parts + 5]
-    growth_ref, flux_ref, consumed_ref = refs[parts + 6 : parts + 9]
-    mass_s, *work = refs[parts + 9 :]
+    coefficients, mass_ref = refs[parts : parts + 4], refs[parts + 4]
+    growth_ref, flux_ref, consumed_ref = refs[parts + 5 : parts + 8]
+    mass_s, *work = refs[parts + 8 :]
     copy_mass(mass_ref, mass_s)
     growth_ref[...] = jnp.zeros_like(growth_ref)
     flux_ref[...] = jnp.zeros_like(flux_ref)
     uptake_sums(row0, seen, *coefficients, mass_s, growth_ref, flux_ref, consumed_ref, *work)
 
 
-def finish(flux_ref, mass_ref, secretion_ref, consumed_refs, net_refs):
+def finish(first_ref, flux_ref, mass_ref, secretion_ref, consumed_refs, net_refs):
     cells = flux_ref.shape[1]
+    resources = secretion_ref.shape[0]
+    turn = lax.rem(resources - first_ref[0], resources)
+    secretion = pltpu.roll(secretion_ref[...].astype(f32), turn, 0).astype(bf16)
     base = None
     for tile in range(cells // WIDE):
         lanes = slice(tile * WIDE, (tile + 1) * WIDE)
         product = (mass_ref[:, lanes].astype(f32) * flux_ref[:, lanes]).astype(bf16)
-        secreted = jnp.dot(secretion_ref[...], product, preferred_element_type=f32)
+        secreted = jnp.dot(secretion, product, preferred_element_type=f32)
         consumed = [ref[:, lanes] for ref in consumed_refs]
         net = secreted - (consumed[0] if len(consumed) == 1 else jnp.concatenate(consumed, axis=0))
         if base is None:
@@ -143,29 +156,29 @@
 
 def second_kernel(row0, parts, owners, *refs):
     seen = refs[:parts]
-    coefficients, mass_ref = refs[parts : parts + 5], refs[parts + 5]
-    growth_in, flux_in, consumed_in, secretion_ref = refs[parts + 6 : parts + 10]
-    growth_ref = refs[parts + 10]
-    net_refs = refs[parts + 11 : parts + 11 + owners]
-    flux_s, consumed_s, mass_s, *work = refs[parts + 11 + owners :]
+    coefficients, mass_ref = refs[parts : parts + 4], refs[parts + 4]
+    growth_in, flux_in, consumed_in, secretion_ref = refs[parts + 5 : parts + 9]
+    growth_ref = refs[parts + 9]
+    net_refs = refs[parts + 10 : parts + 10 + owners]
+    flux_s, consumed_s, mass_s, *work = refs[parts + 10 + owners :]
     copy_mass(mass_ref, mass_s)
     growth_ref[...] = growth_in[...]
     flux_s[...] = flux_in[...]
     uptake_sums(row0, seen, *coefficients, mass_s, growth_ref, flux_s, consumed_s, *work)
-    finish(flux_s, mass_ref, secretion_ref, (consumed_in, consumed_s), net_refs)
+    finish(coefficients[0], flux_s, mass_ref, secretion_ref, (consumed_in, consumed_s), net_refs)
 
 
 def only_kernel(row0, parts, owners, *refs):
     seen = refs[:parts]
-    coefficients, mass_ref, secretion_ref = refs[parts : parts + 5], refs[parts + 5], refs[parts + 6]
-    growth_ref = refs[parts + 7]
-    net_refs = refs[parts + 8 : parts + 8 + owners]
-    flux_s, consumed_s, mass_s, *work = refs[parts + 8 + owners :]
+    coefficients, mass_ref, secretion_ref = refs[parts : parts + 4], refs[parts + 4], refs[parts + 5]
+    growth_ref = refs[parts + 6]
+    net_refs = refs[parts + 7 : parts + 7 + owners]
+    flux_s, consumed_s, mass_s, *work = refs[parts + 7 + owners :]
     copy_mass(mass_ref, mass_s)
     growth_ref[...] = jnp.zeros_like(growth_ref)
     flux_s[...] = jnp.zeros_like(flux_s)
     uptake_sums(row0, seen, *coefficients, mass_s, growth_ref, flux_s, consumed_s, *work)
-    finish(flux_s, mass_ref, secretion_ref, (consumed_s,), net_refs)
+    finish(coefficients[0], flux_s, mass_ref, secretion_ref, (consumed_s,), net_refs)
 
 
 def work_space(rows, strains, cells, resources):
@@ -175,8 +188,8 @@
         pltpu.VMEM((rows, cells), f32),
         pltpu.VMEM((strains, resources), f32),
         pltpu.VMEM((strains, resources), f32),
-        pltpu.VMEM((GROUP, groups, GROUP, LANES), f32),
-        pltpu.VMEM((GROUP, groups, GROUP, LANES), f32),
+        pltpu.VMEM((rows, LANES), f32),
+        pltpu.VMEM((2, GROUP, groups, GROUP, LANES), f32),
         pltpu.VMEM((rows, GROUP, cells), bf16),
     ]
 
@@ -190,7 +203,7 @@
         jax.ShapeDtypeStruct((held, cells) if i == 0 else (held, cells + LANES), f32 if i == 0 else bf16)
         for i in range(total // held)
     )
-    given = [pl.BlockSpec(memory_space=pltpu.SMEM)] + [whole()] * 5
+    given = [pl.BlockSpec(memory_space=pltpu.SMEM)] + [whole()] * 4
     if held % GROUP:
         seen = jnp.concatenate([own] + others, axis=0)
         outs = pl.pallas_call(
@@ -248,13 +261,6 @@
     return [ref[rows, x * plane : (x + 1) * plane].astype(f32) for x in range(planes)]
 
 
-def column(row):
-    size = row.shape[1]
-    shape = (size, size)
-    own = lax.broadcasted_iota(jnp.int32, shape, 0) == lax.broadcasted_iota(jnp.int32, shape, 1)
-    return jnp.sum(jnp.where(own, jnp.broadcast_to(row, shape), 0.0), axis=1, keepdims=True)
-
-
 def step_kernel(planes, plane, mass_ref, field_ref, low_ref, high_ref, sum_ref, net_ref, maintenance_ref,
                 motility_ref, diffusivity_ref, supply_ref, growth_ref, new_ref, partial_ref, traits_s):
     strains = mass_ref.shape[0]
@@ -284,16 +290,6 @@
         lanes = slice(x * plane, (x + 1) * plane)
         change = diffusivity * spread[x] + net_ref[:, lanes] + supply
         partial_ref[:, lanes] = field[x] + time_step * change
-
-
-def close_kernel(planes, plane, partial_ref, *refs):
-    *arrived, new_ref = refs
-    cells = planes * plane
-    base = sum(ref[:, cells : cells + LANES].astype(f32) for ref in arrived)[:, :1]
-    for x in range(planes):
-        lanes = slice(x * plane, (x + 1) * plane)
-        net = sum(ref[:, lanes].astype(f32) for ref in arrived) + base
-        new_ref[:, x, :] = partial_ref[:, lanes] + time_step * net
 
 
 def halo(block, axis):
@@ -332,10 +328,7 @@
     others = [shifted(own, "species", -j) for j in range(1, count)]
     mass = biomass.reshape(strains, cells)
     first = lax.axis_index("species") * held
-    turned = lax.dynamic_slice_in_dim(jnp.concatenate([energy_yield, energy_yield]), first, total)
-    inverse = jnp.broadcast_to((1.0 / turned)[:, None], (total, LANES))
-    secretion = lax.dynamic_slice_in_dim(jnp.concatenate([secretion, secretion]), first, total, 0)
-    coefficients = (first[None].astype(jnp.int32), capacity, affinity, energy_yield[None, :], inverse)
+    coefficients = (first[None].astype(jnp.int32), capacity, affinity, energy_yield[None, :])
     edges = jnp.concatenate([biomass, resources.astype(bf16)], axis=0)
     low, high, gained, nets = exchange(own, others, coefficients, mass, secretion, edges)
     arrived = [shifted(nets[j], "species", j) for j in range(1, count)]
@@ -351,14 +344,8 @@
     )(mass, field, low, high, gained, nets[0], maintenance[None, :], motility[None, :],
       diffusivity[None, :], supply[None, :])
     arrived, partial = lax.optimization_barrier((arrived, partial))
-    new_resources = pl.pallas_call(
-        functools.partial(close_kernel, slab_rows, plane),
-        out_shape=jax.ShapeDtypeStruct(resources.shape, f32),
-        in_specs=[whole()] * count,
-        out_specs=whole(),
-        compiler_params=params(60),
-        cost_estimate=estimate(held * cells),
-    )(partial, *arrived)
+    received = sum(part[:, :cells].astype(f32) + part[:, cells : cells + 1].astype(f32) for part in arrived)
+    new_resources = (partial + time_step * received).reshape(resources.shape)
     return growth, new_biomass, new_resources
 
 

time: 78.4 us -> 73 us (0.931)
  Pallas kernels: 55 us -> 49.6 us
    pallas_call x1, Pallas kernels: 35 us -> 32.1 us  [exchange(): pl.pallas_call(functools.partial(second_kernel, held, len(others), len(ne...]
    pallas_call x1 -> x0, Pallas kernels: 1.97 us -> none  [per_device(): pl.pallas_call(functools.partial(close_kernel, slab_rows, plane), out_sha...]
    add x0 -> x3, other arithmetic: none -> 1.33 us  [the longest x1 1.11 us: per_device(): new_resources = (partial + time_step * received).reshape(resources.shape)]
    reshape x0 -> x1, local copies, waits for them, and re-layouts: none -> 0.92 us  [per_device(): new_resources = (partial + time_step * received).reshape(resources.shape)]
    unnamed x32 -> x22, local copies, waits for them, and re-layouts: 4.49 us -> 3.83 us
  transfers between devices with their start and end apart: 8 -> 8, of which waited for: 1 -> 1; matrix products, arithmetic and copies ran while one was open for 4% -> 2% of each run, Pallas kernels for 68% -> 69%
where the time goes in v4:
time: 73 us; the launch traced here: 72.2 us
  Pallas kernels  49.6 us (68%)
  starting transfers between devices  13.7 us (19%)
  local copies, waits for them, and re-layouts  4.79 us (7%)
  waiting for transfers between devices  1.96 us (3%)
  other arithmetic  1.39 us (2%)
  between operations  0.77 us (1%)
    pallas_call x1, Pallas kernels, exchange(): pl.pallas_call(functools.partial(second_kernel, held, len(others), len(ne...  32.1 us
    pallas_call x1, Pallas kernels, exchange(): pl.pallas_call(functools.partial(first_kernel, 0, 1), out_shape=(sums, su...  12.5 us
    ppermute x6, starting transfers between devices, shifted(): lax.ppermute(value, axis, [(i, (i + shift) % count) for i in range(count)])  11 us
    pallas_call x1, Pallas kernels, per_device(): pl.pallas_call(functools.partial(step_kernel, slab_rows, plane), out_shap...  4.93 us
    unnamed x22, local copies, waits for them, and re-layouts  3.83 us
    ppermute x1, starting transfers between devices, halo(): high = lax.ppermute(block[:, 0, :], axis, backward)  2.63 us
    ppermute x6, waiting for transfers between devices, shifted(): lax.ppermute(value, axis, [(i, (i + shift) % count) for i in range(count)])  1.96 us
  transfers between devices with their start and end apart: 8, of which 1 were waited for; matrix products, arithmetic and copies ran while one was open for 2% of the time, Pallas kernels for 69%

profile of v4, /device:TPU:0, one launch (start us, length us, event | category | flops | bytes accessed | tf_op | source)
XLA Modules:
  0.0 72.2 jit_solution(13472674929016283442)
XLA Ops:
  0.6 1.1 %copy.18 = f32[4,8,2,1024]{3,1,2,0:T(8,128)S(1)} copy(f32[4,8,2,1024]{3,2,1,0:T(2,128)} %bitcast.15) | data formatting | bytes 524288
  1.8 0.0 copy-start.2
  1.8 5.1 %collective-permute-start.2 = (bf16[32,2048]{1,0:T(8,128)(2,1)S(1)}, bf16[32,2048]{1,0:T(8,128)(2,1)S(1)}, u32[]{:S(2)}, u32[]{:S(2)}) collective-permute-start(bf16[32,2048]{1,0:T(8,128)(2,1)S(1)} %convert_element_type.19.refs_0_), channel_id=1, source_target_pairs={{0,3},{1,0},{2,1},{3,2},{4,7},{5,4},{6,5},{7,6},{8,11},{9,8},{10,9... | collective-permute-start | bytes 393224 | tf_op jit(solution)/shard_map/ppermute | solution.py:306
  6.9 0.0 collective-permute-start.3
  6.9 1.0 %collective-permute-start.4 = (bf16[32,2048]{1,0:T(8,128)(2,1)S(1)}, bf16[32,2048]{1,0:T(8,128)(2,1)S(1)}, u32[]{:S(2)}, u32[]{:S(2)}) collective-permute-start(bf16[32,2048]{1,0:T(8,128)(2,1)S(1)} %convert_element_type.19.refs_0_), channel_id=1, source_target_pairs={{0,1},{1,2},{2,3},{3,0},{4,5},{5,6},{6,7},{7,4},{8,9},{9,10},{10,1... | collective-permute-start | bytes 393224 | tf_op jit(solution)/shard_map/ppermute | solution.py:306
  7.9 0.1 copy.20
  8.0 0.1 copy.16
  8.1 1.0 %copy.17 = bf16[16,8,2,1024]{3,1,2,0:T(8,128)(2,1)} copy(bf16[16,8,2,1024]{3,2,1,0:T(2,128)(2,1)S(1)} %bitcast.14) | data formatting | bytes 1048576
  9.1 12.5 %shard_map.121 = (f32[128,2048]{1,0:T(8,128)}, f32[128,2048]{1,0:T(8,128)}, f32[32,2048]{1,0:T(8,128)}) custom-call(bf16[32,2048]{1,0:T(8,128)(2,1)} %copy-done.3, s32[1]{0:T(128)} %bitcast.refs_1_.refs_3_, f32[128,128]{1,0:T(8,128)} %refs_4_.1, f32[128,128]{1,0:T(8,128)} %refs_5_.1, f32[1,128]{1,0:T(1,128)} %bitcast.21, bf16[128,2048]{1,0:T(8,128)(2,1)} %bitcast.18), custom_call_target="tpu_custom_call" | custom-call | flops 335544320 | bytes 1048576 | tf_op jit(solution)/shard_map/pallas_call | solution.py:220
  21.7 0.1 collective-permute-start
  21.8 2.6 %collective-permute-start.1 = (bf16[160,1024]{1,0:T(8,128)(2,1)S(1)}, bf16[160,1024]{1,0:T(8,128)(2,1)S(1)}, u32[]{:S(2)}, u32[]{:S(2)}) collective-permute-start(bf16[160,1024]{1,0:T(8,128)(2,1)S(1)} %get-tuple-element.37), channel_id=1, source_target_pairs={{4,0},{8,4},{12,8},{16,12},{20,16},{24,20},{28,24},{0,28},{5,1},{9... | collective-permute-start | bytes 983048 | tf_op jit(solution)/shard_map/ppermute | solution.py:300
  24.4 0.0 collective-permute-done.2.refs_0_
  24.4 0.0 collective-permute-done.4.refs_2_
  24.4 0.6 copy-done.6
  25.1 0.1 copy-done.7
  25.1 0.0 copy-done.8
  25.2 32.1 %shard_map.122 = (f32[128,2048]{1,0:T(8,128)}, f32[32,2048]{1,0:T(8,128)}, bf16[32,2176]{1,0:T(8,128)(2,1)}, bf16[32,2176]{1,0:T(8,128)(2,1)}, bf16[32,2176]{1,0:T(8,128)(2,1)}) custom-call(bf16[32,2048]{1,0:T(8,128)(2,1)} %copy-done.6, bf16[32,2048]{1,0:T(8,128)(2,1)} %copy-done.7, bf16[32,2048]{1,0:T(8,128)(2,1)} %copy-done.8, s32[1]{0:T(128)} %bitcast.refs_1_.refs_3_, ...), custom_call_target="tpu_custom_call" | custom-call | flops 1006632960 | bytes 1048576 | tf_op jit(solution)/shard_map/pallas_call | solution.py:232
  57.3 2.5 %collective-permute-start.5 = (bf16[32,2176]{1,0:T(8,128)(2,1)}, bf16[32,2176]{1,0:T(8,128)(2,1)S(1)}, u32[]{:S(2)}, u32[]{:S(2)}) collective-permute-start(bf16[32,2176]{1,0:T(8,128)(2,1)} %get-tuple-element.29), channel_id=1, source_target_pairs={{0,1},{1,2},{2,3},{3,0},{4,5},{5,6},{6,7},{7,4},{8,9},{9,10},{10,1... | collective-permute-start | bytes 417800 | tf_op jit(solution)/shard_map/ppermute | solution.py:306
  59.8 0.9 %collective-permute-start.6 = (bf16[32,2176]{1,0:T(8,128)(2,1)}, bf16[32,2176]{1,0:T(8,128)(2,1)S(1)}, u32[]{:S(2)}, u32[]{:S(2)}) collective-permute-start(bf16[32,2176]{1,0:T(8,128)(2,1)} %get-tuple-element.30), channel_id=1, source_target_pairs={{0,2},{1,3},{2,0},{3,1},{4,6},{5,7},{6,4},{7,5},{8,10},{9,11},{10,... | collective-permute-start | bytes 417800 | tf_op jit(solution)/shard_map/ppermute | solution.py:306
  60.7 1.5 %collective-permute-start.7 = (bf16[32,2176]{1,0:T(8,128)(2,1)}, bf16[32,2176]{1,0:T(8,128)(2,1)S(1)}, u32[]{:S(2)}, u32[]{:S(2)}) collective-permute-start(bf16[32,2176]{1,0:T(8,128)(2,1)} %get-tuple-element.31), channel_id=1, source_target_pairs={{0,3},{1,0},{2,1},{3,2},{4,7},{5,4},{6,5},{7,6},{8,11},{9,8},{10,9... | collective-permute-start | bytes 417800 | tf_op jit(solution)/shard_map/ppermute | solution.py:306
  62.1 0.0 collective-permute-done.low_ref
  62.1 0.0 collective-permute-done.1.high_ref
  62.2 0.7 copy-done.4
  62.9 0.1 copy-done.5
  63.0 4.9 %shard_map.123 = (f32[128,2,1024]{2,1,0:T(2,128)}, f32[128,2,1024]{2,1,0:T(2,128)}, f32[32,2048]{1,0:T(8,128)}) custom-call(bf16[128,2048]{1,0:T(8,128)(2,1)} %bitcast.20, f32[32,2048]{1,0:T(8,128)} %bitcast.17, bf16[160,1024]{1,0:T(8,128)(2,1)} %copy-done.4, bf16[160,1024]{1,0:T(8,128)(2,1)} %copy-done.5, f32[128,2048]{1,0:T(8,128)} %get-tuple-element.25.sum_ref, ...), custom_call_target="tpu_custom_call" | custom-call | flops 83886080 | bytes 1048576 | tf_op jit(solution)/shard_map/pallas_call | solution.py:336
  67.9 0.0 collective-permute-done.5
  67.9 1.9 %collective-permute-done.6 = bf16[32,2176]{1,0:T(8,128)(2,1)S(1)} collective-permute-done((bf16[32,2176]{1,0:T(8,128)(2,1)}, bf16[32,2176]{1,0:T(8,128)(2,1)S(1)}, u32[]{:S(2)}, u32[]{:S(2)}) %collective-permute-start.6) | collective-permute-done | bytes 139296 | tf_op jit(solution)/shard_map/ppermute | solution.py:306
  69.9 0.0 collective-permute-done.7
  69.9 0.1 convert_reduce_fusion.2
  70.0 0.1 convert_reduce_fusion
  70.1 1.1 %multiply_add_fusion = f32[32,2048]{1,0:T(8,128)S(1)} fusion(f32[32,2048]{1,0:T(8,128)} %get-tuple-element.33, f32[32]{0:T(128)S(1)} %get-tuple-element.39, bf16[32,2176]{1,0:T(8,128)(2,1)S(1)} %collective-permute-done.7, f32[32]{0:T(128)S(1)} %get-tuple-element.40, bf16[32,2176]{1,0:T(8,128)(2,1)S(1)} %collective-permute-done.6, ...), kind=kLoop, calls=%fused_computation.4 | loop fusion | flops 655360 | bytes 917888 | tf_op jit(solution)/shard_map/add | solution.py:348
  71.2 0.9 %reshape.17 = f32[32,2,1024]{2,1,0:T(2,128)} reshape(f32[32,2048]{1,0:T(8,128)S(1)} %multiply_add_fusion) | data formatting | bytes 524288 | tf_op jit(solution)/shard_map/reshape | solution.py:348
  (16 shorter events, 0.1 us)
Async XLA Ops:
  0.6 7.3 %copy-start.1 = (f32[32,2,1024]{2,1,0:T(2,128)S(1)}, f32[32,2,1024]{2,1,0:T(2,128)}, u32[]{:S(2)}) copy-start(f32[32,2,1024]{2,1,0:T(2,128)} %param.11) | copy-start | bytes 786436
  0.6 7.4 %copy-start = (bf16[128,2,1024]{2,1,0:T(2,128)(2,1)S(1)}, bf16[128,2,1024]{2,1,0:T(2,128)(2,1)}, u32[]{:S(2)}) copy-start(bf16[128,2,1024]{2,1,0:T(2,128)(2,1)} %param.10) | copy-start | bytes 1572868
  1.8 7.3 %copy-start.2 = (f32[4,8,2,1024]{3,1,2,0:T(8,128)}, f32[4,8,2,1024]{3,1,2,0:T(8,128)S(1)}, u32[]{:S(2)}) copy-start(f32[4,8,2,1024]{3,1,2,0:T(8,128)S(1)} %copy.18) | copy-start | bytes 786436
  1.8 7.3 %copy-start.3 = (bf16[32,2048]{1,0:T(8,128)(2,1)}, bf16[32,2048]{1,0:T(8,128)(2,1)S(1)}, u32[]{:S(2)}) copy-start(bf16[32,2048]{1,0:T(8,128)(2,1)S(1)} %convert_element_type.19.refs_0_) | copy-start | bytes 393220
  1.8 22.6 %collective-permute-start.2 = (bf16[32,2048]{1,0:T(8,128)(2,1)S(1)}, bf16[32,2048]{1,0:T(8,128)(2,1)S(1)}, u32[]{:S(2)}, u32[]{:S(2)}) collective-permute-start(bf16[32,2048]{1,0:T(8,128)(2,1)S(1)} %convert_element_type.19.refs_0_), channel_id=1, source_target_pairs={{0,3},{1,0},{2,1},{3,2},{4,7},{5,4},{6,5},{7,6},{8,11},{9,8},{10,9... | collective-permute-start | bytes 393224 | tf_op jit(solution)/shard_map/ppermute | solution.py:306
  6.9 17.5 %collective-permute-start.3 = (bf16[32,2048]{1,0:T(8,128)(2,1)S(1)}, bf16[32,2048]{1,0:T(8,128)(2,1)S(1)}, u32[]{:S(2)}, u32[]{:S(2)}) collective-permute-start(bf16[32,2048]{1,0:T(8,128)(2,1)S(1)} %convert_element_type.19.refs_0_), channel_id=1, source_target_pairs={{0,2},{1,3},{2,0},{3,1},{4,6},{5,7},{6,4},{7,5},{8,10},{9,11},{10,... | collective-permute-start | bytes 393224 | tf_op jit(solution)/shard_map/ppermute | solution.py:306
  6.9 17.5 %collective-permute-start.4 = (bf16[32,2048]{1,0:T(8,128)(2,1)S(1)}, bf16[32,2048]{1,0:T(8,128)(2,1)S(1)}, u32[]{:S(2)}, u32[]{:S(2)}) collective-permute-start(bf16[32,2048]{1,0:T(8,128)(2,1)S(1)} %convert_element_type.19.refs_0_), channel_id=1, source_target_pairs={{0,1},{1,2},{2,3},{3,0},{4,5},{5,6},{6,7},{7,4},{8,9},{9,10},{10,1... | collective-permute-start | bytes 393224 | tf_op jit(solution)/shard_map/ppermute | solution.py:306
  21.7 40.4 %collective-permute-start = (bf16[160,1024]{1,0:T(8,128)(2,1)S(1)}, bf16[160,1024]{1,0:T(8,128)(2,1)S(1)}, u32[]{:S(2)}, u32[]{:S(2)}) collective-permute-start(bf16[160,1024]{1,0:T(8,128)(2,1)S(1)} %get-tuple-element.38), channel_id=1, source_target_pairs={{0,4},{4,8},{8,12},{12,16},{16,20},{20,24},{24,28},{28,0},{1,5},{5... | collective-permute-start | bytes 983048 | tf_op jit(solution)/shard_map/ppermute | solution.py:299
  21.8 40.4 %collective-permute-start.1 = (bf16[160,1024]{1,0:T(8,128)(2,1)S(1)}, bf16[160,1024]{1,0:T(8,128)(2,1)S(1)}, u32[]{:S(2)}, u32[]{:S(2)}) collective-permute-start(bf16[160,1024]{1,0:T(8,128)(2,1)S(1)} %get-tuple-element.37), channel_id=1, source_target_pairs={{4,0},{8,4},{12,8},{16,12},{20,16},{24,20},{28,24},{0,28},{5,1},{9... | collective-permute-start | bytes 983048 | tf_op jit(solution)/shard_map/ppermute | solution.py:300
  24.4 0.7 copy-start.6
  24.4 0.7 copy-start.7
  24.4 0.7 %copy-start.8 = (bf16[32,2048]{1,0:T(8,128)(2,1)}, bf16[32,2048]{1,0:T(8,128)(2,1)S(1)}, u32[]{:S(2)}) copy-start(bf16[32,2048]{1,0:T(8,128)(2,1)S(1)} %collective-permute-done.4.refs_2_) | copy-start | bytes 393220
  57.3 10.7 %collective-permute-start.5 = (bf16[32,2176]{1,0:T(8,128)(2,1)}, bf16[32,2176]{1,0:T(8,128)(2,1)S(1)}, u32[]{:S(2)}, u32[]{:S(2)}) collective-permute-start(bf16[32,2176]{1,0:T(8,128)(2,1)} %get-tuple-element.29), channel_id=1, source_target_pairs={{0,1},{1,2},{2,3},{3,0},{4,5},{5,6},{6,7},{7,4},{8,9},{9,10},{10,1... | collective-permute-start | bytes 417800 | tf_op jit(solution)/shard_map/ppermute | solution.py:306
  59.8 10.1 %collective-permute-start.6 = (bf16[32,2176]{1,0:T(8,128)(2,1)}, bf16[32,2176]{1,0:T(8,128)(2,1)S(1)}, u32[]{:S(2)}, u32[]{:S(2)}) collective-permute-start(bf16[32,2176]{1,0:T(8,128)(2,1)} %get-tuple-element.30), channel_id=1, source_target_pairs={{0,2},{1,3},{2,0},{3,1},{4,6},{5,7},{6,4},{7,5},{8,10},{9,11},{10,... | collective-permute-start | bytes 417800 | tf_op jit(solution)/shard_map/ppermute | solution.py:306
  60.7 9.2 %collective-permute-start.7 = (bf16[32,2176]{1,0:T(8,128)(2,1)}, bf16[32,2176]{1,0:T(8,128)(2,1)S(1)}, u32[]{:S(2)}, u32[]{:S(2)}) collective-permute-start(bf16[32,2176]{1,0:T(8,128)(2,1)} %get-tuple-element.31), channel_id=1, source_target_pairs={{0,3},{1,0},{2,1},{3,2},{4,7},{5,4},{6,5},{7,6},{8,11},{9,8},{10,9... | collective-permute-start | bytes 417800 | tf_op jit(solution)/shard_map/ppermute | solution.py:306
  62.1 0.7 %copy-start.4 = (bf16[160,1024]{1,0:T(8,128)(2,1)}, bf16[160,1024]{1,0:T(8,128)(2,1)S(1)}, u32[]{:S(2)}) copy-start(bf16[160,1024]{1,0:T(8,128)(2,1)S(1)} %collective-permute-done.low_ref) | copy-start | bytes 983044
  62.2 0.9 %copy-start.5 = (bf16[160,1024]{1,0:T(8,128)(2,1)}, bf16[160,1024]{1,0:T(8,128)(2,1)S(1)}, u32[]{:S(2)}) copy-start(bf16[160,1024]{1,0:T(8,128)(2,1)S(1)} %collective-permute-done.1.high_ref) | copy-start | bytes 983044

commit v5 on v4

--- a/solution.py
+++ b/solution.py
@@ -213,7 +213,7 @@
             out_specs=(whole(),) * (1 + len(nets)),
             scratch_shapes=[pltpu.VMEM((strains, cells), f32), pltpu.VMEM((total, cells), f32)]
             + work_space(total, strains, cells, total),
-            compiler_params=params(60),
+            compiler_params=params(28),
             cost_estimate=estimate(total * strains * cells),
         )(seen, *coefficients, mass, secretion)
         return *halo(edges, "space"), outs[0], outs[1:]
@@ -223,7 +223,7 @@
         in_specs=[whole()] + given,
         out_specs=(whole(),) * 3,
         scratch_shapes=work_space(held, strains, cells, total),
-        compiler_params=params(60),
+        compiler_params=params(28),
         cost_estimate=estimate(held * strains * cells),
     )(own, *coefficients, mass)
     edges, consumed = lax.optimization_barrier((edges, consumed))
@@ -236,7 +236,7 @@
         out_specs=(whole(),) * (1 + len(nets)),
         scratch_shapes=[pltpu.VMEM((strains, cells), f32), pltpu.VMEM((rest, cells), f32)]
         + work_space(rest, strains, cells, total),
-        compiler_params=params(60),
+        compiler_params=params(28),
         cost_estimate=estimate(rest * strains * cells),
     )(*others, *coefficients, mass, growth, flux, consumed, secretion)
     return low, high, outs[0], outs[1:]
@@ -339,12 +339,14 @@
         in_specs=[whole()] * 10,
         out_specs=(whole(),) * 3,
         scratch_shapes=[pltpu.VMEM((strains, LANES), f32)],
-        compiler_params=params(60),
+        compiler_params=params(28),
         cost_estimate=estimate(strains * cells * 8),
     )(mass, field, low, high, gained, nets[0], maintenance[None, :], motility[None, :],
       diffusivity[None, :], supply[None, :])
     arrived, partial = lax.optimization_barrier((arrived, partial))
-    received = sum(part[:, :cells].astype(f32) + part[:, cells : cells + 1].astype(f32) for part in arrived)
+    received = sum(part[:, :cells].astype(f32) for part in arrived)
+    base = sum(part[:, cells:].astype(f32) for part in arrived)
+    received = received + jnp.concatenate([base] * (cells // LANES), axis=1)
     new_resources = (partial + time_step * received).reshape(resources.shape)
     return growth, new_biomass, new_resources
 

time: 73 us -> 65.1 us (0.89)
  Pallas kernels: 49.6 us -> 41.9 us
  waiting for transfers between devices: 1.96 us -> 4.38 us
  local copies, waits for them, and re-layouts: 4.79 us -> 3.15 us
  other arithmetic: 1.39 us -> 0.15 us
    pallas_call x1, Pallas kernels: 32.1 us -> 28.8 us  [exchange(): pl.pallas_call(functools.partial(second_kernel, held, len(others), len(ne...]
    pallas_call x1, Pallas kernels: 12.5 us -> 10 us  [exchange(): pl.pallas_call(functools.partial(first_kernel, 0, 1), out_shape=(sums, su...]
    ppermute x6, waiting for transfers between devices: 1.96 us -> 4.37 us  [shifted(): lax.ppermute(value, axis, [(i, (i + shift) % count) for i in range(count)])]
    pallas_call x1, Pallas kernels: 4.93 us -> 3.09 us  [per_device(): pl.pallas_call(functools.partial(step_kernel, slab_rows, plane), out_shap...]
    unnamed x22 -> x38, local copies, waits for them, and re-layouts: 3.83 us -> 2.17 us
    add x1, other arithmetic: 1.11 us -> 0.08 us  [per_device(): new_resources = (partial + time_step * received).reshape(resources.shape)]
  transfers between devices with their start and end apart: 8 -> 8, of which waited for: 1 -> 2; matrix products, arithmetic and copies ran while one was open for 2% -> 1% of each run, Pallas kernels for 69% -> 65%
where the time goes in v5:
time: 65.1 us; the launch traced here: 64.3 us
  Pallas kernels  41.9 us (64%)
  starting transfers between devices  13.8 us (21%)
  waiting for transfers between devices  4.38 us (7%)
  local copies, waits for them, and re-layouts  3.15 us (5%)
  between operations  0.95 us (1%)
    pallas_call x1, Pallas kernels, exchange(): pl.pallas_call(functools.partial(second_kernel, held, len(others), len(ne...  28.8 us
    ppermute x6, starting transfers between devices, shifted(): lax.ppermute(value, axis, [(i, (i + shift) % count) for i in range(count)])  11.1 us
    pallas_call x1, Pallas kernels, exchange(): pl.pallas_call(functools.partial(first_kernel, 0, 1), out_shape=(sums, su...  10 us
    ppermute x6, waiting for transfers between devices, shifted(): lax.ppermute(value, axis, [(i, (i + shift) % count) for i in range(count)])  4.37 us
    pallas_call x1, Pallas kernels, per_device(): pl.pallas_call(functools.partial(step_kernel, slab_rows, plane), out_shap...  3.09 us
    ppermute x1, starting transfers between devices, halo(): high = lax.ppermute(block[:, 0, :], axis, backward)  2.63 us
    unnamed x38, local copies, waits for them, and re-layouts  2.17 us
  transfers between devices with their start and end apart: 8, of which 2 were waited for; matrix products, arithmetic and copies ran while one was open for 1% of the time, Pallas kernels for 65%

profile of v5, /device:TPU:0, one launch (start us, length us, event | category | flops | bytes accessed | tf_op | source)
XLA Modules:
  0.0 64.3 jit_solution(7504820539341933431)
XLA Ops:
  0.6 1.1 %copy.16 = f32[4,8,2,1024]{3,1,2,0:T(8,128)S(1)} copy(f32[4,8,2,1024]{3,2,1,0:T(2,128)} %bitcast.26) | data formatting | bytes 524288
  1.8 5.1 %collective-permute-start.2 = (bf16[32,2048]{1,0:T(8,128)(2,1)S(1)}, bf16[32,2048]{1,0:T(8,128)(2,1)S(1)}, u32[]{:S(2)}, u32[]{:S(2)}) collective-permute-start(bf16[32,2048]{1,0:T(8,128)(2,1)S(1)} %convert_element_type.25.refs_0_), channel_id=1, source_target_pairs={{0,3},{1,0},{2,1},{3,2},{4,7},{5,4},{6,5},{7,6},{8,11},{9,8},{10,9... | collective-permute-start | bytes 393224 | tf_op jit(solution)/shard_map/ppermute | solution.py:306
  6.9 0.0 collective-permute-start.3
  6.9 1.0 %collective-permute-start.4 = (bf16[32,2048]{1,0:T(8,128)(2,1)S(1)}, bf16[32,2048]{1,0:T(8,128)(2,1)S(1)}, u32[]{:S(2)}, u32[]{:S(2)}) collective-permute-start(bf16[32,2048]{1,0:T(8,128)(2,1)S(1)} %convert_element_type.25.refs_0_), channel_id=1, source_target_pairs={{0,1},{1,2},{2,3},{3,0},{4,5},{5,6},{6,7},{7,4},{8,9},{9,10},{10,1... | collective-permute-start | bytes 393224 | tf_op jit(solution)/shard_map/ppermute | solution.py:306
  7.9 0.1 copy.18
  8.0 0.1 copy.14
  8.1 0.0 copy-start
  8.1 0.0 copy-start.1
  8.1 0.0 copy-start.3
  8.1 0.1 copy.15
  8.3 0.6 copy-done
  9.0 0.0 copy-done.1
  9.0 10.0 %shard_map.121 = (f32[128,2048]{1,0:T(8,128)S(1)}, f32[128,2048]{1,0:T(8,128)S(1)}, f32[32,2048]{1,0:T(8,128)S(1)}) custom-call(bf16[32,2048]{1,0:T(8,128)(2,1)S(1)} %convert_element_type.25.refs_0_, s32[1]{0:T(128)} %bitcast.refs_1_.refs_3_, f32[128,128]{1,0:T(8,128)S(1)} %copy-done, f32[128,128]{1,0:T(8,128)S(1)} %copy-done.1, f32[1,128]{1,0:T(1,128)S(1)} %bitcast.19, ...), custom_call_target="tpu_custom_call" | custom-call | flops 335544320 | bytes 1048576 | tf_op jit(solution)/shard_map/pallas_call | solution.py:220
  19.0 0.1 slice_bitcast_fusion
  19.1 0.1 collective-permute-start
  19.1 2.6 %collective-permute-start.1 = (bf16[160,1024]{1,0:T(8,128)(2,1)S(1)}, bf16[160,1024]{1,0:T(8,128)(2,1)S(1)}, u32[]{:S(2)}, u32[]{:S(2)}) collective-permute-start(bf16[160,1024]{1,0:T(8,128)(2,1)S(1)} %get-tuple-element.39), channel_id=1, source_target_pairs={{4,0},{8,4},{12,8},{16,12},{20,16},{24,20},{28,24},{0,28},{5,1},{9... | collective-permute-start | bytes 983048 | tf_op jit(solution)/shard_map/ppermute | solution.py:300
  21.8 0.0 collective-permute-done.2.refs_0_
  21.8 0.0 collective-permute-done.3.refs_1_
  21.8 0.0 collective-permute-done.4.refs_2_
  21.8 0.0 copy-start.4
  21.8 0.0 copy-start.5
  21.8 0.0 copy-start.6
  21.8 0.0 copy-start.7
  21.8 28.8 %shard_map.122 = (f32[128,2048]{1,0:T(8,128)S(1)}, f32[32,2048]{1,0:T(8,128)S(1)}, bf16[32,2176]{1,0:T(8,128)(2,1)S(1)}, bf16[32,2176]{1,0:T(8,128)(2,1)S(1)}, bf16[32,2176]{1,0:T(8,128)(2,1)S(1)}) custom-call(bf16[32,2048]{1,0:T(8,128)(2,1)S(1)} %collective-permute-done.2.refs_0_, bf16[32,2048]{1,0:T(8,128)(2,1)S(1)} %collective-permute-done.3.refs_1_, ...), custom_call_target="tpu_custom_call" | custom-call | flops 1006632960 | bytes 1048576 | tf_op jit(solution)/shard_map/pallas_call | solution.py:232
  50.7 2.5 %collective-permute-start.5 = (bf16[32,2176]{1,0:T(8,128)(2,1)S(1)}, bf16[32,2176]{1,0:T(8,128)(2,1)S(1)}, u32[]{:S(2)}, u32[]{:S(2)}) collective-permute-start(bf16[32,2176]{1,0:T(8,128)(2,1)S(1)} %get-tuple-element.29), channel_id=1, source_target_pairs={{0,1},{1,2},{2,3},{3,0},{4,5},{5,6},{6,7},{7,4},{8,9},{9,10},{10,1... | collective-permute-start | bytes 417800 | tf_op jit(solution)/shard_map/ppermute | solution.py:306
  53.2 0.9 %collective-permute-start.6 = (bf16[32,2176]{1,0:T(8,128)(2,1)S(1)}, bf16[32,2176]{1,0:T(8,128)(2,1)S(1)}, u32[]{:S(2)}, u32[]{:S(2)}) collective-permute-start(bf16[32,2176]{1,0:T(8,128)(2,1)S(1)} %get-tuple-element.30), channel_id=1, source_target_pairs={{0,2},{1,3},{2,0},{3,1},{4,6},{5,7},{6,4},{7,5},{8,10},{9,11},{10,... | collective-permute-start | bytes 417800 | tf_op jit(solution)/shard_map/ppermute | solution.py:306
  54.1 1.5 %collective-permute-start.7 = (bf16[32,2176]{1,0:T(8,128)(2,1)S(1)}, bf16[32,2176]{1,0:T(8,128)(2,1)S(1)}, u32[]{:S(2)}, u32[]{:S(2)}) collective-permute-start(bf16[32,2176]{1,0:T(8,128)(2,1)S(1)} %get-tuple-element.31), channel_id=1, source_target_pairs={{0,3},{1,0},{2,1},{3,2},{4,7},{5,4},{6,5},{7,6},{8,11},{9,8},{10,9... | collective-permute-start | bytes 417800 | tf_op jit(solution)/shard_map/ppermute | solution.py:306
  55.7 3.1 %shard_map.123 = (f32[128,2,1024]{2,1,0:T(2,128)}, f32[128,2,1024]{2,1,0:T(2,128)}, f32[32,2048]{1,0:T(8,128)S(1)}) custom-call(bf16[128,2048]{1,0:T(8,128)(2,1)S(1)} %bitcast.18, f32[32,2048]{1,0:T(8,128)S(1)} %bitcast.15, bf16[160,1024]{1,0:T(8,128)(2,1)S(1)} %collective-permute-done.low_ref, bf16[160,1024]{1,0:T(8,128)(2,1)S(1)} %collective-permute-done.1.high_ref, ...), custom_call_target="tpu_custom_call" | custom-call | flops 83886080 | bytes 1048576 | tf_op jit(solution)/shard_map/pallas_call | solution.py:336
  58.8 0.5 collective-permute-done.5
  59.2 3.9 %collective-permute-done.6 = bf16[32,2176]{1,0:T(8,128)(2,1)S(1)} collective-permute-done((bf16[32,2176]{1,0:T(8,128)(2,1)S(1)}, bf16[32,2176]{1,0:T(8,128)(2,1)S(1)}, u32[]{:S(2)}, u32[]{:S(2)}) %collective-permute-start.6) | collective-permute-done | bytes 139296 | tf_op jit(solution)/shard_map/ppermute | solution.py:306
  63.3 0.1 multiply_add_fusion
  63.4 0.9 %reshape.17 = f32[32,2,1024]{2,1,0:T(2,128)} reshape(f32[32,2048]{1,0:T(8,128)S(1)} %multiply_add_fusion) | data formatting | bytes 524288 | tf_op jit(solution)/shard_map/reshape | solution.py:350
  (32 shorter events, 0.2 us)
Async XLA Ops:
  0.6 7.3 %copy-start.9 = (f32[32,2,1024]{2,1,0:T(2,128)S(1)}, f32[32,2,1024]{2,1,0:T(2,128)}, u32[]{:S(2)}) copy-start(f32[32,2,1024]{2,1,0:T(2,128)} %param.11) | copy-start | bytes 786436
  0.6 7.3 %copy-start.8 = (bf16[128,2,1024]{2,1,0:T(2,128)(2,1)S(1)}, bf16[128,2,1024]{2,1,0:T(2,128)(2,1)}, u32[]{:S(2)}) copy-start(bf16[128,2,1024]{2,1,0:T(2,128)(2,1)} %param.10) | copy-start | bytes 1572868
  1.8 20.0 %collective-permute-start.2 = (bf16[32,2048]{1,0:T(8,128)(2,1)S(1)}, bf16[32,2048]{1,0:T(8,128)(2,1)S(1)}, u32[]{:S(2)}, u32[]{:S(2)}) collective-permute-start(bf16[32,2048]{1,0:T(8,128)(2,1)S(1)} %convert_element_type.25.refs_0_), channel_id=1, source_target_pairs={{0,3},{1,0},{2,1},{3,2},{4,7},{5,4},{6,5},{7,6},{8,11},{9,8},{10,9... | collective-permute-start | bytes 393224 | tf_op jit(solution)/shard_map/ppermute | solution.py:306
  6.9 14.9 %collective-permute-start.3 = (bf16[32,2048]{1,0:T(8,128)(2,1)S(1)}, bf16[32,2048]{1,0:T(8,128)(2,1)S(1)}, u32[]{:S(2)}, u32[]{:S(2)}) collective-permute-start(bf16[32,2048]{1,0:T(8,128)(2,1)S(1)} %convert_element_type.25.refs_0_), channel_id=1, source_target_pairs={{0,2},{1,3},{2,0},{3,1},{4,6},{5,7},{6,4},{7,5},{8,10},{9,11},{10,... | collective-permute-start | bytes 393224 | tf_op jit(solution)/shard_map/ppermute | solution.py:306
  6.9 14.9 %collective-permute-start.4 = (bf16[32,2048]{1,0:T(8,128)(2,1)S(1)}, bf16[32,2048]{1,0:T(8,128)(2,1)S(1)}, u32[]{:S(2)}, u32[]{:S(2)}) collective-permute-start(bf16[32,2048]{1,0:T(8,128)(2,1)S(1)} %convert_element_type.25.refs_0_), channel_id=1, source_target_pairs={{0,1},{1,2},{2,3},{3,0},{4,5},{5,6},{6,7},{7,4},{8,9},{9,10},{10,1... | collective-permute-start | bytes 393224 | tf_op jit(solution)/shard_map/ppermute | solution.py:306
  8.1 0.8 %copy-start = (f32[128,128]{1,0:T(8,128)S(1)}, f32[128,128]{1,0:T(8,128)}, u32[]{:S(2)}) copy-start(f32[128,128]{1,0:T(8,128)} %refs_4_.1) | copy-start | bytes 196612
  8.1 0.9 %copy-start.1 = (f32[128,128]{1,0:T(8,128)S(1)}, f32[128,128]{1,0:T(8,128)}, u32[]{:S(2)}) copy-start(f32[128,128]{1,0:T(8,128)} %refs_5_.1) | copy-start | bytes 196612
  8.1 0.9 %copy-start.3 = (f32[128]{0:T(128)S(1)}, f32[128]{0:T(128)}, u32[]{:S(2)}) copy-start(f32[128]{0:T(128)} %param.15) | copy-start | bytes 1540
  19.0 2.8 %copy-start.2 = (bf16[128,128]{1,0:T(8,128)(2,1)S(1)}, bf16[128,128]{1,0:T(8,128)(2,1)}, u32[]{:S(2)}) copy-start(bf16[128,128]{1,0:T(8,128)(2,1)} %refs_11_.1) | copy-start | bytes 98308
  19.1 36.6 %collective-permute-start = (bf16[160,1024]{1,0:T(8,128)(2,1)S(1)}, bf16[160,1024]{1,0:T(8,128)(2,1)S(1)}, u32[]{:S(2)}, u32[]{:S(2)}) collective-permute-start(bf16[160,1024]{1,0:T(8,128)(2,1)S(1)} %get-tuple-element.40), channel_id=1, source_target_pairs={{0,4},{4,8},{8,12},{12,16},{16,20},{20,24},{24,28},{28,0},{1,5},{5... | collective-permute-start | bytes 983048 | tf_op jit(solution)/shard_map/ppermute | solution.py:299
  19.1 36.5 %collective-permute-start.1 = (bf16[160,1024]{1,0:T(8,128)(2,1)S(1)}, bf16[160,1024]{1,0:T(8,128)(2,1)S(1)}, u32[]{:S(2)}, u32[]{:S(2)}) collective-permute-start(bf16[160,1024]{1,0:T(8,128)(2,1)S(1)} %get-tuple-element.39), channel_id=1, source_target_pairs={{4,0},{8,4},{12,8},{16,12},{20,16},{24,20},{28,24},{0,28},{5,1},{9... | collective-permute-start | bytes 983048 | tf_op jit(solution)/shard_map/ppermute | solution.py:300
  21.8 33.9 %copy-start.4 = (f32[128]{0:T(128)S(1)}, f32[128]{0:T(128)}, u32[]{:S(2)}) copy-start(f32[128]{0:T(128)} %param.16) | copy-start | bytes 1540
  21.8 33.9 %copy-start.5 = (f32[128]{0:T(128)S(1)}, f32[128]{0:T(128)}, u32[]{:S(2)}) copy-start(f32[128]{0:T(128)} %param.17) | copy-start | bytes 1540
  21.8 33.9 %copy-start.6 = (f32[32]{0:T(128)S(1)}, f32[32]{0:T(128)}, u32[]{:S(2)}) copy-start(f32[32]{0:T(128)} %param.18) | copy-start | bytes 388
  21.8 33.9 %copy-start.7 = (f32[32]{0:T(128)S(1)}, f32[32]{0:T(128)}, u32[]{:S(2)}) copy-start(f32[32]{0:T(128)} %param.19) | copy-start | bytes 388
  50.7 8.6 %collective-permute-start.5 = (bf16[32,2176]{1,0:T(8,128)(2,1)S(1)}, bf16[32,2176]{1,0:T(8,128)(2,1)S(1)}, u32[]{:S(2)}, u32[]{:S(2)}) collective-permute-start(bf16[32,2176]{1,0:T(8,128)(2,1)S(1)} %get-tuple-element.29), channel_id=1, source_target_pairs={{0,1},{1,2},{2,3},{3,0},{4,5},{5,6},{6,7},{7,4},{8,9},{9,10},{10,1... | collective-permute-start | bytes 417800 | tf_op jit(solution)/shard_map/ppermute | solution.py:306
  53.2 9.9 %collective-permute-start.6 = (bf16[32,2176]{1,0:T(8,128)(2,1)S(1)}, bf16[32,2176]{1,0:T(8,128)(2,1)S(1)}, u32[]{:S(2)}, u32[]{:S(2)}) collective-permute-start(bf16[32,2176]{1,0:T(8,128)(2,1)S(1)} %get-tuple-element.30), channel_id=1, source_target_pairs={{0,2},{1,3},{2,0},{3,1},{4,6},{5,7},{6,4},{7,5},{8,10},{9,11},{10,... | collective-permute-start | bytes 417800 | tf_op jit(solution)/shard_map/ppermute | solution.py:306
  54.1 9.0 %collective-permute-start.7 = (bf16[32,2176]{1,0:T(8,128)(2,1)S(1)}, bf16[32,2176]{1,0:T(8,128)(2,1)S(1)}, u32[]{:S(2)}, u32[]{:S(2)}) collective-permute-start(bf16[32,2176]{1,0:T(8,128)(2,1)S(1)} %get-tuple-element.31), channel_id=1, source_target_pairs={{0,3},{1,0},{2,1},{3,2},{4,7},{5,4},{6,5},{7,6},{8,11},{9,8},{10,9... | collective-permute-start | bytes 417800 | tf_op jit(solution)/shard_map/ppermute | solution.py:306

commit v6 on v5

--- a/solution.py
+++ b/solution.py
@@ -331,7 +331,8 @@
     coefficients = (first[None].astype(jnp.int32), capacity, affinity, energy_yield[None, :])
     edges = jnp.concatenate([biomass, resources.astype(bf16)], axis=0)
     low, high, gained, nets = exchange(own, others, coefficients, mass, secretion, edges)
-    arrived = [shifted(nets[j], "species", j) for j in range(1, count)]
+    farthest = sorted(range(1, count), key=lambda j: -min(j, count - j))
+    arrived = [shifted(nets[j], "species", j) for j in farthest]
     sums = jax.ShapeDtypeStruct(biomass.shape, f32)
     growth, new_biomass, partial = pl.pallas_call(
         functools.partial(step_kernel, slab_rows, plane),

time: 65.1 us -> 65.4 us (level)
  starting transfers between devices: 13.8 us -> 14.6 us
    ppermute x6, starting transfers between devices: 11.1 us -> 11.9 us  [shifted(): lax.ppermute(value, axis, [(i, (i + shift) % count) for i in range(count)])]
  transfers between devices with their start and end apart: 8 -> 8, of which waited for: 2 -> 1; matrix products, arithmetic and copies ran while one was open for 1% -> 1% of each run, Pallas kernels for 65% -> 64%
where the time goes in v6:
time: 65.4 us; the launch traced here: 65.3 us
  Pallas kernels  41.9 us (64%)
  starting transfers between devices  14.6 us (22%)
  waiting for transfers between devices  4.46 us (7%)
  local copies, waits for them, and re-layouts  3.15 us (5%)
  between operations  0.95 us (1%)
    pallas_call x1, Pallas kernels, exchange(): pl.pallas_call(functools.partial(second_kernel, held, len(others), len(ne...  28.8 us
    ppermute x6, starting transfers between devices, shifted(): lax.ppermute(value, axis, [(i, (i + shift) % count) for i in range(count)])  11.9 us
    pallas_call x1, Pallas kernels, exchange(): pl.pallas_call(functools.partial(first_kernel, 0, 1), out_shape=(sums, su...  10 us
    ppermute x6, waiting for transfers between devices, shifted(): lax.ppermute(value, axis, [(i, (i + shift) % count) for i in range(count)])  4.45 us
    pallas_call x1, Pallas kernels, per_device(): pl.pallas_call(functools.partial(step_kernel, slab_rows, plane), out_shap...  3.09 us
    ppermute x1, starting transfers between devices, halo(): high = lax.ppermute(block[:, 0, :], axis, backward)  2.63 us
    unnamed x38, local copies, waits for them, and re-layouts  2.17 us
  transfers between devices with their start and end apart: 8, of which 1 were waited for; matrix products, arithmetic and copies ran while one was open for 1% of the time, Pallas kernels for 64%

profile of v6, /device:TPU:0, one launch (start us, length us, event | category | flops | bytes accessed | tf_op | source)
XLA Modules:
  0.0 65.3 jit_solution(11656166095361892928)
XLA Ops:
  0.6 1.1 %copy.16 = f32[4,8,2,1024]{3,1,2,0:T(8,128)S(1)} copy(f32[4,8,2,1024]{3,2,1,0:T(2,128)} %bitcast.26) | data formatting | bytes 524288
  1.8 5.1 %collective-permute-start.2 = (bf16[32,2048]{1,0:T(8,128)(2,1)S(1)}, bf16[32,2048]{1,0:T(8,128)(2,1)S(1)}, u32[]{:S(2)}, u32[]{:S(2)}) collective-permute-start(bf16[32,2048]{1,0:T(8,128)(2,1)S(1)} %convert_element_type.25.refs_0_), channel_id=1, source_target_pairs={{0,3},{1,0},{2,1},{3,2},{4,7},{5,4},{6,5},{7,6},{8,11},{9,8},{10,9... | collective-permute-start | bytes 393224 | tf_op jit(solution)/shard_map/ppermute | solution.py:306
  6.9 0.0 collective-permute-start.3
  6.9 1.0 %collective-permute-start.4 = (bf16[32,2048]{1,0:T(8,128)(2,1)S(1)}, bf16[32,2048]{1,0:T(8,128)(2,1)S(1)}, u32[]{:S(2)}, u32[]{:S(2)}) collective-permute-start(bf16[32,2048]{1,0:T(8,128)(2,1)S(1)} %convert_element_type.25.refs_0_), channel_id=1, source_target_pairs={{0,1},{1,2},{2,3},{3,0},{4,5},{5,6},{6,7},{7,4},{8,9},{9,10},{10,1... | collective-permute-start | bytes 393224 | tf_op jit(solution)/shard_map/ppermute | solution.py:306
  7.9 0.1 copy.18
  8.0 0.1 copy.14
  8.1 0.0 copy-start
  8.1 0.0 copy-start.1
  8.1 0.0 copy-start.3
  8.1 0.1 copy.15
  8.3 0.6 copy-done
  9.0 0.0 copy-done.1
  9.0 10.0 %shard_map.121 = (f32[128,2048]{1,0:T(8,128)S(1)}, f32[128,2048]{1,0:T(8,128)S(1)}, f32[32,2048]{1,0:T(8,128)S(1)}) custom-call(bf16[32,2048]{1,0:T(8,128)(2,1)S(1)} %convert_element_type.25.refs_0_, s32[1]{0:T(128)} %bitcast.refs_1_.refs_3_, f32[128,128]{1,0:T(8,128)S(1)} %copy-done, f32[128,128]{1,0:T(8,128)S(1)} %copy-done.1, f32[1,128]{1,0:T(1,128)S(1)} %bitcast.19, ...), custom_call_target="tpu_custom_call" | custom-call | flops 335544320 | bytes 1048576 | tf_op jit(solution)/shard_map/pallas_call | solution.py:220
  19.0 0.1 slice_bitcast_fusion
  19.1 0.1 collective-permute-start
  19.1 2.6 %collective-permute-start.1 = (bf16[160,1024]{1,0:T(8,128)(2,1)S(1)}, bf16[160,1024]{1,0:T(8,128)(2,1)S(1)}, u32[]{:S(2)}, u32[]{:S(2)}) collective-permute-start(bf16[160,1024]{1,0:T(8,128)(2,1)S(1)} %get-tuple-element.39), channel_id=1, source_target_pairs={{4,0},{8,4},{12,8},{16,12},{20,16},{24,20},{28,24},{0,28},{5,1},{9... | collective-permute-start | bytes 983048 | tf_op jit(solution)/shard_map/ppermute | solution.py:300
  21.8 0.0 collective-permute-done.2.refs_0_
  21.8 0.0 collective-permute-done.3.refs_1_
  21.8 0.0 copy-start.4
  21.8 0.0 copy-start.5
  21.8 0.0 copy-start.6
  21.8 0.0 copy-start.7
  21.8 28.8 %shard_map.122 = (f32[128,2048]{1,0:T(8,128)S(1)}, f32[32,2048]{1,0:T(8,128)S(1)}, bf16[32,2176]{1,0:T(8,128)(2,1)S(1)}, bf16[32,2176]{1,0:T(8,128)(2,1)S(1)}, bf16[32,2176]{1,0:T(8,128)(2,1)S(1)}) custom-call(bf16[32,2048]{1,0:T(8,128)(2,1)S(1)} %collective-permute-done.2.refs_0_, bf16[32,2048]{1,0:T(8,128)(2,1)S(1)} %collective-permute-done.3.refs_1_, ...), custom_call_target="tpu_custom_call" | custom-call | flops 1006632960 | bytes 1048576 | tf_op jit(solution)/shard_map/pallas_call | solution.py:232
  50.7 2.0 %collective-permute-start.5 = (bf16[32,2176]{1,0:T(8,128)(2,1)S(1)}, bf16[32,2176]{1,0:T(8,128)(2,1)S(1)}, u32[]{:S(2)}, u32[]{:S(2)}) collective-permute-start(bf16[32,2176]{1,0:T(8,128)(2,1)S(1)} %get-tuple-element.29), channel_id=1, source_target_pairs={{0,2},{1,3},{2,0},{3,1},{4,6},{5,7},{6,4},{7,5},{8,10},{9,11},{10,... | collective-permute-start | bytes 417800 | tf_op jit(solution)/shard_map/ppermute | solution.py:306
  52.7 1.5 %collective-permute-start.6 = (bf16[32,2176]{1,0:T(8,128)(2,1)S(1)}, bf16[32,2176]{1,0:T(8,128)(2,1)S(1)}, u32[]{:S(2)}, u32[]{:S(2)}) collective-permute-start(bf16[32,2176]{1,0:T(8,128)(2,1)S(1)} %get-tuple-element.30), channel_id=1, source_target_pairs={{0,1},{1,2},{2,3},{3,0},{4,5},{5,6},{6,7},{7,4},{8,9},{9,10},{10,1... | collective-permute-start | bytes 417800 | tf_op jit(solution)/shard_map/ppermute | solution.py:306
  54.1 2.4 %collective-permute-start.7 = (bf16[32,2176]{1,0:T(8,128)(2,1)S(1)}, bf16[32,2176]{1,0:T(8,128)(2,1)S(1)}, u32[]{:S(2)}, u32[]{:S(2)}) collective-permute-start(bf16[32,2176]{1,0:T(8,128)(2,1)S(1)} %get-tuple-element.31), channel_id=1, source_target_pairs={{0,3},{1,0},{2,1},{3,2},{4,7},{5,4},{6,5},{7,6},{8,11},{9,8},{10,9... | collective-permute-start | bytes 417800 | tf_op jit(solution)/shard_map/ppermute | solution.py:306
  56.5 0.0 collective-permute-done.low_ref
  56.5 3.1 %shard_map.123 = (f32[128,2,1024]{2,1,0:T(2,128)}, f32[128,2,1024]{2,1,0:T(2,128)}, f32[32,2048]{1,0:T(8,128)S(1)}) custom-call(bf16[128,2048]{1,0:T(8,128)(2,1)S(1)} %bitcast.18, f32[32,2048]{1,0:T(8,128)S(1)} %bitcast.15, bf16[160,1024]{1,0:T(8,128)(2,1)S(1)} %collective-permute-done.low_ref, bf16[160,1024]{1,0:T(8,128)(2,1)S(1)} %collective-permute-done.1.high_ref, ...), custom_call_target="tpu_custom_call" | custom-call | flops 83886080 | bytes 1048576 | tf_op jit(solution)/shard_map/pallas_call | solution.py:337
  59.6 4.4 %collective-permute-done.5 = bf16[32,2176]{1,0:T(8,128)(2,1)S(1)} collective-permute-done((bf16[32,2176]{1,0:T(8,128)(2,1)S(1)}, bf16[32,2176]{1,0:T(8,128)(2,1)S(1)}, u32[]{:S(2)}, u32[]{:S(2)}) %collective-permute-start.5) | collective-permute-done | bytes 139296 | tf_op jit(solution)/shard_map/ppermute | solution.py:306
  64.1 0.0 collective-permute-done.6
  64.2 0.1 multiply_add_fusion
  64.3 0.9 %reshape.17 = f32[32,2,1024]{2,1,0:T(2,128)} reshape(f32[32,2048]{1,0:T(8,128)S(1)} %multiply_add_fusion) | data formatting | bytes 524288 | tf_op jit(solution)/shard_map/reshape | solution.py:351
  (32 shorter events, 0.2 us)
Async XLA Ops:
  0.6 7.3 %copy-start.9 = (f32[32,2,1024]{2,1,0:T(2,128)S(1)}, f32[32,2,1024]{2,1,0:T(2,128)}, u32[]{:S(2)}) copy-start(f32[32,2,1024]{2,1,0:T(2,128)} %param.11) | copy-start | bytes 786436
  0.6 7.3 %copy-start.8 = (bf16[128,2,1024]{2,1,0:T(2,128)(2,1)S(1)}, bf16[128,2,1024]{2,1,0:T(2,128)(2,1)}, u32[]{:S(2)}) copy-start(bf16[128,2,1024]{2,1,0:T(2,128)(2,1)} %param.10) | copy-start | bytes 1572868
  1.8 20.0 %collective-permute-start.2 = (bf16[32,2048]{1,0:T(8,128)(2,1)S(1)}, bf16[32,2048]{1,0:T(8,128)(2,1)S(1)}, u32[]{:S(2)}, u32[]{:S(2)}) collective-permute-start(bf16[32,2048]{1,0:T(8,128)(2,1)S(1)} %convert_element_type.25.refs_0_), channel_id=1, source_target_pairs={{0,3},{1,0},{2,1},{3,2},{4,7},{5,4},{6,5},{7,6},{8,11},{9,8},{10,9... | collective-permute-start | bytes 393224 | tf_op jit(solution)/shard_map/ppermute | solution.py:306
  6.9 14.9 %collective-permute-start.3 = (bf16[32,2048]{1,0:T(8,128)(2,1)S(1)}, bf16[32,2048]{1,0:T(8,128)(2,1)S(1)}, u32[]{:S(2)}, u32[]{:S(2)}) collective-permute-start(bf16[32,2048]{1,0:T(8,128)(2,1)S(1)} %convert_element_type.25.refs_0_), channel_id=1, source_target_pairs={{0,2},{1,3},{2,0},{3,1},{4,6},{5,7},{6,4},{7,5},{8,10},{9,11},{10,... | collective-permute-start | bytes 393224 | tf_op jit(solution)/shard_map/ppermute | solution.py:306
  6.9 14.9 %collective-permute-start.4 = (bf16[32,2048]{1,0:T(8,128)(2,1)S(1)}, bf16[32,2048]{1,0:T(8,128)(2,1)S(1)}, u32[]{:S(2)}, u32[]{:S(2)}) collective-permute-start(bf16[32,2048]{1,0:T(8,128)(2,1)S(1)} %convert_element_type.25.refs_0_), channel_id=1, source_target_pairs={{0,1},{1,2},{2,3},{3,0},{4,5},{5,6},{6,7},{7,4},{8,9},{9,10},{10,1... | collective-permute-start | bytes 393224 | tf_op jit(solution)/shard_map/ppermute | solution.py:306
  8.1 0.8 %copy-start = (f32[128,128]{1,0:T(8,128)S(1)}, f32[128,128]{1,0:T(8,128)}, u32[]{:S(2)}) copy-start(f32[128,128]{1,0:T(8,128)} %refs_4_.1) | copy-start | bytes 196612
  8.1 0.9 %copy-start.1 = (f32[128,128]{1,0:T(8,128)S(1)}, f32[128,128]{1,0:T(8,128)}, u32[]{:S(2)}) copy-start(f32[128,128]{1,0:T(8,128)} %refs_5_.1) | copy-start | bytes 196612
  8.1 0.9 %copy-start.3 = (f32[128]{0:T(128)S(1)}, f32[128]{0:T(128)}, u32[]{:S(2)}) copy-start(f32[128]{0:T(128)} %param.15) | copy-start | bytes 1540
  19.0 2.8 %copy-start.2 = (bf16[128,128]{1,0:T(8,128)(2,1)S(1)}, bf16[128,128]{1,0:T(8,128)(2,1)}, u32[]{:S(2)}) copy-start(bf16[128,128]{1,0:T(8,128)(2,1)} %refs_11_.1) | copy-start | bytes 98308
  19.1 37.4 %collective-permute-start = (bf16[160,1024]{1,0:T(8,128)(2,1)S(1)}, bf16[160,1024]{1,0:T(8,128)(2,1)S(1)}, u32[]{:S(2)}, u32[]{:S(2)}) collective-permute-start(bf16[160,1024]{1,0:T(8,128)(2,1)S(1)} %get-tuple-element.40), channel_id=1, source_target_pairs={{0,4},{4,8},{8,12},{12,16},{16,20},{20,24},{24,28},{28,0},{1,5},{5... | collective-permute-start | bytes 983048 | tf_op jit(solution)/shard_map/ppermute | solution.py:299
  19.1 37.4 %collective-permute-start.1 = (bf16[160,1024]{1,0:T(8,128)(2,1)S(1)}, bf16[160,1024]{1,0:T(8,128)(2,1)S(1)}, u32[]{:S(2)}, u32[]{:S(2)}) collective-permute-start(bf16[160,1024]{1,0:T(8,128)(2,1)S(1)} %get-tuple-element.39), channel_id=1, source_target_pairs={{4,0},{8,4},{12,8},{16,12},{20,16},{24,20},{28,24},{0,28},{5,1},{9... | collective-permute-start | bytes 983048 | tf_op jit(solution)/shard_map/ppermute | solution.py:300
  21.8 34.7 %copy-start.4 = (f32[128]{0:T(128)S(1)}, f32[128]{0:T(128)}, u32[]{:S(2)}) copy-start(f32[128]{0:T(128)} %param.16) | copy-start | bytes 1540
  21.8 34.7 %copy-start.5 = (f32[128]{0:T(128)S(1)}, f32[128]{0:T(128)}, u32[]{:S(2)}) copy-start(f32[128]{0:T(128)} %param.17) | copy-start | bytes 1540
  21.8 34.7 %copy-start.6 = (f32[32]{0:T(128)S(1)}, f32[32]{0:T(128)}, u32[]{:S(2)}) copy-start(f32[32]{0:T(128)} %param.18) | copy-start | bytes 388
  21.8 34.7 %copy-start.7 = (f32[32]{0:T(128)S(1)}, f32[32]{0:T(128)}, u32[]{:S(2)}) copy-start(f32[32]{0:T(128)} %param.19) | copy-start | bytes 388
  50.7 13.4 %collective-permute-start.5 = (bf16[32,2176]{1,0:T(8,128)(2,1)S(1)}, bf16[32,2176]{1,0:T(8,128)(2,1)S(1)}, u32[]{:S(2)}, u32[]{:S(2)}) collective-permute-start(bf16[32,2176]{1,0:T(8,128)(2,1)S(1)} %get-tuple-element.29), channel_id=1, source_target_pairs={{0,2},{1,3},{2,0},{3,1},{4,6},{5,7},{6,4},{7,5},{8,10},{9,11},{10,... | collective-permute-start | bytes 417800 | tf_op jit(solution)/shard_map/ppermute | solution.py:306
  52.7 11.4 %collective-permute-start.6 = (bf16[32,2176]{1,0:T(8,128)(2,1)S(1)}, bf16[32,2176]{1,0:T(8,128)(2,1)S(1)}, u32[]{:S(2)}, u32[]{:S(2)}) collective-permute-start(bf16[32,2176]{1,0:T(8,128)(2,1)S(1)} %get-tuple-element.30), channel_id=1, source_target_pairs={{0,1},{1,2},{2,3},{3,0},{4,5},{5,6},{6,7},{7,4},{8,9},{9,10},{10,1... | collective-permute-start | bytes 417800 | tf_op jit(solution)/shard_map/ppermute | solution.py:306
  54.1 9.9 %collective-permute-start.7 = (bf16[32,2176]{1,0:T(8,128)(2,1)S(1)}, bf16[32,2176]{1,0:T(8,128)(2,1)S(1)}, u32[]{:S(2)}, u32[]{:S(2)}) collective-permute-start(bf16[32,2176]{1,0:T(8,128)(2,1)S(1)} %get-tuple-element.31), channel_id=1, source_target_pairs={{0,3},{1,0},{2,1},{3,2},{4,7},{5,4},{6,5},{7,6},{8,11},{9,8},{10,9... | collective-permute-start | bytes 417800 | tf_op jit(solution)/shard_map/ppermute | solution.py:306
